TPU v7x, 256 devices: a whole 4x4x8 slice. The times are simulated.
256 devices in a mesh: row: 32 (over z, y), col: 8 (over x, core).
Axes of the slice: x: 4, y: 4, z: 8, core: 2. Of those that a mesh axis runs over, the one named last changes fastest.
Arguments:
- candidates: float32 [1024, 131072], P('col', 'row'), may hold values from -64 to 64
- trailing: float32 [512, 131072], P('col', 'row'), may hold values from -64 to 64
- pivots: int32 [64], replicated, may hold values from 0 to 1023, as said below
Outputs:
- r_panel: float32 [64, 64], replicated
- r_trail: float32 [64, 512], P(None, 'col')
- basis: float32 [64, 131072], P(None, 'row')
- trailing_next: float32 [512, 131072], P('col', 'row')
Inputs may be any that keep to these rules, and one draw needn't show every extreme that they name: `pivots`: 64 distinct column numbers; one block of 128 consecutive columns (those of one index of col) holds exactly 32 of them and no block holds more.
All inputs are finite; a program needn't handle non-finite values.
Results may differ from a plain program's by a relative error of at most 0.0003.
Values sent between devices are 32-bit elements; how exact they have to be, the bound alone decides.
No kernel may reach another device: no remote copies, remote signals or barrier semaphores. Data moves between devices by JAX's collectives and lax.ppermute only.
A program may use at most 64 MiB of HBM per device.

v0:
```python
import jax
import jax.numpy as jnp
from jax import lax
from jax.sharding import PartitionSpec as P


def inner(left, right):
    return lax.dot_general(
        left,
        right,
        (((1,), (1,)), ((), ())),
        preferred_element_type=jnp.float32,
        precision=lax.Precision.HIGHEST,
    )


def matmul(left, right):
    return jnp.dot(left, right, preferred_element_type=jnp.float32, precision=lax.Precision.HIGHEST)


def lower_factor(gram_matrix):
    count = gram_matrix.shape[0]
    positions = jnp.arange(count, dtype=jnp.int32)

    def column_step(j, lower):
        row_j = lax.dynamic_index_in_dim(lower, j, 0, keepdims=False)
        column = lax.dynamic_index_in_dim(gram_matrix, j, 1, keepdims=False) - matmul(lower, row_j)
        pivot_value = jnp.sqrt(lax.dynamic_index_in_dim(column, j, 0, keepdims=False))
        fresh = jnp.where(
            positions > j,
            column / pivot_value,
            jnp.where(positions == j, pivot_value, jnp.float32(0.0)),
        )
        return jnp.where((positions == j)[None, :], fresh[:, None], lower)

    return lax.fori_loop(0, count, column_step, jnp.zeros((count, count), jnp.float32))


def lower_inverse(lower):
    count = lower.shape[0]
    positions = jnp.arange(count, dtype=jnp.int32)

    def row_step(i, inverse):
        row_i = lax.dynamic_index_in_dim(lower, i, 0, keepdims=False)
        diagonal_value = lax.dynamic_index_in_dim(row_i, i, 0, keepdims=False)
        off_part = jnp.where(positions < i, row_i, jnp.float32(0.0))
        unit = (positions == i).astype(jnp.float32)
        fresh = (unit - matmul(off_part, inverse)) / diagonal_value
        return jnp.where((positions == i)[:, None], fresh[None, :], inverse)

    return lax.fori_loop(0, count, row_step, jnp.zeros((count, count), jnp.float32))


def factorize(gram_matrix):
    lower = lower_factor(gram_matrix)
    return (lower.T, lower_inverse(lower))


def on_device(candidates, trailing, pivots):
    cand_count = candidates.shape[0]
    my_col = lax.axis_index("col")
    owners = pivots // cand_count
    local_col = pivots - owners * cand_count
    selector = (local_col[:, None] == jnp.arange(cand_count, dtype=jnp.int32)[None, :]) & (
        owners == my_col
    )[:, None]
    picked = matmul(selector.astype(jnp.float32), candidates)
    panel_rows = lax.psum(picked, "col")
    gram_matrix = lax.psum(inner(panel_rows, panel_rows), "row")
    upper_factor, inverse_lower = factorize(gram_matrix)
    ortho_rows = matmul(inverse_lower, panel_rows)
    projected = lax.psum(inner(ortho_rows, trailing), "row")
    trailing_next = trailing - matmul(projected.T, ortho_rows)
    root_rows = jnp.sqrt(jnp.float32(trailing.shape[1] * lax.axis_size("row")))
    return (upper_factor / root_rows, projected / root_rows, ortho_rows * root_rows, trailing_next)


def solution(mesh):
    placed = (P("col", "row"), P("col", "row"), P())
    return jax.shard_map(
        on_device,
        mesh=mesh,
        in_specs=placed,
        out_specs=(P(), P(None, "col"), P(None, "row"), P("col", "row")),
        check_vma=False,
    )
```

profile of v0, /device:TPU:32, one launch (start us, length us, event | category | flops | bytes accessed | tf_op | source)
XLA Modules:
  0.0 569.6 jit_solution(1127908040445458118)
XLA Ops:
  7.2 0.8 broadcast_compare_fusion
  8.8 1.9 fusion.22
  10.7 70.3 %all-reduce.2.cloned.1.call-done = f32[64,4096]{1,0:T(8,128)} async-done(((f32[64,4096]{1,0:T(8,128)}), f32[64,4096]{1,0:T(8,128)}) %all-reduce.2.cloned.1.call-update) | async-done | bytes 1048592 | tf_op jit(solution)/shard_map/psum | solution.py:68
  81.0 2.5 fusion.26
  83.6 137.0 %psum.22 = f32[64,64]{1,0:T(8,128)S(1)} all-reduce(f32[64,64]{1,0:T(8,128)S(1)} %fusion.26), channel_id=1, replica_groups=mesh['row'=32,'col'=8] {'row'}, use_global_device_ids=true, to_apply=%region_1.2 | all-reduce | flops 4096 | bytes 32768 | tf_op jit(solution)/shard_map/psum | solution.py:69
  220.7 100.6 %while.33 = (s32[]{:T(128)}, f32[64,64]{1,0:T(8,128)S(1)}, f32[64,64]{0,1:T(8,128)S(1)}, s32[]{:T(128)}, s32[]{:T(128)}) while((s32[]{:T(128)}, f32[64,64]{1,0:T(8,128)S(1)}, f32[64,64]{0,1:T(8,128)S(1)}, s32[]{:T(128)}, s32[]{:T(128)}) %tuple.84), condition=%wide.region_3.4_spmd.clone.clone, body=%wide.region_2.3_spmd.clone.clone.sunk | while | flops 61891 | bytes 101616 | solution.py:36
  321.3 93.8 %while.34 = (s32[]{:T(128)}, f32[64,64]{1,0:T(8,128)S(1)}, f32[64,64]{1,0:T(8,128)S(1)}, s32[]{:T(128)}, s32[]{:T(128)}, /*index=5*/s32[]{:T(128)}) while((s32[]{:T(128)}, f32[64,64]{1,0:T(8,128)S(1)}, f32[64,64]{1,0:T(8,128)S(1)}, s32[]{:T(128)}, s32[]{:T(128)}, /*index=5*/s32[]{:T(128)}) %tuple.87), condition=%wide.region_5.6_spmd.clone.clone, body=%wide.region_4.5_spmd.clone.clone.sunk | while | flops 61892 | bytes 68859 | solution.py:51
  321.9 0.8 fusion.49
  323.3 0.8 fusion.49
  324.8 0.8 fusion.49
  326.3 0.8 fusion.49
  327.7 0.8 fusion.49
  329.2 0.8 fusion.49
  330.7 0.8 fusion.49
  332.1 0.8 fusion.49
  333.6 0.8 fusion.49
  335.1 0.8 fusion.49
  338.0 0.8 fusion.49
  340.9 0.8 fusion.49
  343.8 0.8 fusion.49
  345.3 0.8 fusion.49
  346.8 0.8 fusion.49
  348.2 0.8 fusion.49
  349.7 0.8 fusion.49
  351.2 0.8 fusion.49
  352.6 0.8 fusion.49
  354.1 0.8 fusion.49
  355.6 0.8 fusion.49
  415.1 3.2 broadcast_multiply_fusion
  418.3 2.2 fusion.27
  420.5 137.7 %psum.23 = f32[64,64]{1,0:T(8,128)S(1)} all-reduce(f32[64,64]{1,0:T(8,128)S(1)} %fusion.27), channel_id=1, replica_groups=mesh['row'=32,'col'=8] {'row'}, use_global_device_ids=true, to_apply=%region_6.7 | all-reduce | flops 4096 | bytes 32768 | tf_op jit(solution)/shard_map/psum | solution.py:72
  558.2 3.2 convolution_subtract_fusion
  (630 shorter events, 134.0 us)
Async XLA Ops:
  7.2 1.6 copy-start
  7.2 73.9 %all-reduce.2.cloned.1.call-start = ((), (), s32[]{:S(2)}) async-start(), calls=%async_computation | async-start | bytes 2097152 | tf_op jit(solution)/shard_map/psum | solution.py:68
Sparse Core Ops, SparseCore 0:
  10.9 70.0 all-reduce.1
where the time goes:
time: 576 us; the launch traced here: 570 us
  blocking collectives  275 us (48%)
  local copies, waits for them, and re-layouts  78.5 us (14%)
  matrix products  72.5 us (13%)
  waiting for transfers between devices  70.3 us (12%)
  loops' own time  46.1 us (8%)
  between operations  14.1 us (2%)
  other arithmetic  13.3 us (2%)
    psum x1, blocking collectives, on_device(): projected = lax.psum(inner(ortho_rows, trailing), 'row')  138 us
    psum x1, blocking collectives, on_device(): gram_matrix = lax.psum(inner(panel_rows, panel_rows), 'row')  137 us
    psum x1, waiting for transfers between devices, on_device(): panel_rows = lax.psum(picked, 'col')  70.3 us
    dot_general x131, matrix products, matmul(): jnp.dot(left, right, preferred_element_type=jnp.float32, precision=lax.Pr...  67.8 us
    another operation x1, loops' own time, lower_factor(): lax.fori_loop(0, count, column_step, jnp.zeros((count, count), jnp.float32))  45.8 us
    dynamic_slice x64, local copies, waits for them, and re-layouts, column_step(): lax.dynamic_index_in_dim(column, j, 0, keepdims=False)  39.6 us
    dynamic_slice x64, local copies, waits for them, and re-layouts, row_step(): diagonal_value = lax.dynamic_index_in_dim(row_i, i, 0, keepdims=False)  38.1 us
  transfers between devices with their start and end apart: 1, of which 1 were waited for; matrix products, arithmetic and copies ran while one was open for 0% of the time, Pallas kernels for 0%

commit v1 on v0

v1 whole, which is shorter than its diff:
```python
import functools

import jax
import jax.numpy as jnp
import numpy as np
from jax import lax
from jax.experimental import pallas as pl
from jax.experimental.pallas import tpu as pltpu
from jax.sharding import PartitionSpec as P

VMEM = pltpu.VMEM
SMEM = pltpu.SMEM
CORES = 2


def split_bf16(value):
    high = value.astype(jnp.bfloat16)
    low = (value - high.astype(jnp.float32)).astype(jnp.bfloat16)
    return high, low


def select_kernel(capacity, x_count, where_ref, pivots_ref, cand_ref, *rest):
    outs, (rows, sems) = rest[:x_count], rest[x_count:]
    cand_count, width = cand_ref.shape
    count = pivots_ref.shape[0]
    me = where_ref[0] * CORES + where_ref[1]

    def row_copy(pivot, slot):
        return pltpu.make_async_copy(
            cand_ref.at[pl.ds(pivot - me * cand_count, 1), :], rows.at[pl.ds(slot, 1), :], sems.at[slot]
        )

    def fetch(i, slot):
        pivot = pivots_ref[i]
        mine = pivot // cand_count == me

        @pl.when(mine)
        def _():
            row_copy(pivot, slot).start()

        return slot + mine.astype(jnp.int32)

    total = lax.fori_loop(0, count, fetch, jnp.int32(0))

    def drain(slot, carry):
        row_copy(me * cand_count, slot).wait()
        return carry

    lax.fori_loop(0, total, drain, 0)
    part = width // x_count
    for k in range(x_count):
        begin = pl.multiple_of((where_ref[0] ^ k) * part, part)
        outs[k][...] = rows[:, pl.ds(begin, part)]


def merge_kernel(x_count, where_ref, owners_ref, slots_ref, *rest):
    sources, (keep_ref, send_ref) = rest[:x_count], rest[x_count:]
    count, half = keep_ref.shape
    my_x, my_core = where_ref[0], where_ref[1]
    keep_at = pl.multiple_of(my_core * half, half)
    send_at = pl.multiple_of((1 - my_core) * half, half)

    def place(i, carry):
        owner = owners_ref[i]
        slot = slots_ref[i]
        away = (owner // CORES) ^ my_x

        for k in range(x_count):

            @pl.when((owner % CORES == my_core) & (away == k))
            def _():
                keep_ref[pl.ds(i, 1), :] = sources[k][pl.ds(slot, 1), pl.ds(keep_at, half)]
                send_ref[pl.ds(i, 1), :] = sources[k][pl.ds(slot, 1), pl.ds(send_at, half)]

        return carry

    lax.fori_loop(0, count, place, 0)


def gram_kernel(x_count, where_ref, *rest):
    mine, other = rest[:x_count], rest[x_count : 2 * x_count]
    trail_ref, sums_ref, panel_ref = rest[2 * x_count :]
    count, piece = mine[0].shape
    width = trail_ref.shape[1]
    my_x, my_core = where_ref[0], where_ref[1]
    for k in range(x_count):
        for core, ref in ((my_core, mine[k]), (1 - my_core, other[k])):
            begin = pl.multiple_of(((my_x ^ k) * CORES + core) * piece, piece)
            high, low = split_bf16(ref[...])
            panel_ref[0:count, pl.ds(begin, piece)] = high
            panel_ref[count : 2 * count, pl.ds(begin, piece)] = low
    total = jnp.zeros((2 * count, 4 * count), jnp.float32)
    for begin in range(0, width, piece):
        block = slice(begin, begin + piece)
        trail_high, trail_low = split_bf16(trail_ref[:, block])
        panel_parts = panel_ref[:, block]
        right = jnp.concatenate(
            [panel_parts[:count], trail_high, panel_parts[count:], trail_low], axis=0
        )
        total += lax.dot_general(
            panel_parts, right, (((1,), (1,)), ((), ())), preferred_element_type=jnp.float32
        )
    lead = total[:count] + total[count:]
    sums_ref[...] = lead[:, : 2 * count] + lead[:, 2 * count :]


def eliminate(work):
    count = work.shape[0]
    rows = lax.broadcasted_iota(jnp.int32, work.shape, 0)
    lanes = lax.broadcasted_iota(jnp.int32, work.shape, 1)
    scale = jnp.zeros(work.shape, jnp.float32)
    for j in range(count):
        row = jnp.broadcast_to(work[j : j + 1, :], work.shape)
        column = jnp.broadcast_to(work[:, j : j + 1], work.shape)
        pivot = jnp.broadcast_to(column[j : j + 1, :], work.shape)
        scale = jnp.where(rows == j, lax.rsqrt(pivot), scale)
        factor = jnp.where(rows > j, column / pivot, 0.0)
        here = lanes == j
        work = jnp.where(here & (rows > j), 0.0, work) - factor * jnp.where(here, 1.0, row)
    return work * scale, scale


def finish_kernel(root, one_ref, two_ref, panel_ref, trail_ref, upper_ref, coef_ref, basis_ref, next_ref, left):
    count = one_ref.shape[0]

    @pl.when(pl.program_id(0) == 0)
    def _():
        work, scale = eliminate(one_ref[...] + two_ref[...])
        square = (count, count)
        rows = lax.broadcasted_iota(jnp.int32, square, 0)
        lanes = lax.broadcasted_iota(jnp.int32, square, 1)
        factor, coef = work[:, :count], work[:, count:]
        upper_ref[...] = jnp.where(lanes >= rows, factor, 0.0) * jnp.float32(1.0 / root)
        coef_ref[...] = coef * jnp.float32(1.0 / root)
        inverse = jnp.where(lanes < rows, factor, jnp.where(lanes == rows, scale[:, :count], 0.0))
        weights = lax.dot_general(
            coef,
            inverse,
            (((0,), (0,)), ((), ())),
            preferred_element_type=jnp.float32,
            precision=lax.Precision.HIGHEST,
        )
        high, low = split_bf16(jnp.concatenate([inverse * jnp.float32(root), weights], axis=0))
        left[...] = jnp.concatenate([high, high, low, low], axis=1)

    block = panel_ref[...]
    both = jnp.dot(
        left[...], jnp.concatenate([block, block], axis=0), preferred_element_type=jnp.float32
    )
    basis_ref[...] = both[:count]
    next_ref[...] = trail_ref[...] - both[count:]


def on_device(candidates, trailing, pivots):
    cand_count, width = candidates.shape
    count = pivots.shape[0]
    col_count, row_count = lax.axis_size("col"), lax.axis_size("row")
    x_count = col_count // CORES
    capacity = count // 2
    piece = width // col_count
    root = float(np.sqrt(np.float32(width * row_count)))
    my_col = lax.axis_index("col")
    place = jnp.stack([my_col // CORES, my_col % CORES]).astype(jnp.int32)
    owners = pivots // cand_count
    order = jnp.arange(count, dtype=jnp.int32)
    earlier = (owners[:, None] == owners[None, :]) & (order[None, :] < order[:, None])
    slots = jnp.sum(earlier.astype(jnp.int32), axis=1)
    f32 = jnp.float32

    def to_x(array, k):
        return lax.ppermute(
            array, "col", [(i, ((i // CORES) ^ k) * CORES + i % CORES) for i in range(col_count)]
        )

    def to_core(array):
        return lax.ppermute(array, "col", [(i, i ^ 1) for i in range(col_count)])

    def to_row(array, k):
        return lax.ppermute(array, "row", [(i, i ^ k) for i in range(row_count)])

    in_vmem, in_smem = pl.BlockSpec(memory_space=VMEM), pl.BlockSpec(memory_space=SMEM)
    quarters = pl.pallas_call(
        functools.partial(select_kernel, capacity, x_count),
        out_shape=[jax.ShapeDtypeStruct((capacity, width // x_count), f32)] * x_count,
        in_specs=[in_smem, in_smem, pl.BlockSpec(memory_space=pl.ANY)],
        out_specs=[in_vmem] * x_count,
        scratch_shapes=[VMEM((capacity, width), f32), pltpu.SemaphoreType.DMA((capacity,))],
        name="select",
    )(place, pivots, candidates)
    arrived = [quarters[0]] + [to_x(quarters[k], k) for k in range(1, x_count)]
    keep, send = pl.pallas_call(
        functools.partial(merge_kernel, x_count),
        out_shape=[jax.ShapeDtypeStruct((count, piece), f32)] * 2,
        in_specs=[in_smem] * 3 + [in_vmem] * x_count,
        out_specs=[in_vmem] * 2,
        name="merge",
    )(place, owners, slots, *arrived)
    passed = to_core(send)
    own_core = (owners % CORES == my_col % CORES)[:, None]
    own_piece = jnp.where(own_core, keep, passed)
    mine = [own_piece] + [to_x(own_piece, k) for k in range(1, x_count)]
    other = [to_core(array) for array in mine]
    sums, panel = pl.pallas_call(
        functools.partial(gram_kernel, x_count),
        out_shape=[
            jax.ShapeDtypeStruct((count, 2 * count), f32),
            jax.ShapeDtypeStruct((2 * count, width), jnp.bfloat16),
        ],
        in_specs=[in_smem] + [in_vmem] * (2 * x_count + 1),
        out_specs=[in_vmem] * 2,
        name="gram",
    )(place, *mine, *other, trailing)
    sums = (sums + to_row(sums, 1)) + (to_row(sums, 2) + to_row(sums, 3))
    sums = (sums + to_row(sums, 4)) + (to_row(sums, 8) + to_row(sums, 12))
    far = to_row(sums, 16)
    steps = col_count
    whole = lambda shape: pl.BlockSpec(shape, lambda i: (0, 0))
    block = lambda rows: pl.BlockSpec((rows, width // steps), lambda i: (0, i))
    return pl.pallas_call(
        functools.partial(finish_kernel, root),
        grid=(steps,),
        out_shape=[
            jax.ShapeDtypeStruct((count, count), f32),
            jax.ShapeDtypeStruct((count, count), f32),
            jax.ShapeDtypeStruct((count, width), f32),
            jax.ShapeDtypeStruct((count, width), f32),
        ],
        in_specs=[whole((count, 2 * count))] * 2 + [block(2 * count), block(count)],
        out_specs=[whole((count, count))] * 2 + [block(count)] * 2,
        scratch_shapes=[VMEM((2 * count, 4 * count), jnp.bfloat16)],
        name="finish",
    )(sums, far, panel, trailing)


def solution(mesh):
    placed = (P("col", "row"), P("col", "row"), P())
    return jax.shard_map(
        on_device,
        mesh=mesh,
        in_specs=placed,
        out_specs=(P(), P(None, "col"), P(None, "row"), P("col", "row")),
        check_vma=False,
    )
```

time: 576 us -> 82.6 us (0.14)
  blocking collectives: 275 us -> 0 us
  local copies, waits for them, and re-layouts: 78.5 us -> 2.12 us
  matrix products: 72.5 us -> 0 us
  loops' own time: 46.1 us -> 0 us
  waiting for transfers between devices: 70.3 us -> 24.3 us
  Pallas kernels: 0 us -> 26 us
  starting transfers between devices: 0.04 us -> 24.7 us
  between operations: 14.1 us -> 0.77 us
  other arithmetic: 13.3 us -> 3.06 us
    psum x2 -> x0, blocking collectives: 275 us -> none  [the longest x1 138 us: on_device(): projected = lax.psum(inner(ortho_rows, trailing), 'row')]
    dynamic_slice x128 -> x0, local copies, waits for them, and re-layouts: 77.7 us -> none  [the longest x64 39.6 us: column_step(): lax.dynamic_index_in_dim(column, j, 0, keepdims=False)]
    dot_general x133 -> x0, matrix products: 72.5 us -> none  [the longest x131 67.8 us: matmul(): jnp.dot(left, right, preferred_element_type=jnp.float32, precision=lax.Pr...]
    psum x1 -> x0, waiting for transfers between devices: 70.3 us -> none  [on_device(): panel_rows = lax.psum(picked, 'col')]
    another operation x2 -> x0, loops' own time: 46.1 us -> none  [the longest x1 45.8 us: lower_factor(): lax.fori_loop(0, count, column_step, jnp.zeros((count, count), jnp.float32))]
    pallas_call x0 -> x4, Pallas kernels: none -> 26 us  [the longest x1 14.9 us: on_device(): pl.pallas_call(functools.partial(finish_kernel, root), grid=(steps,), out...]
    ppermute x0 -> x18, starting transfers between devices: none -> 24.7 us  [the longest x7 15.3 us: to_row(): return lax.ppermute(array, 'row', [(i, i ^ k) for i in range(row_count)])]
    ppermute x0 -> x18, waiting for transfers between devices: none -> 24.3 us  [the longest x6 12.4 us: to_x(): lax.ppermute(array, 'col', [(i, (i // CORES ^ k) * CORES + i % CORES) for...]
  transfers between devices with their start and end apart: 1 -> 18, of which waited for: 1 -> 14; matrix products, arithmetic and copies ran while one was open for 0% -> 1% of each run, Pallas kernels for 0% -> 0%
where the time goes in v1:
time: 82.6 us; the launch traced here: 81 us
  Pallas kernels  26 us (31%)
  starting transfers between devices  24.7 us (30%)
  waiting for transfers between devices  24.3 us (29%)
  other arithmetic  3.06 us (4%)
  local copies, waits for them, and re-layouts  2.12 us (3%)
    ppermute x7, starting transfers between devices, to_row(): return lax.ppermute(array, 'row', [(i, i ^ k) for i in range(row_count)])  15.3 us
    pallas_call x1, Pallas kernels, on_device(): pl.pallas_call(functools.partial(finish_kernel, root), grid=(steps,), out...  14.9 us
    ppermute x6, waiting for transfers between devices, to_x(): lax.ppermute(array, 'col', [(i, (i // CORES ^ k) * CORES + i % CORES) for...  12.4 us
    ppermute x7, waiting for transfers between devices, to_row(): return lax.ppermute(array, 'row', [(i, i ^ k) for i in range(row_count)])  9.02 us
    ppermute x6, starting transfers between devices, to_x(): lax.ppermute(array, 'col', [(i, (i // CORES ^ k) * CORES + i % CORES) for...  8.97 us
    pallas_call x1, Pallas kernels, on_device(): pl.pallas_call(functools.partial(merge_kernel, x_count), out_shape=[jax.S...  4.41 us
    pallas_call x1, Pallas kernels, on_device(): pl.pallas_call(functools.partial(select_kernel, capacity, x_count), out_s...  3.44 us
    pallas_call x1, Pallas kernels, on_device(): pl.pallas_call(functools.partial(gram_kernel, x_count), out_shape=[jax.Sh...  3.25 us
  transfers between devices with their start and end apart: 18, of which 14 were waited for; matrix products, arithmetic and copies ran while one was open for 1% of the time, Pallas kernels for 0%

profile of v1, /device:TPU:32, one launch (start us, length us, event | category | flops | bytes accessed | tf_op | source)
XLA Modules:
  0.0 81.0 jit_solution(1766252787200200370)
XLA Ops:
  0.7 0.6 pad_add_fusion.where_ref
  1.2 3.4 %select.13 = (f32[32,1024]{1,0:T(8,128)}, f32[32,1024]{1,0:T(8,128)}, f32[32,1024]{1,0:T(8,128)}, f32[32,1024]{1,0:T(8,128)}) custom-call(s32[2]{0:T(128)} %pad_add_fusion.where_ref, s32[64]{0:T(128)} %pivots_ref.1, f32[128,4096]{1,0:T(8,128)} %cand_ref.1), custom_call_target="tpu_custom_call" | custom-call | tf_op jit(solution)/shard_map/select/pallas_call | solution.py:182
  4.7 1.6 %collective-permute-start = (f32[32,1024]{1,0:T(8,128)}, f32[32,1024]{1,0:T(8,128)S(1)}, u32[]{:S(2)}, u32[]{:S(2)}) collective-permute-start(f32[32,1024]{1,0:T(8,128)} %get-tuple-element.13), channel_id=1, source_target_pairs={{0,2},{1,3},{2,0},{3,1},{4,6},{5,7},{6,4},{7,5},{8,10},{9,11},{10,... | collective-permute-start | bytes 393224 | tf_op jit(solution)/shard_map/ppermute | solution.py:171
  6.3 2.4 %collective-permute-start.1 = (f32[32,1024]{1,0:T(8,128)}, f32[32,1024]{1,0:T(8,128)S(1)}, u32[]{:S(2)}, u32[]{:S(2)}) collective-permute-start(f32[32,1024]{1,0:T(8,128)} %get-tuple-element.14), channel_id=1, source_target_pairs={{0,4},{1,5},{2,6},{3,7},{4,0},{5,1},{6,2},{7,3},{8,12},{9,13},{10,... | collective-permute-start | bytes 393224 | tf_op jit(solution)/shard_map/ppermute | solution.py:171
  8.7 0.8 collective-permute-start.2
  9.5 0.7 convert_reduce_fusion.slots_ref
  10.2 1.2 %collective-permute-done.rest_1_ = f32[32,1024]{1,0:T(8,128)S(1)} collective-permute-done((f32[32,1024]{1,0:T(8,128)}, f32[32,1024]{1,0:T(8,128)S(1)}, u32[]{:S(2)}, u32[]{:S(2)}) %collective-permute-start) | collective-permute-done | bytes 131104 | tf_op jit(solution)/shard_map/ppermute | solution.py:171
  11.4 3.6 %collective-permute-done.1.rest_2_ = f32[32,1024]{1,0:T(8,128)S(1)} collective-permute-done((f32[32,1024]{1,0:T(8,128)}, f32[32,1024]{1,0:T(8,128)S(1)}, u32[]{:S(2)}, u32[]{:S(2)}) %collective-permute-start.1) | collective-permute-done | bytes 131104 | tf_op jit(solution)/shard_map/ppermute | solution.py:171
  15.0 2.0 %collective-permute-done.2.rest_3_ = f32[32,1024]{1,0:T(8,128)S(1)} collective-permute-done((f32[32,1024]{1,0:T(8,128)}, f32[32,1024]{1,0:T(8,128)S(1)}, u32[]{:S(2)}, u32[]{:S(2)}) %collective-permute-start.2) | collective-permute-done | bytes 131104 | tf_op jit(solution)/shard_map/ppermute | solution.py:171
  17.0 0.6 copy-done.10
  17.7 4.4 %merge.1 = (f32[64,512]{1,0:T(8,128)}, f32[64,512]{1,0:T(8,128)}) custom-call(s32[2]{0:T(128)} %pad_add_fusion.where_ref, s32[64]{0:T(128)} %copy-done.13, s32[64]{0:T(128)} %convert_reduce_fusion.slots_ref, f32[32,1024]{1,0:T(8,128)} %get-tuple-element.12.rest_0_, f32[32,1024]{1,0:T(8,128)} %copy-done.7, f32[32,1024]{1,0:T(8,128)} %copy-done.9, ...), custom_call_target="tpu_custom_call" | custom-call | tf_op jit(solution)/shard_map/merge/pallas_call | solution.py:191
  22.1 1.6 %collective-permute-done.3 = f32[64,512]{1,0:T(8,128)S(1)} collective-permute-done((f32[64,512]{1,0:T(8,128)}, f32[64,512]{1,0:T(8,128)S(1)}, u32[]{:S(2)}, u32[]{:S(2)}) %collective-permute-start.3) | collective-permute-done | bytes 131104 | tf_op jit(solution)/shard_map/ppermute | solution.py:176
  23.6 1.0 %broadcast_select_fusion.rest_0_ = f32[64,512]{1,0:T(8,128)S(1)} fusion(f32[64,512]{1,0:T(8,128)} %get-tuple-element.16, f32[64,512]{1,0:T(8,128)S(1)} %collective-permute-done.3, pred[64]{0:T(512)(128)(4,1)S(1)} %get-tuple-element.20), kind=kLoop, calls=%fused_computation | loop fusion | flops 32768 | bytes 393280 | tf_op jit(solution)/shard_map/jit(_where)/select_n | solution.py:200
  24.6 0.9 %collective-permute-start.6 = (f32[64,512]{1,0:T(8,128)S(1)}, f32[64,512]{1,0:T(8,128)S(1)}, u32[]{:S(2)}, u32[]{:S(2)}) collective-permute-start(f32[64,512]{1,0:T(8,128)S(1)} %broadcast_select_fusion.rest_0_), channel_id=1, source_target_pairs={{0,6},{1,7},{2,4},{3,5},{4,2},{5,3},{6,0},{7,1},{8,14},{9,15},{10,... | collective-permute-start | bytes 393224 | tf_op jit(solution)/shard_map/ppermute | solution.py:171
  26.1 2.7 %collective-permute-start.4 = (f32[64,512]{1,0:T(8,128)S(1)}, f32[64,512]{1,0:T(8,128)S(1)}, u32[]{:S(2)}, u32[]{:S(2)}) collective-permute-start(f32[64,512]{1,0:T(8,128)S(1)} %broadcast_select_fusion.rest_0_), channel_id=1, source_target_pairs={{0,2},{1,3},{2,0},{3,1},{4,6},{5,7},{6,4},{7,5},{8,10},{9,11},{10,... | collective-permute-start | bytes 393224 | tf_op jit(solution)/shard_map/ppermute | solution.py:171
  28.8 5.5 %collective-permute-done.6.rest_3_ = f32[64,512]{1,0:T(8,128)S(1)} collective-permute-done((f32[64,512]{1,0:T(8,128)S(1)}, f32[64,512]{1,0:T(8,128)S(1)}, u32[]{:S(2)}, u32[]{:S(2)}) %collective-permute-start.6) | collective-permute-done | bytes 131104 | tf_op jit(solution)/shard_map/ppermute | solution.py:171
  35.0 0.7 collective-permute-done.10.rest_7_
  36.5 0.6 copy-done.11
  37.2 3.3 %gram.1 = (f32[64,128]{1,0:T(8,128)}, bf16[128,4096]{1,0:T(8,128)(2,1)}) custom-call(s32[2]{0:T(128)} %pad_add_fusion.where_ref, f32[64,512]{1,0:T(8,128)} %copy-done, f32[64,512]{1,0:T(8,128)} %copy-done.4, f32[64,512]{1,0:T(8,128)} %copy-done.3, f32[64,512]{1,0:T(8,128)} %copy-done.2, f32[64,512]{1,0:T(8,128)} %copy-done.5, f32[64,512]{1,0:T(8,128)} %copy-done.11, ...), custom_call_target="tpu_custom_call" | custom-call | tf_op jit(solution)/shard_map/gram/pallas_call | solution.py:203
  40.4 3.0 %collective-permute-start.13 = (f32[64,128]{1,0:T(8,128)}, f32[64,128]{1,0:T(8,128)S(1)}, u32[]{:S(2)}, u32[]{:S(2)}) collective-permute-start(f32[64,128]{1,0:T(8,128)} %get-tuple-element.18), channel_id=1, source_target_pairs={{0,24},{8,16},{16,8},{24,0},{32,56},{40,48},{48,40},{56,32},{64,88... | collective-permute-start | bytes 98312 | tf_op jit(solution)/shard_map/ppermute | solution.py:179
  43.4 0.6 collective-permute-start.12
  44.5 1.2 %collective-permute-done.13 = f32[64,128]{1,0:T(8,128)S(1)} collective-permute-done((f32[64,128]{1,0:T(8,128)}, f32[64,128]{1,0:T(8,128)S(1)}, u32[]{:S(2)}, u32[]{:S(2)}) %collective-permute-start.13) | collective-permute-done | bytes 32800 | tf_op jit(solution)/shard_map/ppermute | solution.py:179
  45.7 3.3 %collective-permute-done.12 = f32[64,128]{1,0:T(8,128)S(1)} collective-permute-done((f32[64,128]{1,0:T(8,128)}, f32[64,128]{1,0:T(8,128)S(1)}, u32[]{:S(2)}, u32[]{:S(2)}) %collective-permute-start.12) | collective-permute-done | bytes 32800 | tf_op jit(solution)/shard_map/ppermute | solution.py:179
  49.0 0.8 add_add_fusion.1
  49.8 2.0 %collective-permute-start.16 = (f32[64,128]{1,0:T(8,128)S(1)}, f32[64,128]{1,0:T(8,128)S(1)}, u32[]{:S(2)}, u32[]{:S(2)}) collective-permute-start(f32[64,128]{1,0:T(8,128)S(1)} %add_add_fusion.1), channel_id=1, source_target_pairs={{0,96},{8,104},{16,112},{24,120},{32,64},{40,72},{48,80},{56,88},{... | collective-permute-start | bytes 98312 | tf_op jit(solution)/shard_map/ppermute | solution.py:179
  51.8 1.4 %collective-permute-start.15 = (f32[64,128]{1,0:T(8,128)S(1)}, f32[64,128]{1,0:T(8,128)S(1)}, u32[]{:S(2)}, u32[]{:S(2)}) collective-permute-start(f32[64,128]{1,0:T(8,128)S(1)} %add_add_fusion.1), channel_id=1, source_target_pairs={{0,64},{8,72},{16,80},{24,88},{32,96},{40,104},{48,112},{56,120},{... | collective-permute-start | bytes 98312 | tf_op jit(solution)/shard_map/ppermute | solution.py:179
  53.3 1.4 %collective-permute-start.14 = (f32[64,128]{1,0:T(8,128)S(1)}, f32[64,128]{1,0:T(8,128)S(1)}, u32[]{:S(2)}, u32[]{:S(2)}) collective-permute-start(f32[64,128]{1,0:T(8,128)S(1)} %add_add_fusion.1), channel_id=1, source_target_pairs={{0,32},{8,40},{16,48},{24,56},{32,0},{40,8},{48,16},{56,24},{64,96... | collective-permute-start | bytes 98312 | tf_op jit(solution)/shard_map/ppermute | solution.py:179
  54.6 2.2 %collective-permute-done.15 = f32[64,128]{1,0:T(8,128)S(1)} collective-permute-done((f32[64,128]{1,0:T(8,128)S(1)}, f32[64,128]{1,0:T(8,128)S(1)}, u32[]{:S(2)}, u32[]{:S(2)}) %collective-permute-start.15) | collective-permute-done | bytes 32800 | tf_op jit(solution)/shard_map/ppermute | solution.py:179
  57.3 6.3 %collective-permute-start.17 = (f32[64,128]{1,0:T(8,128)S(1)}, f32[64,128]{1,0:T(8,128)S(1)}, u32[]{:S(2)}, u32[]{:S(2)}) collective-permute-start(f32[64,128]{1,0:T(8,128)S(1)} %add_add_fusion.one_ref), channel_id=1, source_target_pairs={{0,128},{8,136},{16,144},{24,152},{32,160},{40,168},{48,176},{56,1... | collective-permute-start | bytes 98312 | tf_op jit(solution)/shard_map/ppermute | solution.py:179
  63.6 1.9 %collective-permute-done.17.two_ref = f32[64,128]{1,0:T(8,128)S(1)} collective-permute-done((f32[64,128]{1,0:T(8,128)S(1)}, f32[64,128]{1,0:T(8,128)S(1)}, u32[]{:S(2)}, u32[]{:S(2)}) %collective-permute-start.17) | collective-permute-done | bytes 32800 | tf_op jit(solution)/shard_map/ppermute | solution.py:179
  65.5 0.6 copy-done.12
  66.1 14.9 %finish.1 = (f32[64,64]{1,0:T(8,128)}, f32[64,64]{1,0:T(8,128)}, f32[64,4096]{1,0:T(8,128)}, f32[64,4096]{1,0:T(8,128)}) custom-call(f32[64,128]{1,0:T(8,128)} %copy-done.1, f32[64,128]{1,0:T(8,128)} %copy-done.12, bf16[128,4096]{1,0:T(8,128)(2,1)} %get-tuple-element.19.panel_ref, f32[64,4096]{1,0:T(8,128)} %trail_ref.1), custom_call_target="tpu_custom_call" | custom-call | tf_op jit(solution)/shard_map/finish/pallas_call | solution.py:219
  (44 shorter events, 2.9 us)
Async XLA Ops:
  0.6 8.8 %copy-start.14 = (s32[64]{0:T(128)S(1)}, s32[64]{0:T(128)}, u32[]{:S(2)}) copy-start(s32[64]{0:T(128)} %pivots_ref.1) | copy-start | bytes 772
  4.7 6.7 %collective-permute-start = (f32[32,1024]{1,0:T(8,128)}, f32[32,1024]{1,0:T(8,128)S(1)}, u32[]{:S(2)}, u32[]{:S(2)}) collective-permute-start(f32[32,1024]{1,0:T(8,128)} %get-tuple-element.13), channel_id=1, source_target_pairs={{0,2},{1,3},{2,0},{3,1},{4,6},{5,7},{6,4},{7,5},{8,10},{9,11},{10,... | collective-permute-start | bytes 393224 | tf_op jit(solution)/shard_map/ppermute | solution.py:171
  6.3 8.7 %collective-permute-start.1 = (f32[32,1024]{1,0:T(8,128)}, f32[32,1024]{1,0:T(8,128)S(1)}, u32[]{:S(2)}, u32[]{:S(2)}) collective-permute-start(f32[32,1024]{1,0:T(8,128)} %get-tuple-element.14), channel_id=1, source_target_pairs={{0,4},{1,5},{2,6},{3,7},{4,0},{5,1},{6,2},{7,3},{8,12},{9,13},{10,... | collective-permute-start | bytes 393224 | tf_op jit(solution)/shard_map/ppermute | solution.py:171
  8.7 8.3 %collective-permute-start.2 = (f32[32,1024]{1,0:T(8,128)}, f32[32,1024]{1,0:T(8,128)S(1)}, u32[]{:S(2)}, u32[]{:S(2)}) collective-permute-start(f32[32,1024]{1,0:T(8,128)} %get-tuple-element.15), channel_id=1, source_target_pairs={{0,6},{1,7},{2,4},{3,5},{4,2},{5,3},{6,0},{7,1},{8,14},{9,15},{10,... | collective-permute-start | bytes 393224 | tf_op jit(solution)/shard_map/ppermute | solution.py:171
  9.5 7.5 %copy-start.13 = (s32[64]{0:T(128)}, s32[64]{0:T(128)S(1)}, u32[]{:S(2)}) copy-start(s32[64]{0:T(128)S(1)} %get-tuple-element.21.owners_ref) | copy-start | bytes 772
  11.4 5.7 %copy-start.7 = (f32[32,1024]{1,0:T(8,128)}, f32[32,1024]{1,0:T(8,128)S(1)}, u32[]{:S(2)}) copy-start(f32[32,1024]{1,0:T(8,128)S(1)} %collective-permute-done.rest_1_) | copy-start | bytes 393220
  15.0 2.1 %copy-start.9 = (f32[32,1024]{1,0:T(8,128)}, f32[32,1024]{1,0:T(8,128)S(1)}, u32[]{:S(2)}) copy-start(f32[32,1024]{1,0:T(8,128)S(1)} %collective-permute-done.1.rest_2_) | copy-start | bytes 393220
  17.0 0.6 copy-start.10
  22.1 1.6 %collective-permute-start.3 = (f32[64,512]{1,0:T(8,128)}, f32[64,512]{1,0:T(8,128)S(1)}, u32[]{:S(2)}, u32[]{:S(2)}) collective-permute-start(f32[64,512]{1,0:T(8,128)} %get-tuple-element.17), channel_id=1, source_target_pairs={{0,1},{1,0},{2,3},{3,2},{4,5},{5,4},{6,7},{7,6},{8,9},{9,8},{10,11... | collective-permute-start | bytes 393224 | tf_op jit(solution)/shard_map/ppermute | solution.py:176
  24.6 11.6 %copy-start = (f32[64,512]{1,0:T(8,128)}, f32[64,512]{1,0:T(8,128)S(1)}, u32[]{:S(2)}) copy-start(f32[64,512]{1,0:T(8,128)S(1)} %broadcast_select_fusion.rest_0_) | copy-start | bytes 393220
  24.6 9.7 %collective-permute-start.6 = (f32[64,512]{1,0:T(8,128)S(1)}, f32[64,512]{1,0:T(8,128)S(1)}, u32[]{:S(2)}, u32[]{:S(2)}) collective-permute-start(f32[64,512]{1,0:T(8,128)S(1)} %broadcast_select_fusion.rest_0_), channel_id=1, source_target_pairs={{0,6},{1,7},{2,4},{3,5},{4,2},{5,3},{6,0},{7,1},{8,14},{9,15},{10,... | collective-permute-start | bytes 393224 | tf_op jit(solution)/shard_map/ppermute | solution.py:171
  25.6 8.8 %collective-permute-start.5 = (f32[64,512]{1,0:T(8,128)S(1)}, f32[64,512]{1,0:T(8,128)S(1)}, u32[]{:S(2)}, u32[]{:S(2)}) collective-permute-start(f32[64,512]{1,0:T(8,128)S(1)} %broadcast_select_fusion.rest_0_), channel_id=1, source_target_pairs={{0,4},{1,5},{2,6},{3,7},{4,0},{5,1},{6,2},{7,3},{8,12},{9,13},{10,... | collective-permute-start | bytes 393224 | tf_op jit(solution)/shard_map/ppermute | solution.py:171
  26.1 8.8 %collective-permute-start.4 = (f32[64,512]{1,0:T(8,128)S(1)}, f32[64,512]{1,0:T(8,128)S(1)}, u32[]{:S(2)}, u32[]{:S(2)}) collective-permute-start(f32[64,512]{1,0:T(8,128)S(1)} %broadcast_select_fusion.rest_0_), channel_id=1, source_target_pairs={{0,2},{1,3},{2,0},{3,1},{4,6},{5,7},{6,4},{7,5},{8,10},{9,11},{10,... | collective-permute-start | bytes 393224 | tf_op jit(solution)/shard_map/ppermute | solution.py:171
  28.8 6.1 %collective-permute-start.7 = (f32[64,512]{1,0:T(8,128)S(1)}, f32[64,512]{1,0:T(8,128)S(1)}, u32[]{:S(2)}, u32[]{:S(2)}) collective-permute-start(f32[64,512]{1,0:T(8,128)S(1)} %broadcast_select_fusion.rest_0_), channel_id=1, source_target_pairs={{0,1},{1,0},{2,3},{3,2},{4,5},{5,4},{6,7},{7,6},{8,9},{9,8},{10,11... | collective-permute-start | bytes 393224 | tf_op jit(solution)/shard_map/ppermute | solution.py:176
  34.3 2.0 %copy-start.2 = (f32[64,512]{1,0:T(8,128)}, f32[64,512]{1,0:T(8,128)S(1)}, u32[]{:S(2)}) copy-start(f32[64,512]{1,0:T(8,128)S(1)} %collective-permute-done.6.rest_3_) | copy-start | bytes 393220
  34.3 1.3 %collective-permute-start.10 = (f32[64,512]{1,0:T(8,128)S(1)}, f32[64,512]{1,0:T(8,128)S(1)}, u32[]{:S(2)}, u32[]{:S(2)}) collective-permute-start(f32[64,512]{1,0:T(8,128)S(1)} %collective-permute-done.6.rest_3_), channel_id=1, source_target_pairs={{0,1},{1,0},{2,3},{3,2},{4,5},{5,4},{6,7},{7,6},{8,9},{9,8},{10,11... | collective-permute-start | bytes 393224 | tf_op jit(solution)/shard_map/ppermute | solution.py:176
  34.3 2.0 %copy-start.3 = (f32[64,512]{1,0:T(8,128)}, f32[64,512]{1,0:T(8,128)S(1)}, u32[]{:S(2)}) copy-start(f32[64,512]{1,0:T(8,128)S(1)} %collective-permute-done.5.rest_2_) | copy-start | bytes 393220
  34.3 1.5 %collective-permute-start.9 = (f32[64,512]{1,0:T(8,128)S(1)}, f32[64,512]{1,0:T(8,128)S(1)}, u32[]{:S(2)}, u32[]{:S(2)}) collective-permute-start(f32[64,512]{1,0:T(8,128)S(1)} %collective-permute-done.5.rest_2_), channel_id=1, source_target_pairs={{0,1},{1,0},{2,3},{3,2},{4,5},{5,4},{6,7},{7,6},{8,9},{9,8},{10,11... | collective-permute-start | bytes 393224 | tf_op jit(solution)/shard_map/ppermute | solution.py:176
  34.9 1.4 %copy-start.4 = (f32[64,512]{1,0:T(8,128)}, f32[64,512]{1,0:T(8,128)S(1)}, u32[]{:S(2)}) copy-start(f32[64,512]{1,0:T(8,128)S(1)} %collective-permute-done.4.rest_1_) | copy-start | bytes 393220
  34.9 1.3 %collective-permute-start.8 = (f32[64,512]{1,0:T(8,128)S(1)}, f32[64,512]{1,0:T(8,128)S(1)}, u32[]{:S(2)}, u32[]{:S(2)}) collective-permute-start(f32[64,512]{1,0:T(8,128)S(1)} %collective-permute-done.4.rest_1_), channel_id=1, source_target_pairs={{0,1},{1,0},{2,3},{3,2},{4,5},{5,4},{6,7},{7,6},{8,9},{9,8},{10,11... | collective-permute-start | bytes 393224 | tf_op jit(solution)/shard_map/ppermute | solution.py:176
  34.9 1.4 %copy-start.5 = (f32[64,512]{1,0:T(8,128)}, f32[64,512]{1,0:T(8,128)S(1)}, u32[]{:S(2)}) copy-start(f32[64,512]{1,0:T(8,128)S(1)} %collective-permute-done.7.rest_4_) | copy-start | bytes 393220
  35.7 0.7 copy-start.6
  35.8 0.7 copy-start.8
  36.5 0.6 copy-start.11
  40.4 5.3 %collective-permute-start.13 = (f32[64,128]{1,0:T(8,128)}, f32[64,128]{1,0:T(8,128)S(1)}, u32[]{:S(2)}, u32[]{:S(2)}) collective-permute-start(f32[64,128]{1,0:T(8,128)} %get-tuple-element.18), channel_id=1, source_target_pairs={{0,24},{8,16},{16,8},{24,0},{32,56},{40,48},{48,40},{56,32},{64,88... | collective-permute-start | bytes 98312 | tf_op jit(solution)/shard_map/ppermute | solution.py:179
  43.4 5.6 %collective-permute-start.12 = (f32[64,128]{1,0:T(8,128)}, f32[64,128]{1,0:T(8,128)S(1)}, u32[]{:S(2)}, u32[]{:S(2)}) collective-permute-start(f32[64,128]{1,0:T(8,128)} %get-tuple-element.18), channel_id=1, source_target_pairs={{0,16},{8,24},{16,0},{24,8},{32,48},{40,56},{48,32},{56,40},{64,80... | collective-permute-start | bytes 98312 | tf_op jit(solution)/shard_map/ppermute | solution.py:179
  44.0 5.0 %collective-permute-start.11 = (f32[64,128]{1,0:T(8,128)}, f32[64,128]{1,0:T(8,128)S(1)}, u32[]{:S(2)}, u32[]{:S(2)}) collective-permute-start(f32[64,128]{1,0:T(8,128)} %get-tuple-element.18), channel_id=1, source_target_pairs={{0,8},{8,0},{16,24},{24,16},{32,40},{40,32},{48,56},{56,48},{64,72... | collective-permute-start | bytes 98312 | tf_op jit(solution)/shard_map/ppermute | solution.py:179
  49.8 4.8 %collective-permute-start.16 = (f32[64,128]{1,0:T(8,128)S(1)}, f32[64,128]{1,0:T(8,128)S(1)}, u32[]{:S(2)}, u32[]{:S(2)}) collective-permute-start(f32[64,128]{1,0:T(8,128)S(1)} %add_add_fusion.1), channel_id=1, source_target_pairs={{0,96},{8,104},{16,112},{24,120},{32,64},{40,72},{48,80},{56,88},{... | collective-permute-start | bytes 98312 | tf_op jit(solution)/shard_map/ppermute | solution.py:179
  51.8 5.0 %collective-permute-start.15 = (f32[64,128]{1,0:T(8,128)S(1)}, f32[64,128]{1,0:T(8,128)S(1)}, u32[]{:S(2)}, u32[]{:S(2)}) collective-permute-start(f32[64,128]{1,0:T(8,128)S(1)} %add_add_fusion.1), channel_id=1, source_target_pairs={{0,64},{8,72},{16,80},{24,88},{32,96},{40,104},{48,112},{56,120},{... | collective-permute-start | bytes 98312 | tf_op jit(solution)/shard_map/ppermute | solution.py:179
  53.3 4.0 %collective-permute-start.14 = (f32[64,128]{1,0:T(8,128)S(1)}, f32[64,128]{1,0:T(8,128)S(1)}, u32[]{:S(2)}, u32[]{:S(2)}) collective-permute-start(f32[64,128]{1,0:T(8,128)S(1)} %add_add_fusion.1), channel_id=1, source_target_pairs={{0,32},{8,40},{16,48},{24,56},{32,0},{40,8},{48,16},{56,24},{64,96... | collective-permute-start | bytes 98312 | tf_op jit(solution)/shard_map/ppermute | solution.py:179
  57.2 8.2 %copy-start.1 = (f32[64,128]{1,0:T(8,128)}, f32[64,128]{1,0:T(8,128)S(1)}, u32[]{:S(2)}) copy-start(f32[64,128]{1,0:T(8,128)S(1)} %add_add_fusion.one_ref) | copy-start | bytes 98308
  57.3 8.2 %collective-permute-start.17 = (f32[64,128]{1,0:T(8,128)S(1)}, f32[64,128]{1,0:T(8,128)S(1)}, u32[]{:S(2)}, u32[]{:S(2)}) collective-permute-start(f32[64,128]{1,0:T(8,128)S(1)} %add_add_fusion.one_ref), channel_id=1, source_target_pairs={{0,128},{8,136},{16,144},{24,152},{32,160},{40,168},{48,176},{56,1... | collective-permute-start | bytes 98312 | tf_op jit(solution)/shard_map/ppermute | solution.py:179
  (1 other events, 0.6 us)

commit v2 on v1

--- a/solution.py
+++ b/solution.py
@@ -19,11 +19,12 @@
     return high, low
 
 
-def select_kernel(capacity, x_count, where_ref, pivots_ref, cand_ref, *rest):
+def select_kernel(x_count, pivots_ref, cand_ref, *rest):
     outs, (rows, sems) = rest[:x_count], rest[x_count:]
     cand_count, width = cand_ref.shape
     count = pivots_ref.shape[0]
-    me = where_ref[0] * CORES + where_ref[1]
+    me = lax.axis_index("col")
+    rows[...] = jnp.zeros_like(rows)
 
     def row_copy(pivot, slot):
         return pltpu.make_async_copy(
@@ -49,40 +50,32 @@
     lax.fori_loop(0, total, drain, 0)
     part = width // x_count
     for k in range(x_count):
-        begin = pl.multiple_of((where_ref[0] ^ k) * part, part)
+        begin = pl.multiple_of(((me // CORES) ^ k) * part, part)
         outs[k][...] = rows[:, pl.ds(begin, part)]
 
 
-def merge_kernel(x_count, where_ref, owners_ref, slots_ref, *rest):
+def merge_kernel(x_count, keys_ref, *rest):
     sources, (keep_ref, send_ref) = rest[:x_count], rest[x_count:]
     count, half = keep_ref.shape
-    my_x, my_core = where_ref[0], where_ref[1]
-    keep_at = pl.multiple_of(my_core * half, half)
-    send_at = pl.multiple_of((1 - my_core) * half, half)
-
-    def place(i, carry):
-        owner = owners_ref[i]
-        slot = slots_ref[i]
-        away = (owner // CORES) ^ my_x
-
-        for k in range(x_count):
-
-            @pl.when((owner % CORES == my_core) & (away == k))
-            def _():
-                keep_ref[pl.ds(i, 1), :] = sources[k][pl.ds(slot, 1), pl.ds(keep_at, half)]
-                send_ref[pl.ds(i, 1), :] = sources[k][pl.ds(slot, 1), pl.ds(send_at, half)]
-
-        return carry
-
-    lax.fori_loop(0, count, place, 0)
-
-
-def gram_kernel(x_count, where_ref, *rest):
+    held = x_count * sources[0].shape[0]
+    my_core = lax.axis_index("col") % CORES
+    lanes = lax.broadcasted_iota(jnp.int32, (count, held), 1)
+    pick = (keys_ref[...] == lanes).astype(jnp.float32).astype(jnp.bfloat16)
+    pick = jnp.concatenate([pick, pick], axis=1)
+    for out_ref, core in ((send_ref, 1 - my_core), (keep_ref, my_core)):
+        begin = pl.multiple_of(core * half, half)
+        value = jnp.concatenate([ref[:, pl.ds(begin, half)] for ref in sources], axis=0)
+        parts = jnp.concatenate(split_bf16(value), axis=0)
+        out_ref[...] = jnp.dot(pick, parts, preferred_element_type=jnp.float32)
+
+
+def gram_kernel(x_count, *rest):
     mine, other = rest[:x_count], rest[x_count : 2 * x_count]
     trail_ref, sums_ref, panel_ref = rest[2 * x_count :]
     count, piece = mine[0].shape
     width = trail_ref.shape[1]
-    my_x, my_core = where_ref[0], where_ref[1]
+    me = lax.axis_index("col")
+    my_x, my_core = me // CORES, me % CORES
     for k in range(x_count):
         for core, ref in ((my_core, mine[k]), (1 - my_core, other[k])):
             begin = pl.multiple_of(((my_x ^ k) * CORES + core) * piece, piece)
@@ -143,7 +136,9 @@
         high, low = split_bf16(jnp.concatenate([inverse * jnp.float32(root), weights], axis=0))
         left[...] = jnp.concatenate([high, high, low, low], axis=1)
 
-    block = panel_ref[...]
+    width = next_ref.shape[1]
+    here = pl.ds(pl.multiple_of(pl.program_id(0) * width, width), width)
+    block = panel_ref[:, here]
     both = jnp.dot(
         left[...], jnp.concatenate([block, block], axis=0), preferred_element_type=jnp.float32
     )
@@ -160,11 +155,12 @@
     piece = width // col_count
     root = float(np.sqrt(np.float32(width * row_count)))
     my_col = lax.axis_index("col")
-    place = jnp.stack([my_col // CORES, my_col % CORES]).astype(jnp.int32)
     owners = pivots // cand_count
     order = jnp.arange(count, dtype=jnp.int32)
     earlier = (owners[:, None] == owners[None, :]) & (order[None, :] < order[:, None])
     slots = jnp.sum(earlier.astype(jnp.int32), axis=1)
+    away = (owners // CORES) ^ (my_col // CORES)
+    keys = jnp.where(owners % CORES == my_col % CORES, away * capacity + slots, -1)[:, None]
     f32 = jnp.float32
 
     def to_x(array, k):
@@ -178,41 +174,41 @@
     def to_row(array, k):
         return lax.ppermute(array, "row", [(i, i ^ k) for i in range(row_count)])
 
+    def near(array):
+        return pltpu.with_memory_space_constraint(array, VMEM)
+
     in_vmem, in_smem = pl.BlockSpec(memory_space=VMEM), pl.BlockSpec(memory_space=SMEM)
     quarters = pl.pallas_call(
-        functools.partial(select_kernel, capacity, x_count),
-        out_shape=[jax.ShapeDtypeStruct((capacity, width // x_count), f32)] * x_count,
-        in_specs=[in_smem, in_smem, pl.BlockSpec(memory_space=pl.ANY)],
+        functools.partial(select_kernel, x_count),
+        out_shape=[VMEM((capacity, width // x_count), f32)] * x_count,
+        in_specs=[in_smem, pl.BlockSpec(memory_space=pl.ANY)],
         out_specs=[in_vmem] * x_count,
         scratch_shapes=[VMEM((capacity, width), f32), pltpu.SemaphoreType.DMA((capacity,))],
         name="select",
-    )(place, pivots, candidates)
+    )(pivots, candidates)
     arrived = [quarters[0]] + [to_x(quarters[k], k) for k in range(1, x_count)]
     keep, send = pl.pallas_call(
         functools.partial(merge_kernel, x_count),
-        out_shape=[jax.ShapeDtypeStruct((count, piece), f32)] * 2,
-        in_specs=[in_smem] * 3 + [in_vmem] * x_count,
+        out_shape=[VMEM((count, piece), f32)] * 2,
+        in_specs=[in_vmem] * (1 + x_count),
         out_specs=[in_vmem] * 2,
         name="merge",
-    )(place, owners, slots, *arrived)
-    passed = to_core(send)
-    own_core = (owners % CORES == my_col % CORES)[:, None]
-    own_piece = jnp.where(own_core, keep, passed)
+    )(near(keys), *map(near, arrived))
+    own_piece = keep + to_core(send)
     mine = [own_piece] + [to_x(own_piece, k) for k in range(1, x_count)]
     other = [to_core(array) for array in mine]
     sums, panel = pl.pallas_call(
         functools.partial(gram_kernel, x_count),
-        out_shape=[
-            jax.ShapeDtypeStruct((count, 2 * count), f32),
-            jax.ShapeDtypeStruct((2 * count, width), jnp.bfloat16),
-        ],
-        in_specs=[in_smem] + [in_vmem] * (2 * x_count + 1),
+        out_shape=[VMEM((count, 2 * count), f32), VMEM((2 * count, width), jnp.bfloat16)],
+        in_specs=[in_vmem] * (2 * x_count + 1),
         out_specs=[in_vmem] * 2,
         name="gram",
-    )(place, *mine, *other, trailing)
-    sums = (sums + to_row(sums, 1)) + (to_row(sums, 2) + to_row(sums, 3))
-    sums = (sums + to_row(sums, 4)) + (to_row(sums, 8) + to_row(sums, 12))
-    far = to_row(sums, 16)
+    )(*map(near, mine), *map(near, other), near(trailing))
+    step = 1
+    while step < row_count // 2:
+        sums = sums + to_row(sums, step)
+        step *= 2
+    far = to_row(sums, step)
     steps = col_count
     whole = lambda shape: pl.BlockSpec(shape, lambda i: (0, 0))
     block = lambda rows: pl.BlockSpec((rows, width // steps), lambda i: (0, i))
@@ -225,11 +221,11 @@
             jax.ShapeDtypeStruct((count, width), f32),
             jax.ShapeDtypeStruct((count, width), f32),
         ],
-        in_specs=[whole((count, 2 * count))] * 2 + [block(2 * count), block(count)],
+        in_specs=[in_vmem] * 3 + [block(count)],
         out_specs=[whole((count, count))] * 2 + [block(count)] * 2,
         scratch_shapes=[VMEM((2 * count, 4 * count), jnp.bfloat16)],
         name="finish",
-    )(sums, far, panel, trailing)
+    )(near(sums), near(far), near(panel), trailing)
 
 
 def solution(mesh):

time: 82.6 us -> 72.4 us (0.88)
  the two profiles are of different devices: /device:TPU:32 before, /device:TPU:16 now
where the time goes in v2:
time: 72.4 us; the launch traced here: 71.7 us
  waiting for transfers between devices  28.8 us (40%)
  starting transfers between devices  23.5 us (32%)
  Pallas kernels  18.3 us (25%)
  between operations  0.74 us (1%)
    pallas_call x1, Pallas kernels, on_device(): pl.pallas_call(functools.partial(finish_kernel, root), grid=(steps,), out...  14.6 us
    ppermute x5, starting transfers between devices, to_row(): return lax.ppermute(array, 'row', [(i, i ^ k) for i in range(row_count)])  14 us
    ppermute x5, waiting for transfers between devices, to_row(): return lax.ppermute(array, 'row', [(i, i ^ k) for i in range(row_count)])  13.5 us
    ppermute x6, waiting for transfers between devices, to_x(): lax.ppermute(array, 'col', [(i, (i // CORES ^ k) * CORES + i % CORES) for...  12.6 us
    ppermute x6, starting transfers between devices, to_x(): lax.ppermute(array, 'col', [(i, (i // CORES ^ k) * CORES + i % CORES) for...  8.97 us
    ppermute x5, waiting for transfers between devices, to_core(): return lax.ppermute(array, 'col', [(i, i ^ 1) for i in range(col_count)])  2.68 us
    pallas_call x1, Pallas kernels, on_device(): pl.pallas_call(functools.partial(select_kernel, x_count), out_shape=[VMEM...  2.46 us
  transfers between devices with their start and end apart: 16, of which 14 were waited for; matrix products, arithmetic and copies ran while one was open for 0% of the time, Pallas kernels for 0%

profile of v2, /device:TPU:16, one launch (start us, length us, event | category | flops | bytes accessed | tf_op | source)
XLA Modules:
  0.0 71.7 jit_solution(9850637964105616155)
XLA Ops:
  0.7 2.5 %select.17 = (f32[32,1024]{1,0:T(8,128)S(1)}, f32[32,1024]{1,0:T(8,128)S(1)}, f32[32,1024]{1,0:T(8,128)S(1)}, f32[32,1024]{1,0:T(8,128)S(1)}) custom-call(s32[64]{0:T(128)} %pivots_ref.1, f32[128,4096]{1,0:T(8,128)} %cand_ref.1), custom_call_target="tpu_custom_call" | custom-call | tf_op jit(solution)/shard_map/select/pallas_call | solution.py:181
  3.1 1.8 %collective-permute-start = (f32[32,1024]{1,0:T(8,128)S(1)}, f32[32,1024]{1,0:T(8,128)S(1)}, u32[]{:S(2)}, u32[]{:S(2)}) collective-permute-start(f32[32,1024]{1,0:T(8,128)S(1)} %get-tuple-element.13), channel_id=1, source_target_pairs={{0,2},{1,3},{2,0},{3,1},{4,6},{5,7},{6,4},{7,5},{8,10},{9,11},{10,... | collective-permute-start | bytes 393224 | tf_op jit(solution)/shard_map/ppermute | solution.py:167
  4.9 2.9 %collective-permute-start.1 = (f32[32,1024]{1,0:T(8,128)S(1)}, f32[32,1024]{1,0:T(8,128)S(1)}, u32[]{:S(2)}, u32[]{:S(2)}) collective-permute-start(f32[32,1024]{1,0:T(8,128)S(1)} %get-tuple-element.14), channel_id=1, source_target_pairs={{0,4},{1,5},{2,6},{3,7},{4,0},{5,1},{6,2},{7,3},{8,12},{9,13},{10,... | collective-permute-start | bytes 393224 | tf_op jit(solution)/shard_map/ppermute | solution.py:167
  7.9 0.2 convert_reduce_fusion
  8.2 0.1 copy.8.keys_ref
  8.2 1.3 %collective-permute-done.rest_1_ = f32[32,1024]{1,0:T(8,128)S(1)} collective-permute-done((f32[32,1024]{1,0:T(8,128)S(1)}, f32[32,1024]{1,0:T(8,128)S(1)}, u32[]{:S(2)}, u32[]{:S(2)}) %collective-permute-start) | collective-permute-done | bytes 131104 | tf_op jit(solution)/shard_map/ppermute | solution.py:167
  9.5 3.9 %collective-permute-done.1.rest_2_ = f32[32,1024]{1,0:T(8,128)S(1)} collective-permute-done((f32[32,1024]{1,0:T(8,128)S(1)}, f32[32,1024]{1,0:T(8,128)S(1)}, u32[]{:S(2)}, u32[]{:S(2)}) %collective-permute-start.1) | collective-permute-done | bytes 131104 | tf_op jit(solution)/shard_map/ppermute | solution.py:167
  13.5 1.8 %collective-permute-done.2.rest_3_ = f32[32,1024]{1,0:T(8,128)S(1)} collective-permute-done((f32[32,1024]{1,0:T(8,128)S(1)}, f32[32,1024]{1,0:T(8,128)S(1)}, u32[]{:S(2)}, u32[]{:S(2)}) %collective-permute-start.2) | collective-permute-done | bytes 131104 | tf_op jit(solution)/shard_map/ppermute | solution.py:167
  15.3 0.2 merge.1
  15.5 0.1 collective-permute-start.3
  15.6 1.3 %collective-permute-done.3 = f32[64,512]{1,0:T(8,128)S(1)} collective-permute-done((f32[64,512]{1,0:T(8,128)S(1)}, f32[64,512]{1,0:T(8,128)S(1)}, u32[]{:S(2)}, u32[]{:S(2)}) %collective-permute-start.3) | collective-permute-done | bytes 131104 | tf_op jit(solution)/shard_map/ppermute | solution.py:172
  17.0 1.4 %collective-permute-start.6 = (f32[64,512]{1,0:T(8,128)S(1)}, f32[64,512]{1,0:T(8,128)S(1)}, u32[]{:S(2)}, u32[]{:S(2)}) collective-permute-start(f32[64,512]{1,0:T(8,128)S(1)} %add.34.rest_0_), channel_id=1, source_target_pairs={{0,6},{1,7},{2,4},{3,5},{4,2},{5,3},{6,0},{7,1},{8,14},{9,15},{10,... | collective-permute-start | bytes 393224 | tf_op jit(solution)/shard_map/ppermute | solution.py:167
  18.4 0.3 collective-permute-start.5
  18.7 2.5 %collective-permute-start.4 = (f32[64,512]{1,0:T(8,128)S(1)}, f32[64,512]{1,0:T(8,128)S(1)}, u32[]{:S(2)}, u32[]{:S(2)}) collective-permute-start(f32[64,512]{1,0:T(8,128)S(1)} %add.34.rest_0_), channel_id=1, source_target_pairs={{0,2},{1,3},{2,0},{3,1},{4,6},{5,7},{6,4},{7,5},{8,10},{9,11},{10,... | collective-permute-start | bytes 393224 | tf_op jit(solution)/shard_map/ppermute | solution.py:167
  21.2 5.5 %collective-permute-done.6.rest_3_ = f32[64,512]{1,0:T(8,128)S(1)} collective-permute-done((f32[64,512]{1,0:T(8,128)S(1)}, f32[64,512]{1,0:T(8,128)S(1)}, u32[]{:S(2)}, u32[]{:S(2)}) %collective-permute-start.6) | collective-permute-done | bytes 131104 | tf_op jit(solution)/shard_map/ppermute | solution.py:167
  26.7 0.5 collective-permute-start.9
  27.2 0.1 collective-permute-done.4.rest_1_
  27.3 0.7 collective-permute-done.10.rest_7_
  28.0 0.2 collective-permute-done.9.rest_6_
  28.2 0.4 collective-permute-done.8.rest_5_
  28.6 1.0 %gram.1 = (f32[64,128]{1,0:T(8,128)S(1)}, bf16[128,4096]{1,0:T(8,128)(2,1)S(1)}) custom-call(f32[64,512]{1,0:T(8,128)S(1)} %add.34.rest_0_, f32[64,512]{1,0:T(8,128)S(1)} %collective-permute-done.4.rest_1_, f32[64,512]{1,0:T(8,128)S(1)} %collective-permute-done.5.rest_2_, f32[64,512]{1,0:T(8,128)S(1)} %collective-permute-done.6.rest_3_, ...), custom_call_target="tpu_custom_call" | custom-call | tf_op jit(solution)/shard_map/gram/pallas_call | solution.py:200
  29.6 1.4 %collective-permute-start.11 = (f32[64,128]{1,0:T(8,128)S(1)}, f32[64,128]{1,0:T(8,128)S(1)}, u32[]{:S(2)}, u32[]{:S(2)}) collective-permute-start(f32[64,128]{1,0:T(8,128)S(1)} %get-tuple-element.18), channel_id=1, source_target_pairs={{0,8},{8,0},{16,24},{24,16},{32,40},{40,32},{48,56},{56,48},{64,72... | collective-permute-start | bytes 98312 | tf_op jit(solution)/shard_map/ppermute | solution.py:175
  31.0 2.6 %collective-permute-done.11 = f32[64,128]{1,0:T(8,128)S(1)} collective-permute-done((f32[64,128]{1,0:T(8,128)S(1)}, f32[64,128]{1,0:T(8,128)S(1)}, u32[]{:S(2)}, u32[]{:S(2)}) %collective-permute-start.11) | collective-permute-done | bytes 32800 | tf_op jit(solution)/shard_map/ppermute | solution.py:175
  33.6 0.3 collective-permute-start.12
  33.9 5.1 %collective-permute-done.12 = f32[64,128]{1,0:T(8,128)S(1)} collective-permute-done((f32[64,128]{1,0:T(8,128)S(1)}, f32[64,128]{1,0:T(8,128)S(1)}, u32[]{:S(2)}, u32[]{:S(2)}) %collective-permute-start.12) | collective-permute-done | bytes 32800 | tf_op jit(solution)/shard_map/ppermute | solution.py:175
  39.0 1.9 %collective-permute-start.13 = (f32[64,128]{1,0:T(8,128)S(1)}, f32[64,128]{1,0:T(8,128)S(1)}, u32[]{:S(2)}, u32[]{:S(2)}) collective-permute-start(f32[64,128]{1,0:T(8,128)S(1)} %add.36), channel_id=1, source_target_pairs={{0,32},{8,40},{16,48},{24,56},{32,0},{40,8},{48,16},{56,24},{64,96... | collective-permute-start | bytes 98312 | tf_op jit(solution)/shard_map/ppermute | solution.py:175
  41.0 2.0 %collective-permute-done.13 = f32[64,128]{1,0:T(8,128)S(1)} collective-permute-done((f32[64,128]{1,0:T(8,128)S(1)}, f32[64,128]{1,0:T(8,128)S(1)}, u32[]{:S(2)}, u32[]{:S(2)}) %collective-permute-start.13) | collective-permute-done | bytes 32800 | tf_op jit(solution)/shard_map/ppermute | solution.py:175
  43.0 3.4 %collective-permute-start.14 = (f32[64,128]{1,0:T(8,128)S(1)}, f32[64,128]{1,0:T(8,128)S(1)}, u32[]{:S(2)}, u32[]{:S(2)}) collective-permute-start(f32[64,128]{1,0:T(8,128)S(1)} %add.37), channel_id=1, source_target_pairs={{0,64},{8,72},{16,80},{24,88},{32,96},{40,104},{48,112},{56,120},{... | collective-permute-start | bytes 98312 | tf_op jit(solution)/shard_map/ppermute | solution.py:175
  46.4 1.9 %collective-permute-done.14 = f32[64,128]{1,0:T(8,128)S(1)} collective-permute-done((f32[64,128]{1,0:T(8,128)S(1)}, f32[64,128]{1,0:T(8,128)S(1)}, u32[]{:S(2)}, u32[]{:S(2)}) %collective-permute-start.14) | collective-permute-done | bytes 32800 | tf_op jit(solution)/shard_map/ppermute | solution.py:175
  48.3 6.9 %collective-permute-start.15 = (f32[64,128]{1,0:T(8,128)S(1)}, f32[64,128]{1,0:T(8,128)S(1)}, u32[]{:S(2)}, u32[]{:S(2)}) collective-permute-start(f32[64,128]{1,0:T(8,128)S(1)} %add.38.one_ref), channel_id=1, source_target_pairs={{0,128},{8,136},{16,144},{24,152},{32,160},{40,168},{48,176},{56,1... | collective-permute-start | bytes 98312 | tf_op jit(solution)/shard_map/ppermute | solution.py:175
  55.2 1.9 %collective-permute-done.15.two_ref = f32[64,128]{1,0:T(8,128)S(1)} collective-permute-done((f32[64,128]{1,0:T(8,128)S(1)}, f32[64,128]{1,0:T(8,128)S(1)}, u32[]{:S(2)}, u32[]{:S(2)}) %collective-permute-start.15) | collective-permute-done | bytes 32800 | tf_op jit(solution)/shard_map/ppermute | solution.py:175
  57.1 14.6 %finish.1 = (f32[64,64]{1,0:T(8,128)}, f32[64,64]{1,0:T(8,128)}, f32[64,4096]{1,0:T(8,128)}, f32[64,4096]{1,0:T(8,128)}) custom-call(f32[64,128]{1,0:T(8,128)S(1)} %add.38.one_ref, f32[64,128]{1,0:T(8,128)S(1)} %collective-permute-done.15.two_ref, bf16[128,4096]{1,0:T(8,128)(2,1)S(1)} %get-tuple-element.19.panel_ref, f32[64,4096]{1,0:T(8,128)} %trail_ref.1), custom_call_target="tpu_custom_call" | custom-call | tf_op jit(solution)/shard_map/finish/pallas_call | solution.py:215
  (17 shorter events, 0.2 us)
Async XLA Ops:
  0.6 7.3 %copy-start.1 = (s32[64]{0:T(128)S(1)}, s32[64]{0:T(128)}, u32[]{:S(2)}) copy-start(s32[64]{0:T(128)} %pivots_ref.1) | copy-start | bytes 772
  0.6 28.0 %copy-start = (f32[64,4096]{1,0:T(8,128)S(1)}, f32[64,4096]{1,0:T(8,128)}, u32[]{:S(2)}) copy-start(f32[64,4096]{1,0:T(8,128)} %trail_ref.1) | copy-start | bytes 3145732
  3.1 6.4 %collective-permute-start = (f32[32,1024]{1,0:T(8,128)S(1)}, f32[32,1024]{1,0:T(8,128)S(1)}, u32[]{:S(2)}, u32[]{:S(2)}) collective-permute-start(f32[32,1024]{1,0:T(8,128)S(1)} %get-tuple-element.13), channel_id=1, source_target_pairs={{0,2},{1,3},{2,0},{3,1},{4,6},{5,7},{6,4},{7,5},{8,10},{9,11},{10,... | collective-permute-start | bytes 393224 | tf_op jit(solution)/shard_map/ppermute | solution.py:167
  4.9 8.6 %collective-permute-start.1 = (f32[32,1024]{1,0:T(8,128)S(1)}, f32[32,1024]{1,0:T(8,128)S(1)}, u32[]{:S(2)}, u32[]{:S(2)}) collective-permute-start(f32[32,1024]{1,0:T(8,128)S(1)} %get-tuple-element.14), channel_id=1, source_target_pairs={{0,4},{1,5},{2,6},{3,7},{4,0},{5,1},{6,2},{7,3},{8,12},{9,13},{10,... | collective-permute-start | bytes 393224 | tf_op jit(solution)/shard_map/ppermute | solution.py:167
  7.8 7.5 %collective-permute-start.2 = (f32[32,1024]{1,0:T(8,128)S(1)}, f32[32,1024]{1,0:T(8,128)S(1)}, u32[]{:S(2)}, u32[]{:S(2)}) collective-permute-start(f32[32,1024]{1,0:T(8,128)S(1)} %get-tuple-element.15), channel_id=1, source_target_pairs={{0,6},{1,7},{2,4},{3,5},{4,2},{5,3},{6,0},{7,1},{8,14},{9,15},{10,... | collective-permute-start | bytes 393224 | tf_op jit(solution)/shard_map/ppermute | solution.py:167
  15.5 1.4 %collective-permute-start.3 = (f32[64,512]{1,0:T(8,128)S(1)}, f32[64,512]{1,0:T(8,128)S(1)}, u32[]{:S(2)}, u32[]{:S(2)}) collective-permute-start(f32[64,512]{1,0:T(8,128)S(1)} %get-tuple-element.17), channel_id=1, source_target_pairs={{0,1},{1,0},{2,3},{3,2},{4,5},{5,4},{6,7},{7,6},{8,9},{9,8},{10,11... | collective-permute-start | bytes 393224 | tf_op jit(solution)/shard_map/ppermute | solution.py:172
  17.0 9.7 %collective-permute-start.6 = (f32[64,512]{1,0:T(8,128)S(1)}, f32[64,512]{1,0:T(8,128)S(1)}, u32[]{:S(2)}, u32[]{:S(2)}) collective-permute-start(f32[64,512]{1,0:T(8,128)S(1)} %add.34.rest_0_), channel_id=1, source_target_pairs={{0,6},{1,7},{2,4},{3,5},{4,2},{5,3},{6,0},{7,1},{8,14},{9,15},{10,... | collective-permute-start | bytes 393224 | tf_op jit(solution)/shard_map/ppermute | solution.py:167
  18.4 8.3 %collective-permute-start.5 = (f32[64,512]{1,0:T(8,128)S(1)}, f32[64,512]{1,0:T(8,128)S(1)}, u32[]{:S(2)}, u32[]{:S(2)}) collective-permute-start(f32[64,512]{1,0:T(8,128)S(1)} %add.34.rest_0_), channel_id=1, source_target_pairs={{0,4},{1,5},{2,6},{3,7},{4,0},{5,1},{6,2},{7,3},{8,12},{9,13},{10,... | collective-permute-start | bytes 393224 | tf_op jit(solution)/shard_map/ppermute | solution.py:167
  18.7 8.6 %collective-permute-start.4 = (f32[64,512]{1,0:T(8,128)S(1)}, f32[64,512]{1,0:T(8,128)S(1)}, u32[]{:S(2)}, u32[]{:S(2)}) collective-permute-start(f32[64,512]{1,0:T(8,128)S(1)} %add.34.rest_0_), channel_id=1, source_target_pairs={{0,2},{1,3},{2,0},{3,1},{4,6},{5,7},{6,4},{7,5},{8,10},{9,11},{10,... | collective-permute-start | bytes 393224 | tf_op jit(solution)/shard_map/ppermute | solution.py:167
  21.2 6.1 %collective-permute-start.7 = (f32[64,512]{1,0:T(8,128)S(1)}, f32[64,512]{1,0:T(8,128)S(1)}, u32[]{:S(2)}, u32[]{:S(2)}) collective-permute-start(f32[64,512]{1,0:T(8,128)S(1)} %add.34.rest_0_), channel_id=1, source_target_pairs={{0,1},{1,0},{2,3},{3,2},{4,5},{5,4},{6,7},{7,6},{8,9},{9,8},{10,11... | collective-permute-start | bytes 393224 | tf_op jit(solution)/shard_map/ppermute | solution.py:172
  26.7 1.3 %collective-permute-start.10 = (f32[64,512]{1,0:T(8,128)S(1)}, f32[64,512]{1,0:T(8,128)S(1)}, u32[]{:S(2)}, u32[]{:S(2)}) collective-permute-start(f32[64,512]{1,0:T(8,128)S(1)} %collective-permute-done.6.rest_3_), channel_id=1, source_target_pairs={{0,1},{1,0},{2,3},{3,2},{4,5},{5,4},{6,7},{7,6},{8,9},{9,8},{10,11... | collective-permute-start | bytes 393224 | tf_op jit(solution)/shard_map/ppermute | solution.py:172
  26.7 1.5 %collective-permute-start.9 = (f32[64,512]{1,0:T(8,128)S(1)}, f32[64,512]{1,0:T(8,128)S(1)}, u32[]{:S(2)}, u32[]{:S(2)}) collective-permute-start(f32[64,512]{1,0:T(8,128)S(1)} %collective-permute-done.5.rest_2_), channel_id=1, source_target_pairs={{0,1},{1,0},{2,3},{3,2},{4,5},{5,4},{6,7},{7,6},{8,9},{9,8},{10,11... | collective-permute-start | bytes 393224 | tf_op jit(solution)/shard_map/ppermute | solution.py:172
  27.3 1.3 %collective-permute-start.8 = (f32[64,512]{1,0:T(8,128)S(1)}, f32[64,512]{1,0:T(8,128)S(1)}, u32[]{:S(2)}, u32[]{:S(2)}) collective-permute-start(f32[64,512]{1,0:T(8,128)S(1)} %collective-permute-done.4.rest_1_), channel_id=1, source_target_pairs={{0,1},{1,0},{2,3},{3,2},{4,5},{5,4},{6,7},{7,6},{8,9},{9,8},{10,11... | collective-permute-start | bytes 393224 | tf_op jit(solution)/shard_map/ppermute | solution.py:172
  29.6 4.0 %collective-permute-start.11 = (f32[64,128]{1,0:T(8,128)S(1)}, f32[64,128]{1,0:T(8,128)S(1)}, u32[]{:S(2)}, u32[]{:S(2)}) collective-permute-start(f32[64,128]{1,0:T(8,128)S(1)} %get-tuple-element.18), channel_id=1, source_target_pairs={{0,8},{8,0},{16,24},{24,16},{32,40},{40,32},{48,56},{56,48},{64,72... | collective-permute-start | bytes 98312 | tf_op jit(solution)/shard_map/ppermute | solution.py:175
  33.6 5.4 %collective-permute-start.12 = (f32[64,128]{1,0:T(8,128)S(1)}, f32[64,128]{1,0:T(8,128)S(1)}, u32[]{:S(2)}, u32[]{:S(2)}) collective-permute-start(f32[64,128]{1,0:T(8,128)S(1)} %add.35), channel_id=1, source_target_pairs={{0,16},{8,24},{16,0},{24,8},{32,48},{40,56},{48,32},{56,40},{64,80... | collective-permute-start | bytes 98312 | tf_op jit(solution)/shard_map/ppermute | solution.py:175
  39.0 3.9 %collective-permute-start.13 = (f32[64,128]{1,0:T(8,128)S(1)}, f32[64,128]{1,0:T(8,128)S(1)}, u32[]{:S(2)}, u32[]{:S(2)}) collective-permute-start(f32[64,128]{1,0:T(8,128)S(1)} %add.36), channel_id=1, source_target_pairs={{0,32},{8,40},{16,48},{24,56},{32,0},{40,8},{48,16},{56,24},{64,96... | collective-permute-start | bytes 98312 | tf_op jit(solution)/shard_map/ppermute | solution.py:175
  43.0 5.3 %collective-permute-start.14 = (f32[64,128]{1,0:T(8,128)S(1)}, f32[64,128]{1,0:T(8,128)S(1)}, u32[]{:S(2)}, u32[]{:S(2)}) collective-permute-start(f32[64,128]{1,0:T(8,128)S(1)} %add.37), channel_id=1, source_target_pairs={{0,64},{8,72},{16,80},{24,88},{32,96},{40,104},{48,112},{56,120},{... | collective-permute-start | bytes 98312 | tf_op jit(solution)/shard_map/ppermute | solution.py:175
  48.3 8.8 %collective-permute-start.15 = (f32[64,128]{1,0:T(8,128)S(1)}, f32[64,128]{1,0:T(8,128)S(1)}, u32[]{:S(2)}, u32[]{:S(2)}) collective-permute-start(f32[64,128]{1,0:T(8,128)S(1)} %add.38.one_ref), channel_id=1, source_target_pairs={{0,128},{8,136},{16,144},{24,152},{32,160},{40,168},{48,176},{56,1... | collective-permute-start | bytes 98312 | tf_op jit(solution)/shard_map/ppermute | solution.py:175

commit v3 on v2

--- a/solution.py
+++ b/solution.py
@@ -41,7 +41,7 @@
 
         return slot + mine.astype(jnp.int32)
 
-    total = lax.fori_loop(0, count, fetch, jnp.int32(0))
+    total = lax.fori_loop(0, count, fetch, jnp.int32(0), unroll=8)
 
     def drain(slot, carry):
         row_copy(me * cand_count, slot).wait()
@@ -97,53 +97,95 @@
     sums_ref[...] = lead[:, : 2 * count] + lead[:, 2 * count :]
 
 
+def outer_sum(left, right):
+    def parts(value):
+        first = value.astype(jnp.bfloat16).astype(jnp.float32)
+        rest = value - first
+        second = rest.astype(jnp.bfloat16).astype(jnp.float32)
+        return first, second, rest - second
+
+    l1, l2, l3 = parts(left)
+    r1, r2, r3 = parts(right)
+    return lax.dot_general(
+        jnp.concatenate([l1, l1, l2, l2, l1, l3], axis=0).astype(jnp.bfloat16),
+        jnp.concatenate([r1, r2, r1, r2, r3, r1], axis=0).astype(jnp.bfloat16),
+        (((0,), (0,)), ((), ())),
+        preferred_element_type=jnp.float32,
+    )
+
+
 def eliminate(work):
-    count = work.shape[0]
-    rows = lax.broadcasted_iota(jnp.int32, work.shape, 0)
-    lanes = lax.broadcasted_iota(jnp.int32, work.shape, 1)
-    scale = jnp.zeros(work.shape, jnp.float32)
-    for j in range(count):
-        row = jnp.broadcast_to(work[j : j + 1, :], work.shape)
-        column = jnp.broadcast_to(work[:, j : j + 1], work.shape)
-        pivot = jnp.broadcast_to(column[j : j + 1, :], work.shape)
-        scale = jnp.where(rows == j, lax.rsqrt(pivot), scale)
-        factor = jnp.where(rows > j, column / pivot, 0.0)
-        here = lanes == j
-        work = jnp.where(here & (rows > j), 0.0, work) - factor * jnp.where(here, 1.0, row)
-    return work * scale, scale
-
-
-def finish_kernel(root, one_ref, two_ref, panel_ref, trail_ref, upper_ref, coef_ref, basis_ref, next_ref, left):
+    size = 8
+    count, width = work.shape
+    shape = (size, width)
+    blocks = [work[begin : begin + size] for begin in range(0, count, size)]
+    rows = lax.broadcasted_iota(jnp.int32, shape, 0)
+    lanes = lax.broadcasted_iota(jnp.int32, shape, 1)
+    scales = []
+    for b in range(len(blocks)):
+        block = blocks[b]
+        columns = [
+            jnp.broadcast_to(block[:, size * b + k : size * b + k + 1], shape) for k in range(size)
+        ]
+        scale = jnp.zeros(shape, jnp.float32)
+        for j in range(size):
+            pivot = jnp.broadcast_to(columns[j][j : j + 1], shape)
+            scale = jnp.where(rows == j, lax.rsqrt(pivot), scale)
+            below = rows > j
+            factor = jnp.where(below, columns[j] * (1.0 / pivot), 0.0)
+            for k in range(j + 1, size):
+                columns[k] -= factor * jnp.broadcast_to(columns[k][j : j + 1], shape)
+            here = lanes == size * b + j
+            row = jnp.where(here, 1.0, jnp.broadcast_to(block[j : j + 1], shape))
+            block = jnp.where(here & below, 0.0, block) - factor * row
+        block *= scale
+        blocks[b] = block
+        scales.append(scale)
+        if b + 1 < len(blocks):
+            place = lanes - size * b
+            inside = (place >= 0) & (place < size)
+            inverse = jnp.where(place < rows, block, jnp.where(place == rows, scale, 0.0))
+            update = outer_sum(block[:, :count], jnp.where(inside, inverse, block))
+            for c in range(b + 1, len(blocks)):
+                blocks[c] = jnp.where(inside, 0.0, blocks[c]) - update[size * c : size * (c + 1)]
+    return jnp.concatenate(blocks, axis=0), jnp.concatenate(scales, axis=0)
+
+
+def finish_kernel(
+    root, one_ref, two_ref, panel_ref, trail_ref, upper_ref, coef_ref, basis_ref, next_ref, trail, basis, left_over, in_sem, out_sems
+):
     count = one_ref.shape[0]
-
-    @pl.when(pl.program_id(0) == 0)
-    def _():
-        work, scale = eliminate(one_ref[...] + two_ref[...])
-        square = (count, count)
-        rows = lax.broadcasted_iota(jnp.int32, square, 0)
-        lanes = lax.broadcasted_iota(jnp.int32, square, 1)
-        factor, coef = work[:, :count], work[:, count:]
-        upper_ref[...] = jnp.where(lanes >= rows, factor, 0.0) * jnp.float32(1.0 / root)
-        coef_ref[...] = coef * jnp.float32(1.0 / root)
-        inverse = jnp.where(lanes < rows, factor, jnp.where(lanes == rows, scale[:, :count], 0.0))
-        weights = lax.dot_general(
-            coef,
-            inverse,
-            (((0,), (0,)), ((), ())),
-            preferred_element_type=jnp.float32,
-            precision=lax.Precision.HIGHEST,
-        )
-        high, low = split_bf16(jnp.concatenate([inverse * jnp.float32(root), weights], axis=0))
-        left[...] = jnp.concatenate([high, high, low, low], axis=1)
-
-    width = next_ref.shape[1]
-    here = pl.ds(pl.multiple_of(pl.program_id(0) * width, width), width)
-    block = panel_ref[:, here]
-    both = jnp.dot(
-        left[...], jnp.concatenate([block, block], axis=0), preferred_element_type=jnp.float32
-    )
-    basis_ref[...] = both[:count]
-    next_ref[...] = trail_ref[...] - both[count:]
+    fetch = pltpu.make_async_copy(trail_ref, trail, in_sem)
+    fetch.start()
+    work, scale = eliminate(one_ref[...] + two_ref[...])
+    square = (count, count)
+    rows = lax.broadcasted_iota(jnp.int32, square, 0)
+    lanes = lax.broadcasted_iota(jnp.int32, square, 1)
+    factor, coef = work[:, :count], work[:, count:]
+    upper_ref[...] = jnp.where(lanes >= rows, factor, 0.0) * jnp.float32(1.0 / root)
+    coef_ref[...] = coef * jnp.float32(1.0 / root)
+    inverse = jnp.where(lanes < rows, factor, jnp.where(lanes == rows, scale[:, :count], 0.0))
+    weights = outer_sum(coef, inverse)
+    high, low = split_bf16(jnp.concatenate([inverse * jnp.float32(root), weights], axis=0))
+    left = jnp.concatenate([high, high, low, low], axis=1)
+    fetch.wait()
+    chunks = out_sems.shape[0]
+    width = panel_ref.shape[1] // chunks
+    copies = []
+    for c in range(chunks):
+        here = slice(c * width, (c + 1) * width)
+        block = panel_ref[:, here]
+        both = jnp.dot(
+            left, jnp.concatenate([block, block], axis=0), preferred_element_type=jnp.float32
+        )
+        basis[:, here] = both[:count]
+        left_over[:, here] = trail[:, here] - both[count:]
+        for i, (source, target) in enumerate(((basis, basis_ref), (left_over, next_ref))):
+            copy = pltpu.make_async_copy(source.at[:, here], target.at[:, here], out_sems.at[c, i])
+            copy.start()
+            copies.append(copy)
+    for copy in copies:
+        copy.wait()
 
 
 def on_device(candidates, trailing, pivots):
@@ -204,26 +246,20 @@
         out_specs=[in_vmem] * 2,
         name="gram",
     )(*map(near, mine), *map(near, other), near(trailing))
-    step = 1
-    while step < row_count // 2:
+    steps = (1, 3, 4, 8, 28)
+    for step in steps[:-1]:
         sums = sums + to_row(sums, step)
-        step *= 2
-    far = to_row(sums, step)
-    steps = col_count
-    whole = lambda shape: pl.BlockSpec(shape, lambda i: (0, 0))
-    block = lambda rows: pl.BlockSpec((rows, width // steps), lambda i: (0, i))
+    far = to_row(sums, steps[-1])
+    anywhere = pl.BlockSpec(memory_space=pl.ANY)
+    large = (count, width)
     return pl.pallas_call(
         functools.partial(finish_kernel, root),
-        grid=(steps,),
-        out_shape=[
-            jax.ShapeDtypeStruct((count, count), f32),
-            jax.ShapeDtypeStruct((count, count), f32),
-            jax.ShapeDtypeStruct((count, width), f32),
-            jax.ShapeDtypeStruct((count, width), f32),
-        ],
-        in_specs=[in_vmem] * 3 + [block(count)],
-        out_specs=[whole((count, count))] * 2 + [block(count)] * 2,
-        scratch_shapes=[VMEM((2 * count, 4 * count), jnp.bfloat16)],
+        out_shape=[jax.ShapeDtypeStruct((count, count), f32)] * 2
+        + [jax.ShapeDtypeStruct(large, f32)] * 2,
+        in_specs=[in_vmem] * 3 + [anywhere],
+        out_specs=[in_vmem] * 2 + [anywhere] * 2,
+        scratch_shapes=[VMEM(large, f32)] * 3
+        + [pltpu.SemaphoreType.DMA(()), pltpu.SemaphoreType.DMA((4, 2))],
         name="finish",
     )(near(sums), near(far), near(panel), trailing)
 

time: 72.4 us -> 61.4 us (0.85)
  the two profiles are of different devices: /device:TPU:16 before, /device:TPU:32 now
where the time goes in v3:
time: 61.4 us; the launch traced here: 61.6 us
  waiting for transfers between devices  27.9 us (45%)
  starting transfers between devices  23.3 us (38%)
  Pallas kernels  9.27 us (15%)
  between operations  0.74 us (1%)
    ppermute x5, starting transfers between devices, to_row(): return lax.ppermute(array, 'row', [(i, i ^ k) for i in range(row_count)])  13.7 us
    ppermute x6, waiting for transfers between devices, to_x(): lax.ppermute(array, 'col', [(i, (i // CORES ^ k) * CORES + i % CORES) for...  13.2 us
    ppermute x5, waiting for transfers between devices, to_row(): return lax.ppermute(array, 'row', [(i, i ^ k) for i in range(row_count)])  12.1 us
    ppermute x6, starting transfers between devices, to_x(): lax.ppermute(array, 'col', [(i, (i // CORES ^ k) * CORES + i % CORES) for...  8.97 us
    pallas_call x1, Pallas kernels, on_device(): pl.pallas_call(functools.partial(finish_kernel, root), out_shape=[jax.Sha...  5.72 us
    ppermute x5, waiting for transfers between devices, to_core(): return lax.ppermute(array, 'col', [(i, i ^ 1) for i in range(col_count)])  2.68 us
    pallas_call x1, Pallas kernels, on_device(): pl.pallas_call(functools.partial(select_kernel, x_count), out_shape=[VMEM...  2.35 us
  transfers between devices with their start and end apart: 16, of which 14 were waited for; matrix products, arithmetic and copies ran while one was open for 0% of the time, Pallas kernels for 0%

profile of v3, /device:TPU:32, one launch (start us, length us, event | category | flops | bytes accessed | tf_op | source)
XLA Modules:
  0.0 61.6 jit_solution(7367695008030373555)
XLA Ops:
  0.7 2.4 %select.17 = (f32[32,1024]{1,0:T(8,128)S(1)}, f32[32,1024]{1,0:T(8,128)S(1)}, f32[32,1024]{1,0:T(8,128)S(1)}, f32[32,1024]{1,0:T(8,128)S(1)}) custom-call(s32[64]{0:T(128)} %pivots_ref.1, f32[128,4096]{1,0:T(8,128)} %cand_ref.1), custom_call_target="tpu_custom_call" | custom-call | tf_op jit(solution)/shard_map/select/pallas_call | solution.py:223
  3.0 1.8 %collective-permute-start = (f32[32,1024]{1,0:T(8,128)S(1)}, f32[32,1024]{1,0:T(8,128)S(1)}, u32[]{:S(2)}, u32[]{:S(2)}) collective-permute-start(f32[32,1024]{1,0:T(8,128)S(1)} %get-tuple-element.13), channel_id=1, source_target_pairs={{0,2},{1,3},{2,0},{3,1},{4,6},{5,7},{6,4},{7,5},{8,10},{9,11},{10,... | collective-permute-start | bytes 393224 | tf_op jit(solution)/shard_map/ppermute | solution.py:209
  4.8 2.7 %collective-permute-start.1 = (f32[32,1024]{1,0:T(8,128)S(1)}, f32[32,1024]{1,0:T(8,128)S(1)}, u32[]{:S(2)}, u32[]{:S(2)}) collective-permute-start(f32[32,1024]{1,0:T(8,128)S(1)} %get-tuple-element.14), channel_id=1, source_target_pairs={{0,4},{1,5},{2,6},{3,7},{4,0},{5,1},{6,2},{7,3},{8,12},{9,13},{10,... | collective-permute-start | bytes 393224 | tf_op jit(solution)/shard_map/ppermute | solution.py:209
  7.5 0.3 collective-permute-start.2
  7.8 0.2 convert_reduce_fusion
  8.0 0.1 copy.8.keys_ref
  8.1 1.0 %collective-permute-done.rest_1_ = f32[32,1024]{1,0:T(8,128)S(1)} collective-permute-done((f32[32,1024]{1,0:T(8,128)S(1)}, f32[32,1024]{1,0:T(8,128)S(1)}, u32[]{:S(2)}, u32[]{:S(2)}) %collective-permute-start) | collective-permute-done | bytes 131104 | tf_op jit(solution)/shard_map/ppermute | solution.py:209
  9.2 4.5 %collective-permute-done.1.rest_2_ = f32[32,1024]{1,0:T(8,128)S(1)} collective-permute-done((f32[32,1024]{1,0:T(8,128)S(1)}, f32[32,1024]{1,0:T(8,128)S(1)}, u32[]{:S(2)}, u32[]{:S(2)}) %collective-permute-start.1) | collective-permute-done | bytes 131104 | tf_op jit(solution)/shard_map/ppermute | solution.py:209
  13.7 2.1 %collective-permute-done.2.rest_3_ = f32[32,1024]{1,0:T(8,128)S(1)} collective-permute-done((f32[32,1024]{1,0:T(8,128)S(1)}, f32[32,1024]{1,0:T(8,128)S(1)}, u32[]{:S(2)}, u32[]{:S(2)}) %collective-permute-start.2) | collective-permute-done | bytes 131104 | tf_op jit(solution)/shard_map/ppermute | solution.py:209
  15.8 0.2 merge.1
  16.0 0.1 collective-permute-start.3
  16.1 1.3 %collective-permute-done.3 = f32[64,512]{1,0:T(8,128)S(1)} collective-permute-done((f32[64,512]{1,0:T(8,128)S(1)}, f32[64,512]{1,0:T(8,128)S(1)}, u32[]{:S(2)}, u32[]{:S(2)}) %collective-permute-start.3) | collective-permute-done | bytes 131104 | tf_op jit(solution)/shard_map/ppermute | solution.py:214
  17.5 0.8 %collective-permute-start.6 = (f32[64,512]{1,0:T(8,128)S(1)}, f32[64,512]{1,0:T(8,128)S(1)}, u32[]{:S(2)}, u32[]{:S(2)}) collective-permute-start(f32[64,512]{1,0:T(8,128)S(1)} %add.34.rest_0_), channel_id=1, source_target_pairs={{0,6},{1,7},{2,4},{3,5},{4,2},{5,3},{6,0},{7,1},{8,14},{9,15},{10,... | collective-permute-start | bytes 393224 | tf_op jit(solution)/shard_map/ppermute | solution.py:209
  18.3 0.9 %collective-permute-start.5 = (f32[64,512]{1,0:T(8,128)S(1)}, f32[64,512]{1,0:T(8,128)S(1)}, u32[]{:S(2)}, u32[]{:S(2)}) collective-permute-start(f32[64,512]{1,0:T(8,128)S(1)} %add.34.rest_0_), channel_id=1, source_target_pairs={{0,4},{1,5},{2,6},{3,7},{4,0},{5,1},{6,2},{7,3},{8,12},{9,13},{10,... | collective-permute-start | bytes 393224 | tf_op jit(solution)/shard_map/ppermute | solution.py:209
  19.1 2.5 %collective-permute-start.4 = (f32[64,512]{1,0:T(8,128)S(1)}, f32[64,512]{1,0:T(8,128)S(1)}, u32[]{:S(2)}, u32[]{:S(2)}) collective-permute-start(f32[64,512]{1,0:T(8,128)S(1)} %add.34.rest_0_), channel_id=1, source_target_pairs={{0,2},{1,3},{2,0},{3,1},{4,6},{5,7},{6,4},{7,5},{8,10},{9,11},{10,... | collective-permute-start | bytes 393224 | tf_op jit(solution)/shard_map/ppermute | solution.py:209
  21.6 5.5 %collective-permute-done.6.rest_3_ = f32[64,512]{1,0:T(8,128)S(1)} collective-permute-done((f32[64,512]{1,0:T(8,128)S(1)}, f32[64,512]{1,0:T(8,128)S(1)}, u32[]{:S(2)}, u32[]{:S(2)}) %collective-permute-start.6) | collective-permute-done | bytes 131104 | tf_op jit(solution)/shard_map/ppermute | solution.py:209
  27.1 0.5 collective-permute-start.9
  27.6 0.1 collective-permute-done.4.rest_1_
  27.7 0.7 %collective-permute-done.10.rest_7_ = f32[64,512]{1,0:T(8,128)S(1)} collective-permute-done((f32[64,512]{1,0:T(8,128)S(1)}, f32[64,512]{1,0:T(8,128)S(1)}, u32[]{:S(2)}, u32[]{:S(2)}) %collective-permute-start.10) | collective-permute-done | bytes 131104 | tf_op jit(solution)/shard_map/ppermute | solution.py:214
  28.5 0.2 collective-permute-done.9.rest_6_
  28.6 0.4 collective-permute-done.8.rest_5_
  29.1 1.0 %gram.1 = (f32[64,128]{1,0:T(8,128)S(1)}, bf16[128,4096]{1,0:T(8,128)(2,1)S(1)}) custom-call(f32[64,512]{1,0:T(8,128)S(1)} %add.34.rest_0_, f32[64,512]{1,0:T(8,128)S(1)} %collective-permute-done.4.rest_1_, f32[64,512]{1,0:T(8,128)S(1)} %collective-permute-done.5.rest_2_, f32[64,512]{1,0:T(8,128)S(1)} %collective-permute-done.6.rest_3_, ...), custom_call_target="tpu_custom_call" | custom-call | tf_op jit(solution)/shard_map/gram/pallas_call | solution.py:242
  30.1 1.7 %collective-permute-start.11 = (f32[64,128]{1,0:T(8,128)S(1)}, f32[64,128]{1,0:T(8,128)S(1)}, u32[]{:S(2)}, u32[]{:S(2)}) collective-permute-start(f32[64,128]{1,0:T(8,128)S(1)} %get-tuple-element.18), channel_id=1, source_target_pairs={{0,8},{8,0},{16,24},{24,16},{32,40},{40,32},{48,56},{56,48},{64,72... | collective-permute-start | bytes 98312 | tf_op jit(solution)/shard_map/ppermute | solution.py:217
  31.7 2.3 %collective-permute-done.11 = f32[64,128]{1,0:T(8,128)S(1)} collective-permute-done((f32[64,128]{1,0:T(8,128)S(1)}, f32[64,128]{1,0:T(8,128)S(1)}, u32[]{:S(2)}, u32[]{:S(2)}) %collective-permute-start.11) | collective-permute-done | bytes 32800 | tf_op jit(solution)/shard_map/ppermute | solution.py:217
  34.1 3.0 %collective-permute-start.12 = (f32[64,128]{1,0:T(8,128)S(1)}, f32[64,128]{1,0:T(8,128)S(1)}, u32[]{:S(2)}, u32[]{:S(2)}) collective-permute-start(f32[64,128]{1,0:T(8,128)S(1)} %add.35), channel_id=1, source_target_pairs={{0,24},{8,16},{16,8},{24,0},{32,56},{40,48},{48,40},{56,32},{64,88... | collective-permute-start | bytes 98312 | tf_op jit(solution)/shard_map/ppermute | solution.py:217
  37.1 2.1 %collective-permute-done.12 = f32[64,128]{1,0:T(8,128)S(1)} collective-permute-done((f32[64,128]{1,0:T(8,128)S(1)}, f32[64,128]{1,0:T(8,128)S(1)}, u32[]{:S(2)}, u32[]{:S(2)}) %collective-permute-start.12) | collective-permute-done | bytes 32800 | tf_op jit(solution)/shard_map/ppermute | solution.py:217
  39.3 3.8 %collective-permute-done.13 = f32[64,128]{1,0:T(8,128)S(1)} collective-permute-done((f32[64,128]{1,0:T(8,128)S(1)}, f32[64,128]{1,0:T(8,128)S(1)}, u32[]{:S(2)}, u32[]{:S(2)}) %collective-permute-start.13) | collective-permute-done | bytes 32800 | tf_op jit(solution)/shard_map/ppermute | solution.py:217
  43.1 3.3 %collective-permute-start.14 = (f32[64,128]{1,0:T(8,128)S(1)}, f32[64,128]{1,0:T(8,128)S(1)}, u32[]{:S(2)}, u32[]{:S(2)}) collective-permute-start(f32[64,128]{1,0:T(8,128)S(1)} %add.37), channel_id=1, source_target_pairs={{0,64},{8,72},{16,80},{24,88},{32,96},{40,104},{48,112},{56,120},{... | collective-permute-start | bytes 98312 | tf_op jit(solution)/shard_map/ppermute | solution.py:217
  46.4 1.9 %collective-permute-done.14 = f32[64,128]{1,0:T(8,128)S(1)} collective-permute-done((f32[64,128]{1,0:T(8,128)S(1)}, f32[64,128]{1,0:T(8,128)S(1)}, u32[]{:S(2)}, u32[]{:S(2)}) %collective-permute-start.14) | collective-permute-done | bytes 32800 | tf_op jit(solution)/shard_map/ppermute | solution.py:217
  48.3 5.7 %collective-permute-start.15 = (f32[64,128]{1,0:T(8,128)S(1)}, f32[64,128]{1,0:T(8,128)S(1)}, u32[]{:S(2)}, u32[]{:S(2)}) collective-permute-start(f32[64,128]{1,0:T(8,128)S(1)} %add.38.one_ref), channel_id=1, source_target_pairs={{0,224},{8,232},{16,240},{24,248},{32,192},{40,200},{48,208},{56,2... | collective-permute-start | bytes 98312 | tf_op jit(solution)/shard_map/ppermute | solution.py:217
  54.0 1.9 %collective-permute-done.15.two_ref = f32[64,128]{1,0:T(8,128)S(1)} collective-permute-done((f32[64,128]{1,0:T(8,128)S(1)}, f32[64,128]{1,0:T(8,128)S(1)}, u32[]{:S(2)}, u32[]{:S(2)}) %collective-permute-start.15) | collective-permute-done | bytes 32800 | tf_op jit(solution)/shard_map/ppermute | solution.py:217
  55.9 5.7 %finish.1 = (f32[64,64]{1,0:T(8,128)}, f32[64,64]{1,0:T(8,128)}, f32[64,4096]{1,0:T(8,128)}, f32[64,4096]{1,0:T(8,128)}) custom-call(f32[64,128]{1,0:T(8,128)S(1)} %add.38.one_ref, f32[64,128]{1,0:T(8,128)S(1)} %collective-permute-done.15.two_ref, bf16[128,4096]{1,0:T(8,128)(2,1)S(1)} %get-tuple-element.19.panel_ref, f32[64,4096]{1,0:T(8,128)} %trail_ref.1), custom_call_target="tpu_custom_call" | custom-call | tf_op jit(solution)/shard_map/finish/pallas_call | solution.py:255
  (17 shorter events, 0.2 us)
Async XLA Ops:
  0.6 7.2 %copy-start.1 = (s32[64]{0:T(128)S(1)}, s32[64]{0:T(128)}, u32[]{:S(2)}) copy-start(s32[64]{0:T(128)} %pivots_ref.1) | copy-start | bytes 772
  0.6 28.4 %copy-start = (f32[64,4096]{1,0:T(8,128)S(1)}, f32[64,4096]{1,0:T(8,128)}, u32[]{:S(2)}) copy-start(f32[64,4096]{1,0:T(8,128)} %trail_ref.1) | copy-start | bytes 3145732
  3.0 6.2 %collective-permute-start = (f32[32,1024]{1,0:T(8,128)S(1)}, f32[32,1024]{1,0:T(8,128)S(1)}, u32[]{:S(2)}, u32[]{:S(2)}) collective-permute-start(f32[32,1024]{1,0:T(8,128)S(1)} %get-tuple-element.13), channel_id=1, source_target_pairs={{0,2},{1,3},{2,0},{3,1},{4,6},{5,7},{6,4},{7,5},{8,10},{9,11},{10,... | collective-permute-start | bytes 393224 | tf_op jit(solution)/shard_map/ppermute | solution.py:209
  4.8 8.9 %collective-permute-start.1 = (f32[32,1024]{1,0:T(8,128)S(1)}, f32[32,1024]{1,0:T(8,128)S(1)}, u32[]{:S(2)}, u32[]{:S(2)}) collective-permute-start(f32[32,1024]{1,0:T(8,128)S(1)} %get-tuple-element.14), channel_id=1, source_target_pairs={{0,4},{1,5},{2,6},{3,7},{4,0},{5,1},{6,2},{7,3},{8,12},{9,13},{10,... | collective-permute-start | bytes 393224 | tf_op jit(solution)/shard_map/ppermute | solution.py:209
  7.5 8.3 %collective-permute-start.2 = (f32[32,1024]{1,0:T(8,128)S(1)}, f32[32,1024]{1,0:T(8,128)S(1)}, u32[]{:S(2)}, u32[]{:S(2)}) collective-permute-start(f32[32,1024]{1,0:T(8,128)S(1)} %get-tuple-element.15), channel_id=1, source_target_pairs={{0,6},{1,7},{2,4},{3,5},{4,2},{5,3},{6,0},{7,1},{8,14},{9,15},{10,... | collective-permute-start | bytes 393224 | tf_op jit(solution)/shard_map/ppermute | solution.py:209
  16.0 1.4 %collective-permute-start.3 = (f32[64,512]{1,0:T(8,128)S(1)}, f32[64,512]{1,0:T(8,128)S(1)}, u32[]{:S(2)}, u32[]{:S(2)}) collective-permute-start(f32[64,512]{1,0:T(8,128)S(1)} %get-tuple-element.17), channel_id=1, source_target_pairs={{0,1},{1,0},{2,3},{3,2},{4,5},{5,4},{6,7},{7,6},{8,9},{9,8},{10,11... | collective-permute-start | bytes 393224 | tf_op jit(solution)/shard_map/ppermute | solution.py:214
  17.5 9.7 %collective-permute-start.6 = (f32[64,512]{1,0:T(8,128)S(1)}, f32[64,512]{1,0:T(8,128)S(1)}, u32[]{:S(2)}, u32[]{:S(2)}) collective-permute-start(f32[64,512]{1,0:T(8,128)S(1)} %add.34.rest_0_), channel_id=1, source_target_pairs={{0,6},{1,7},{2,4},{3,5},{4,2},{5,3},{6,0},{7,1},{8,14},{9,15},{10,... | collective-permute-start | bytes 393224 | tf_op jit(solution)/shard_map/ppermute | solution.py:209
  18.3 8.9 %collective-permute-start.5 = (f32[64,512]{1,0:T(8,128)S(1)}, f32[64,512]{1,0:T(8,128)S(1)}, u32[]{:S(2)}, u32[]{:S(2)}) collective-permute-start(f32[64,512]{1,0:T(8,128)S(1)} %add.34.rest_0_), channel_id=1, source_target_pairs={{0,4},{1,5},{2,6},{3,7},{4,0},{5,1},{6,2},{7,3},{8,12},{9,13},{10,... | collective-permute-start | bytes 393224 | tf_op jit(solution)/shard_map/ppermute | solution.py:209
  19.1 8.6 %collective-permute-start.4 = (f32[64,512]{1,0:T(8,128)S(1)}, f32[64,512]{1,0:T(8,128)S(1)}, u32[]{:S(2)}, u32[]{:S(2)}) collective-permute-start(f32[64,512]{1,0:T(8,128)S(1)} %add.34.rest_0_), channel_id=1, source_target_pairs={{0,2},{1,3},{2,0},{3,1},{4,6},{5,7},{6,4},{7,5},{8,10},{9,11},{10,... | collective-permute-start | bytes 393224 | tf_op jit(solution)/shard_map/ppermute | solution.py:209
  21.6 6.1 %collective-permute-start.7 = (f32[64,512]{1,0:T(8,128)S(1)}, f32[64,512]{1,0:T(8,128)S(1)}, u32[]{:S(2)}, u32[]{:S(2)}) collective-permute-start(f32[64,512]{1,0:T(8,128)S(1)} %add.34.rest_0_), channel_id=1, source_target_pairs={{0,1},{1,0},{2,3},{3,2},{4,5},{5,4},{6,7},{7,6},{8,9},{9,8},{10,11... | collective-permute-start | bytes 393224 | tf_op jit(solution)/shard_map/ppermute | solution.py:214
  27.1 1.3 %collective-permute-start.10 = (f32[64,512]{1,0:T(8,128)S(1)}, f32[64,512]{1,0:T(8,128)S(1)}, u32[]{:S(2)}, u32[]{:S(2)}) collective-permute-start(f32[64,512]{1,0:T(8,128)S(1)} %collective-permute-done.6.rest_3_), channel_id=1, source_target_pairs={{0,1},{1,0},{2,3},{3,2},{4,5},{5,4},{6,7},{7,6},{8,9},{9,8},{10,11... | collective-permute-start | bytes 393224 | tf_op jit(solution)/shard_map/ppermute | solution.py:214
  27.1 1.5 %collective-permute-start.9 = (f32[64,512]{1,0:T(8,128)S(1)}, f32[64,512]{1,0:T(8,128)S(1)}, u32[]{:S(2)}, u32[]{:S(2)}) collective-permute-start(f32[64,512]{1,0:T(8,128)S(1)} %collective-permute-done.5.rest_2_), channel_id=1, source_target_pairs={{0,1},{1,0},{2,3},{3,2},{4,5},{5,4},{6,7},{7,6},{8,9},{9,8},{10,11... | collective-permute-start | bytes 393224 | tf_op jit(solution)/shard_map/ppermute | solution.py:214
  27.7 1.3 %collective-permute-start.8 = (f32[64,512]{1,0:T(8,128)S(1)}, f32[64,512]{1,0:T(8,128)S(1)}, u32[]{:S(2)}, u32[]{:S(2)}) collective-permute-start(f32[64,512]{1,0:T(8,128)S(1)} %collective-permute-done.4.rest_1_), channel_id=1, source_target_pairs={{0,1},{1,0},{2,3},{3,2},{4,5},{5,4},{6,7},{7,6},{8,9},{9,8},{10,11... | collective-permute-start | bytes 393224 | tf_op jit(solution)/shard_map/ppermute | solution.py:214
  30.1 4.0 %collective-permute-start.11 = (f32[64,128]{1,0:T(8,128)S(1)}, f32[64,128]{1,0:T(8,128)S(1)}, u32[]{:S(2)}, u32[]{:S(2)}) collective-permute-start(f32[64,128]{1,0:T(8,128)S(1)} %get-tuple-element.18), channel_id=1, source_target_pairs={{0,8},{8,0},{16,24},{24,16},{32,40},{40,32},{48,56},{56,48},{64,72... | collective-permute-start | bytes 98312 | tf_op jit(solution)/shard_map/ppermute | solution.py:217
  34.1 5.1 %collective-permute-start.12 = (f32[64,128]{1,0:T(8,128)S(1)}, f32[64,128]{1,0:T(8,128)S(1)}, u32[]{:S(2)}, u32[]{:S(2)}) collective-permute-start(f32[64,128]{1,0:T(8,128)S(1)} %add.35), channel_id=1, source_target_pairs={{0,24},{8,16},{16,8},{24,0},{32,56},{40,48},{48,40},{56,32},{64,88... | collective-permute-start | bytes 98312 | tf_op jit(solution)/shard_map/ppermute | solution.py:217
  39.2 3.9 %collective-permute-start.13 = (f32[64,128]{1,0:T(8,128)S(1)}, f32[64,128]{1,0:T(8,128)S(1)}, u32[]{:S(2)}, u32[]{:S(2)}) collective-permute-start(f32[64,128]{1,0:T(8,128)S(1)} %add.36), channel_id=1, source_target_pairs={{0,32},{8,40},{16,48},{24,56},{32,0},{40,8},{48,16},{56,24},{64,96... | collective-permute-start | bytes 98312 | tf_op jit(solution)/shard_map/ppermute | solution.py:217
  43.1 5.2 %collective-permute-start.14 = (f32[64,128]{1,0:T(8,128)S(1)}, f32[64,128]{1,0:T(8,128)S(1)}, u32[]{:S(2)}, u32[]{:S(2)}) collective-permute-start(f32[64,128]{1,0:T(8,128)S(1)} %add.37), channel_id=1, source_target_pairs={{0,64},{8,72},{16,80},{24,88},{32,96},{40,104},{48,112},{56,120},{... | collective-permute-start | bytes 98312 | tf_op jit(solution)/shard_map/ppermute | solution.py:217
  48.3 7.6 %collective-permute-start.15 = (f32[64,128]{1,0:T(8,128)S(1)}, f32[64,128]{1,0:T(8,128)S(1)}, u32[]{:S(2)}, u32[]{:S(2)}) collective-permute-start(f32[64,128]{1,0:T(8,128)S(1)} %add.38.one_ref), channel_id=1, source_target_pairs={{0,224},{8,232},{16,240},{24,248},{32,192},{40,200},{48,208},{56,2... | collective-permute-start | bytes 98312 | tf_op jit(solution)/shard_map/ppermute | solution.py:217

commit v4 on v3

--- a/solution.py
+++ b/solution.py
@@ -77,7 +77,8 @@
     me = lax.axis_index("col")
     my_x, my_core = me // CORES, me % CORES
     for k in range(x_count):
-        for core, ref in ((my_core, mine[k]), (1 - my_core, other[k])):
+        near_core = my_core if k == 0 else 1 - my_core
+        for core, ref in ((near_core, mine[k]), (1 - near_core, other[k])):
             begin = pl.multiple_of(((my_x ^ k) * CORES + core) * piece, piece)
             high, low = split_bf16(ref[...])
             panel_ref[0:count, pl.ds(begin, piece)] = high
@@ -202,13 +203,12 @@
     earlier = (owners[:, None] == owners[None, :]) & (order[None, :] < order[:, None])
     slots = jnp.sum(earlier.astype(jnp.int32), axis=1)
     away = (owners // CORES) ^ (my_col // CORES)
-    keys = jnp.where(owners % CORES == my_col % CORES, away * capacity + slots, -1)[:, None]
+    held = (owners % CORES == my_col % CORES) == (away == 0)
+    keys = jnp.where(held, away * capacity + slots, -1)[:, None]
     f32 = jnp.float32
 
     def to_x(array, k):
-        return lax.ppermute(
-            array, "col", [(i, ((i // CORES) ^ k) * CORES + i % CORES) for i in range(col_count)]
-        )
+        return lax.ppermute(array, "col", [(i, i ^ (CORES * k + 1)) for i in range(col_count)])
 
     def to_core(array):
         return lax.ppermute(array, "col", [(i, i ^ 1) for i in range(col_count)])
@@ -246,10 +246,9 @@
         out_specs=[in_vmem] * 2,
         name="gram",
     )(*map(near, mine), *map(near, other), near(trailing))
-    steps = (1, 3, 4, 8, 28)
-    for step in steps[:-1]:
-        sums = sums + to_row(sums, step)
-    far = to_row(sums, steps[-1])
+    for step in (1, 4):
+        sums = (sums + to_row(sums, step)) + (to_row(sums, 2 * step) + to_row(sums, 3 * step))
+    far = to_row(sums, 28)
     anywhere = pl.BlockSpec(memory_space=pl.ANY)
     large = (count, width)
     return pl.pallas_call(

time: 61.4 us -> 60.7 us (0.989)
  waiting for transfers between devices: 27.9 us -> 25.8 us
  starting transfers between devices: 23.3 us -> 24 us
    ppermute x5 -> x7, waiting for transfers between devices: 12.1 us -> 8.82 us  [to_row(): return lax.ppermute(array, 'row', [(i, i ^ k) for i in range(row_count)])]
    ppermute x6, waiting for transfers between devices: 13.2 us -> 14.7 us  [to_x(): lax.ppermute(array, 'col', [(i, i ^ CORES * k + 1) for i in range(col_cou...]
    ppermute x5 -> x7, starting transfers between devices: 13.7 us -> 14.9 us  [to_row(): return lax.ppermute(array, 'row', [(i, i ^ k) for i in range(row_count)])]
    ppermute x6, starting transfers between devices: 8.97 us -> 7.8 us  [to_x(): lax.ppermute(array, 'col', [(i, i ^ CORES * k + 1) for i in range(col_cou...]
    ppermute x5, starting transfers between devices: 0.61 us -> 1.35 us  [to_core(): return lax.ppermute(array, 'col', [(i, i ^ 1) for i in range(col_count)])]
  transfers between devices with their start and end apart: 16 -> 18, of which waited for: 14 -> 13; matrix products, arithmetic and copies ran while one was open for 0% -> 0% of each run, Pallas kernels for 0% -> 0%
where the time goes in v4:
time: 60.7 us; the launch traced here: 60.4 us
  waiting for transfers between devices  25.8 us (43%)
  starting transfers between devices  24 us (40%)
  Pallas kernels  9.49 us (16%)
  between operations  0.74 us (1%)
    ppermute x7, starting transfers between devices, to_row(): return lax.ppermute(array, 'row', [(i, i ^ k) for i in range(row_count)])  14.9 us
    ppermute x6, waiting for transfers between devices, to_x(): lax.ppermute(array, 'col', [(i, i ^ CORES * k + 1) for i in range(col_cou...  14.7 us
    ppermute x7, waiting for transfers between devices, to_row(): return lax.ppermute(array, 'row', [(i, i ^ k) for i in range(row_count)])  8.82 us
    ppermute x6, starting transfers between devices, to_x(): lax.ppermute(array, 'col', [(i, i ^ CORES * k + 1) for i in range(col_cou...  7.8 us
    pallas_call x1, Pallas kernels, on_device(): pl.pallas_call(functools.partial(finish_kernel, root), out_shape=[jax.Sha...  5.72 us
    pallas_call x1, Pallas kernels, on_device(): pl.pallas_call(functools.partial(select_kernel, x_count), out_shape=[VMEM...  2.57 us
    ppermute x5, waiting for transfers between devices, to_core(): return lax.ppermute(array, 'col', [(i, i ^ 1) for i in range(col_count)])  2.29 us
    ppermute x5, starting transfers between devices, to_core(): return lax.ppermute(array, 'col', [(i, i ^ 1) for i in range(col_count)])  1.35 us
  transfers between devices with their start and end apart: 18, of which 13 were waited for; matrix products, arithmetic and copies ran while one was open for 0% of the time, Pallas kernels for 0%

profile of v4, /device:TPU:32, one launch (start us, length us, event | category | flops | bytes accessed | tf_op | source)
XLA Modules:
  0.0 60.4 jit_solution(6640721842922399503)
XLA Ops:
  0.7 2.6 %select.17 = (f32[32,1024]{1,0:T(8,128)S(1)}, f32[32,1024]{1,0:T(8,128)S(1)}, f32[32,1024]{1,0:T(8,128)S(1)}, f32[32,1024]{1,0:T(8,128)S(1)}) custom-call(s32[64]{0:T(128)} %pivots_ref.1, f32[128,4096]{1,0:T(8,128)} %cand_ref.1), custom_call_target="tpu_custom_call" | custom-call | tf_op jit(solution)/shard_map/select/pallas_call | solution.py:223
  3.2 0.9 %collective-permute-start = (f32[32,1024]{1,0:T(8,128)S(1)}, f32[32,1024]{1,0:T(8,128)S(1)}, u32[]{:S(2)}, u32[]{:S(2)}) collective-permute-start(f32[32,1024]{1,0:T(8,128)S(1)} %get-tuple-element.13), channel_id=1, source_target_pairs={{0,3},{1,2},{2,1},{3,0},{4,7},{5,6},{6,5},{7,4},{8,11},{9,10},{10,... | collective-permute-start | bytes 393224 | tf_op jit(solution)/shard_map/ppermute | solution.py:211
  4.1 3.0 %collective-permute-start.1 = (f32[32,1024]{1,0:T(8,128)S(1)}, f32[32,1024]{1,0:T(8,128)S(1)}, u32[]{:S(2)}, u32[]{:S(2)}) collective-permute-start(f32[32,1024]{1,0:T(8,128)S(1)} %get-tuple-element.14), channel_id=1, source_target_pairs={{0,5},{1,4},{2,7},{3,6},{4,1},{5,0},{6,3},{7,2},{8,13},{9,12},{10,... | collective-permute-start | bytes 393224 | tf_op jit(solution)/shard_map/ppermute | solution.py:211
  7.1 0.2 collective-permute-start.2
  7.7 1.3 %collective-permute-done.rest_1_ = f32[32,1024]{1,0:T(8,128)S(1)} collective-permute-done((f32[32,1024]{1,0:T(8,128)S(1)}, f32[32,1024]{1,0:T(8,128)S(1)}, u32[]{:S(2)}, u32[]{:S(2)}) %collective-permute-start) | collective-permute-done | bytes 131104 | tf_op jit(solution)/shard_map/ppermute | solution.py:211
  9.0 4.9 %collective-permute-done.1.rest_2_ = f32[32,1024]{1,0:T(8,128)S(1)} collective-permute-done((f32[32,1024]{1,0:T(8,128)S(1)}, f32[32,1024]{1,0:T(8,128)S(1)}, u32[]{:S(2)}, u32[]{:S(2)}) %collective-permute-start.1) | collective-permute-done | bytes 131104 | tf_op jit(solution)/shard_map/ppermute | solution.py:211
  14.0 2.8 %collective-permute-done.2.rest_3_ = f32[32,1024]{1,0:T(8,128)S(1)} collective-permute-done((f32[32,1024]{1,0:T(8,128)S(1)}, f32[32,1024]{1,0:T(8,128)S(1)}, u32[]{:S(2)}, u32[]{:S(2)}) %collective-permute-start.2) | collective-permute-done | bytes 131104 | tf_op jit(solution)/shard_map/ppermute | solution.py:211
  16.8 0.2 merge.1
  17.2 1.2 %collective-permute-done.3 = f32[64,512]{1,0:T(8,128)S(1)} collective-permute-done((f32[64,512]{1,0:T(8,128)S(1)}, f32[64,512]{1,0:T(8,128)S(1)}, u32[]{:S(2)}, u32[]{:S(2)}) %collective-permute-start.3) | collective-permute-done | bytes 131104 | tf_op jit(solution)/shard_map/ppermute | solution.py:214
  18.5 0.4 collective-permute-start.6
  18.9 0.6 %collective-permute-start.5 = (f32[64,512]{1,0:T(8,128)S(1)}, f32[64,512]{1,0:T(8,128)S(1)}, u32[]{:S(2)}, u32[]{:S(2)}) collective-permute-start(f32[64,512]{1,0:T(8,128)S(1)} %add.40.rest_0_), channel_id=1, source_target_pairs={{0,5},{1,4},{2,7},{3,6},{4,1},{5,0},{6,3},{7,2},{8,13},{9,12},{10,... | collective-permute-start | bytes 393224 | tf_op jit(solution)/shard_map/ppermute | solution.py:211
  19.5 2.6 %collective-permute-start.4 = (f32[64,512]{1,0:T(8,128)S(1)}, f32[64,512]{1,0:T(8,128)S(1)}, u32[]{:S(2)}, u32[]{:S(2)}) collective-permute-start(f32[64,512]{1,0:T(8,128)S(1)} %add.40.rest_0_), channel_id=1, source_target_pairs={{0,3},{1,2},{2,1},{3,0},{4,7},{5,6},{6,5},{7,4},{8,11},{9,10},{10,... | collective-permute-start | bytes 393224 | tf_op jit(solution)/shard_map/ppermute | solution.py:211
  22.2 0.3 collective-permute-start.7
  22.5 5.6 %collective-permute-done.6.rest_3_ = f32[64,512]{1,0:T(8,128)S(1)} collective-permute-done((f32[64,512]{1,0:T(8,128)S(1)}, f32[64,512]{1,0:T(8,128)S(1)}, u32[]{:S(2)}, u32[]{:S(2)}) %collective-permute-start.6) | collective-permute-done | bytes 131104 | tf_op jit(solution)/shard_map/ppermute | solution.py:211
  28.2 0.4 collective-permute-start.9
  28.6 0.3 collective-permute-start.8
  28.9 0.5 collective-permute-done.10.rest_7_
  29.6 0.3 collective-permute-done.8.rest_5_
  30.0 1.0 %gram.1 = (f32[64,128]{1,0:T(8,128)S(1)}, bf16[128,4096]{1,0:T(8,128)(2,1)S(1)}) custom-call(f32[64,512]{1,0:T(8,128)S(1)} %add.40.rest_0_, f32[64,512]{1,0:T(8,128)S(1)} %collective-permute-done.4.rest_1_, f32[64,512]{1,0:T(8,128)S(1)} %collective-permute-done.5.rest_2_, f32[64,512]{1,0:T(8,128)S(1)} %collective-permute-done.6.rest_3_, ...), custom_call_target="tpu_custom_call" | custom-call | tf_op jit(solution)/shard_map/gram/pallas_call | solution.py:242
  30.9 3.1 %collective-permute-start.13 = (f32[64,128]{1,0:T(8,128)S(1)}, f32[64,128]{1,0:T(8,128)S(1)}, u32[]{:S(2)}, u32[]{:S(2)}) collective-permute-start(f32[64,128]{1,0:T(8,128)S(1)} %get-tuple-element.18), channel_id=1, source_target_pairs={{0,24},{8,16},{16,8},{24,0},{32,56},{40,48},{48,40},{56,32},{64,88... | collective-permute-start | bytes 98312 | tf_op jit(solution)/shard_map/ppermute | solution.py:217
  34.0 0.6 %collective-permute-start.12 = (f32[64,128]{1,0:T(8,128)S(1)}, f32[64,128]{1,0:T(8,128)S(1)}, u32[]{:S(2)}, u32[]{:S(2)}) collective-permute-start(f32[64,128]{1,0:T(8,128)S(1)} %get-tuple-element.18), channel_id=1, source_target_pairs={{0,16},{8,24},{16,0},{24,8},{32,48},{40,56},{48,32},{56,40},{64,80... | collective-permute-start | bytes 98312 | tf_op jit(solution)/shard_map/ppermute | solution.py:217
  34.7 0.4 collective-permute-start.11
  35.1 1.0 %collective-permute-done.13 = f32[64,128]{1,0:T(8,128)S(1)} collective-permute-done((f32[64,128]{1,0:T(8,128)S(1)}, f32[64,128]{1,0:T(8,128)S(1)}, u32[]{:S(2)}, u32[]{:S(2)}) %collective-permute-start.13) | collective-permute-done | bytes 32800 | tf_op jit(solution)/shard_map/ppermute | solution.py:217
  36.1 3.3 %collective-permute-done.12 = f32[64,128]{1,0:T(8,128)S(1)} collective-permute-done((f32[64,128]{1,0:T(8,128)S(1)}, f32[64,128]{1,0:T(8,128)S(1)}, u32[]{:S(2)}, u32[]{:S(2)}) %collective-permute-start.12) | collective-permute-done | bytes 32800 | tf_op jit(solution)/shard_map/ppermute | solution.py:217
  39.5 2.0 %collective-permute-start.16 = (f32[64,128]{1,0:T(8,128)S(1)}, f32[64,128]{1,0:T(8,128)S(1)}, u32[]{:S(2)}, u32[]{:S(2)}) collective-permute-start(f32[64,128]{1,0:T(8,128)S(1)} %add_add_fusion.1), channel_id=1, source_target_pairs={{0,96},{8,104},{16,112},{24,120},{32,64},{40,72},{48,80},{56,88},{... | collective-permute-start | bytes 98312 | tf_op jit(solution)/shard_map/ppermute | solution.py:217
  41.5 1.4 %collective-permute-start.15 = (f32[64,128]{1,0:T(8,128)S(1)}, f32[64,128]{1,0:T(8,128)S(1)}, u32[]{:S(2)}, u32[]{:S(2)}) collective-permute-start(f32[64,128]{1,0:T(8,128)S(1)} %add_add_fusion.1), channel_id=1, source_target_pairs={{0,64},{8,72},{16,80},{24,88},{32,96},{40,104},{48,112},{56,120},{... | collective-permute-start | bytes 98312 | tf_op jit(solution)/shard_map/ppermute | solution.py:217
  42.9 1.4 %collective-permute-start.14 = (f32[64,128]{1,0:T(8,128)S(1)}, f32[64,128]{1,0:T(8,128)S(1)}, u32[]{:S(2)}, u32[]{:S(2)}) collective-permute-start(f32[64,128]{1,0:T(8,128)S(1)} %add_add_fusion.1), channel_id=1, source_target_pairs={{0,32},{8,40},{16,48},{24,56},{32,0},{40,8},{48,16},{56,24},{64,96... | collective-permute-start | bytes 98312 | tf_op jit(solution)/shard_map/ppermute | solution.py:217
  44.3 2.2 %collective-permute-done.15 = f32[64,128]{1,0:T(8,128)S(1)} collective-permute-done((f32[64,128]{1,0:T(8,128)S(1)}, f32[64,128]{1,0:T(8,128)S(1)}, u32[]{:S(2)}, u32[]{:S(2)}) %collective-permute-start.15) | collective-permute-done | bytes 32800 | tf_op jit(solution)/shard_map/ppermute | solution.py:217
  46.5 0.4 collective-permute-done.14
  46.9 5.9 %collective-permute-start.17 = (f32[64,128]{1,0:T(8,128)S(1)}, f32[64,128]{1,0:T(8,128)S(1)}, u32[]{:S(2)}, u32[]{:S(2)}) collective-permute-start(f32[64,128]{1,0:T(8,128)S(1)} %add_add_fusion.one_ref), channel_id=1, source_target_pairs={{0,224},{8,232},{16,240},{24,248},{32,192},{40,200},{48,208},{56,2... | collective-permute-start | bytes 98312 | tf_op jit(solution)/shard_map/ppermute | solution.py:217
  52.8 1.9 %collective-permute-done.17.two_ref = f32[64,128]{1,0:T(8,128)S(1)} collective-permute-done((f32[64,128]{1,0:T(8,128)S(1)}, f32[64,128]{1,0:T(8,128)S(1)}, u32[]{:S(2)}, u32[]{:S(2)}) %collective-permute-start.17) | collective-permute-done | bytes 32800 | tf_op jit(solution)/shard_map/ppermute | solution.py:217
  54.7 5.7 %finish.1 = (f32[64,64]{1,0:T(8,128)}, f32[64,64]{1,0:T(8,128)}, f32[64,4096]{1,0:T(8,128)}, f32[64,4096]{1,0:T(8,128)}) custom-call(f32[64,128]{1,0:T(8,128)S(1)} %add_add_fusion.one_ref, f32[64,128]{1,0:T(8,128)S(1)} %collective-permute-done.17.two_ref, bf16[128,4096]{1,0:T(8,128)(2,1)S(1)} %get-tuple-element.19.panel_ref, f32[64,4096]{1,0:T(8,128)} %trail_ref.1), custom_call_target="tpu_custom_call" | custom-call | tf_op jit(solution)/shard_map/finish/pallas_call | solution.py:254
  (19 shorter events, 0.9 us)
Async XLA Ops:
  0.6 6.7 %copy-start.1 = (s32[64]{0:T(128)S(1)}, s32[64]{0:T(128)}, u32[]{:S(2)}) copy-start(s32[64]{0:T(128)} %pivots_ref.1) | copy-start | bytes 772
  0.6 29.3 %copy-start = (f32[64,4096]{1,0:T(8,128)S(1)}, f32[64,4096]{1,0:T(8,128)}, u32[]{:S(2)}) copy-start(f32[64,4096]{1,0:T(8,128)} %trail_ref.1) | copy-start | bytes 3145732
  3.2 5.8 %collective-permute-start = (f32[32,1024]{1,0:T(8,128)S(1)}, f32[32,1024]{1,0:T(8,128)S(1)}, u32[]{:S(2)}, u32[]{:S(2)}) collective-permute-start(f32[32,1024]{1,0:T(8,128)S(1)} %get-tuple-element.13), channel_id=1, source_target_pairs={{0,3},{1,2},{2,1},{3,0},{4,7},{5,6},{6,5},{7,4},{8,11},{9,10},{10,... | collective-permute-start | bytes 393224 | tf_op jit(solution)/shard_map/ppermute | solution.py:211
  4.1 9.8 %collective-permute-start.1 = (f32[32,1024]{1,0:T(8,128)S(1)}, f32[32,1024]{1,0:T(8,128)S(1)}, u32[]{:S(2)}, u32[]{:S(2)}) collective-permute-start(f32[32,1024]{1,0:T(8,128)S(1)} %get-tuple-element.14), channel_id=1, source_target_pairs={{0,5},{1,4},{2,7},{3,6},{4,1},{5,0},{6,3},{7,2},{8,13},{9,12},{10,... | collective-permute-start | bytes 393224 | tf_op jit(solution)/shard_map/ppermute | solution.py:211
  7.1 9.7 %collective-permute-start.2 = (f32[32,1024]{1,0:T(8,128)S(1)}, f32[32,1024]{1,0:T(8,128)S(1)}, u32[]{:S(2)}, u32[]{:S(2)}) collective-permute-start(f32[32,1024]{1,0:T(8,128)S(1)} %get-tuple-element.15), channel_id=1, source_target_pairs={{0,7},{1,6},{2,5},{3,4},{4,3},{5,2},{6,1},{7,0},{8,15},{9,14},{10,... | collective-permute-start | bytes 393224 | tf_op jit(solution)/shard_map/ppermute | solution.py:211
  17.0 1.4 %collective-permute-start.3 = (f32[64,512]{1,0:T(8,128)S(1)}, f32[64,512]{1,0:T(8,128)S(1)}, u32[]{:S(2)}, u32[]{:S(2)}) collective-permute-start(f32[64,512]{1,0:T(8,128)S(1)} %get-tuple-element.17), channel_id=1, source_target_pairs={{0,1},{1,0},{2,3},{3,2},{4,5},{5,4},{6,7},{7,6},{8,9},{9,8},{10,11... | collective-permute-start | bytes 393224 | tf_op jit(solution)/shard_map/ppermute | solution.py:214
  18.5 9.6 %collective-permute-start.6 = (f32[64,512]{1,0:T(8,128)S(1)}, f32[64,512]{1,0:T(8,128)S(1)}, u32[]{:S(2)}, u32[]{:S(2)}) collective-permute-start(f32[64,512]{1,0:T(8,128)S(1)} %add.40.rest_0_), channel_id=1, source_target_pairs={{0,7},{1,6},{2,5},{3,4},{4,3},{5,2},{6,1},{7,0},{8,15},{9,14},{10,... | collective-permute-start | bytes 393224 | tf_op jit(solution)/shard_map/ppermute | solution.py:211
  18.9 9.3 %collective-permute-start.5 = (f32[64,512]{1,0:T(8,128)S(1)}, f32[64,512]{1,0:T(8,128)S(1)}, u32[]{:S(2)}, u32[]{:S(2)}) collective-permute-start(f32[64,512]{1,0:T(8,128)S(1)} %add.40.rest_0_), channel_id=1, source_target_pairs={{0,5},{1,4},{2,7},{3,6},{4,1},{5,0},{6,3},{7,2},{8,13},{9,12},{10,... | collective-permute-start | bytes 393224 | tf_op jit(solution)/shard_map/ppermute | solution.py:211
  19.5 9.1 %collective-permute-start.4 = (f32[64,512]{1,0:T(8,128)S(1)}, f32[64,512]{1,0:T(8,128)S(1)}, u32[]{:S(2)}, u32[]{:S(2)}) collective-permute-start(f32[64,512]{1,0:T(8,128)S(1)} %add.40.rest_0_), channel_id=1, source_target_pairs={{0,3},{1,2},{2,1},{3,0},{4,7},{5,6},{6,5},{7,4},{8,11},{9,10},{10,... | collective-permute-start | bytes 393224 | tf_op jit(solution)/shard_map/ppermute | solution.py:211
  22.2 6.7 %collective-permute-start.7 = (f32[64,512]{1,0:T(8,128)S(1)}, f32[64,512]{1,0:T(8,128)S(1)}, u32[]{:S(2)}, u32[]{:S(2)}) collective-permute-start(f32[64,512]{1,0:T(8,128)S(1)} %add.40.rest_0_), channel_id=1, source_target_pairs={{0,1},{1,0},{2,3},{3,2},{4,5},{5,4},{6,7},{7,6},{8,9},{9,8},{10,11... | collective-permute-start | bytes 393224 | tf_op jit(solution)/shard_map/ppermute | solution.py:214
  28.1 1.3 %collective-permute-start.10 = (f32[64,512]{1,0:T(8,128)S(1)}, f32[64,512]{1,0:T(8,128)S(1)}, u32[]{:S(2)}, u32[]{:S(2)}) collective-permute-start(f32[64,512]{1,0:T(8,128)S(1)} %collective-permute-done.6.rest_3_), channel_id=1, source_target_pairs={{0,1},{1,0},{2,3},{3,2},{4,5},{5,4},{6,7},{7,6},{8,9},{9,8},{10,11... | collective-permute-start | bytes 393224 | tf_op jit(solution)/shard_map/ppermute | solution.py:214
  28.2 1.4 %collective-permute-start.9 = (f32[64,512]{1,0:T(8,128)S(1)}, f32[64,512]{1,0:T(8,128)S(1)}, u32[]{:S(2)}, u32[]{:S(2)}) collective-permute-start(f32[64,512]{1,0:T(8,128)S(1)} %collective-permute-done.5.rest_2_), channel_id=1, source_target_pairs={{0,1},{1,0},{2,3},{3,2},{4,5},{5,4},{6,7},{7,6},{8,9},{9,8},{10,11... | collective-permute-start | bytes 393224 | tf_op jit(solution)/shard_map/ppermute | solution.py:214
  28.6 1.3 %collective-permute-start.8 = (f32[64,512]{1,0:T(8,128)S(1)}, f32[64,512]{1,0:T(8,128)S(1)}, u32[]{:S(2)}, u32[]{:S(2)}) collective-permute-start(f32[64,512]{1,0:T(8,128)S(1)} %collective-permute-done.4.rest_1_), channel_id=1, source_target_pairs={{0,1},{1,0},{2,3},{3,2},{4,5},{5,4},{6,7},{7,6},{8,9},{9,8},{10,11... | collective-permute-start | bytes 393224 | tf_op jit(solution)/shard_map/ppermute | solution.py:214
  30.9 5.2 %collective-permute-start.13 = (f32[64,128]{1,0:T(8,128)S(1)}, f32[64,128]{1,0:T(8,128)S(1)}, u32[]{:S(2)}, u32[]{:S(2)}) collective-permute-start(f32[64,128]{1,0:T(8,128)S(1)} %get-tuple-element.18), channel_id=1, source_target_pairs={{0,24},{8,16},{16,8},{24,0},{32,56},{40,48},{48,40},{56,32},{64,88... | collective-permute-start | bytes 98312 | tf_op jit(solution)/shard_map/ppermute | solution.py:217
  34.0 5.4 %collective-permute-start.12 = (f32[64,128]{1,0:T(8,128)S(1)}, f32[64,128]{1,0:T(8,128)S(1)}, u32[]{:S(2)}, u32[]{:S(2)}) collective-permute-start(f32[64,128]{1,0:T(8,128)S(1)} %get-tuple-element.18), channel_id=1, source_target_pairs={{0,16},{8,24},{16,0},{24,8},{32,48},{40,56},{48,32},{56,40},{64,80... | collective-permute-start | bytes 98312 | tf_op jit(solution)/shard_map/ppermute | solution.py:217
  34.7 4.8 %collective-permute-start.11 = (f32[64,128]{1,0:T(8,128)S(1)}, f32[64,128]{1,0:T(8,128)S(1)}, u32[]{:S(2)}, u32[]{:S(2)}) collective-permute-start(f32[64,128]{1,0:T(8,128)S(1)} %get-tuple-element.18), channel_id=1, source_target_pairs={{0,8},{8,0},{16,24},{24,16},{32,40},{40,32},{48,56},{56,48},{64,72... | collective-permute-start | bytes 98312 | tf_op jit(solution)/shard_map/ppermute | solution.py:217
  39.5 4.8 %collective-permute-start.16 = (f32[64,128]{1,0:T(8,128)S(1)}, f32[64,128]{1,0:T(8,128)S(1)}, u32[]{:S(2)}, u32[]{:S(2)}) collective-permute-start(f32[64,128]{1,0:T(8,128)S(1)} %add_add_fusion.1), channel_id=1, source_target_pairs={{0,96},{8,104},{16,112},{24,120},{32,64},{40,72},{48,80},{56,88},{... | collective-permute-start | bytes 98312 | tf_op jit(solution)/shard_map/ppermute | solution.py:217
  41.5 5.0 %collective-permute-start.15 = (f32[64,128]{1,0:T(8,128)S(1)}, f32[64,128]{1,0:T(8,128)S(1)}, u32[]{:S(2)}, u32[]{:S(2)}) collective-permute-start(f32[64,128]{1,0:T(8,128)S(1)} %add_add_fusion.1), channel_id=1, source_target_pairs={{0,64},{8,72},{16,80},{24,88},{32,96},{40,104},{48,112},{56,120},{... | collective-permute-start | bytes 98312 | tf_op jit(solution)/shard_map/ppermute | solution.py:217
  42.9 4.0 %collective-permute-start.14 = (f32[64,128]{1,0:T(8,128)S(1)}, f32[64,128]{1,0:T(8,128)S(1)}, u32[]{:S(2)}, u32[]{:S(2)}) collective-permute-start(f32[64,128]{1,0:T(8,128)S(1)} %add_add_fusion.1), channel_id=1, source_target_pairs={{0,32},{8,40},{16,48},{24,56},{32,0},{40,8},{48,16},{56,24},{64,96... | collective-permute-start | bytes 98312 | tf_op jit(solution)/shard_map/ppermute | solution.py:217
  46.9 7.8 %collective-permute-start.17 = (f32[64,128]{1,0:T(8,128)S(1)}, f32[64,128]{1,0:T(8,128)S(1)}, u32[]{:S(2)}, u32[]{:S(2)}) collective-permute-start(f32[64,128]{1,0:T(8,128)S(1)} %add_add_fusion.one_ref), channel_id=1, source_target_pairs={{0,224},{8,232},{16,240},{24,248},{32,192},{40,200},{48,208},{56,2... | collective-permute-start | bytes 98312 | tf_op jit(solution)/shard_map/ppermute | solution.py:217

commit v5 on v4

--- a/solution.py
+++ b/solution.py
@@ -203,12 +203,11 @@
     earlier = (owners[:, None] == owners[None, :]) & (order[None, :] < order[:, None])
     slots = jnp.sum(earlier.astype(jnp.int32), axis=1)
     away = (owners // CORES) ^ (my_col // CORES)
-    held = (owners % CORES == my_col % CORES) == (away == 0)
-    keys = jnp.where(held, away * capacity + slots, -1)[:, None]
+    keys = jnp.where(owners % CORES == my_col % CORES, away * capacity + slots, -1)[:, None]
     f32 = jnp.float32
 
-    def to_x(array, k):
-        return lax.ppermute(array, "col", [(i, i ^ (CORES * k + 1)) for i in range(col_count)])
+    def to_x(array, k, cross):
+        return lax.ppermute(array, "col", [(i, i ^ (CORES * k + cross)) for i in range(col_count)])
 
     def to_core(array):
         return lax.ppermute(array, "col", [(i, i ^ 1) for i in range(col_count)])
@@ -228,7 +227,7 @@
         scratch_shapes=[VMEM((capacity, width), f32), pltpu.SemaphoreType.DMA((capacity,))],
         name="select",
     )(pivots, candidates)
-    arrived = [quarters[0]] + [to_x(quarters[k], k) for k in range(1, x_count)]
+    arrived = [quarters[0]] + [to_x(quarters[k], k, 0) for k in range(1, x_count)]
     keep, send = pl.pallas_call(
         functools.partial(merge_kernel, x_count),
         out_shape=[VMEM((count, piece), f32)] * 2,
@@ -237,7 +236,7 @@
         name="merge",
     )(near(keys), *map(near, arrived))
     own_piece = keep + to_core(send)
-    mine = [own_piece] + [to_x(own_piece, k) for k in range(1, x_count)]
+    mine = [own_piece] + [to_x(own_piece, k, 1) for k in range(1, x_count)]
     other = [to_core(array) for array in mine]
     sums, panel = pl.pallas_call(
         functools.partial(gram_kernel, x_count),
@@ -246,9 +245,9 @@
         out_specs=[in_vmem] * 2,
         name="gram",
     )(*map(near, mine), *map(near, other), near(trailing))
-    for step in (1, 4):
-        sums = (sums + to_row(sums, step)) + (to_row(sums, 2 * step) + to_row(sums, 3 * step))
-    far = to_row(sums, 28)
+    for one, two in ((1, 3), (4, 28)):
+        sums = (sums + to_row(sums, one)) + (to_row(sums, two) + to_row(sums, one ^ two))
+    far = to_row(sums, 8)
     anywhere = pl.BlockSpec(memory_space=pl.ANY)
     large = (count, width)
     return pl.pallas_call(

time: 60.7 us -> 61.3 us (level)
  waiting for transfers between devices: 25.8 us -> 29.8 us
  starting transfers between devices: 24 us -> 20.6 us
    ppermute x7, waiting for transfers between devices: 8.82 us -> 14.8 us  [to_row(): return lax.ppermute(array, 'row', [(i, i ^ k) for i in range(row_count)])]
    ppermute x7, starting transfers between devices: 14.9 us -> 10.9 us  [to_row(): return lax.ppermute(array, 'row', [(i, i ^ k) for i in range(row_count)])]
    ppermute x6, waiting for transfers between devices: 14.7 us -> 12.7 us  [to_x(): lax.ppermute(array, 'col', [(i, i ^ CORES * k + cross) for i in range(col...]
    ppermute x6, starting transfers between devices: 7.8 us -> 8.45 us  [to_x(): lax.ppermute(array, 'col', [(i, i ^ CORES * k + cross) for i in range(col...]
where the time goes in v5:
time: 61.3 us; the launch traced here: 61.1 us
  waiting for transfers between devices  29.8 us (49%)
  starting transfers between devices  20.6 us (34%)
  Pallas kernels  9.54 us (16%)
  between operations  0.75 us (1%)
    ppermute x7, waiting for transfers between devices, to_row(): return lax.ppermute(array, 'row', [(i, i ^ k) for i in range(row_count)])  14.8 us
    ppermute x6, waiting for transfers between devices, to_x(): lax.ppermute(array, 'col', [(i, i ^ CORES * k + cross) for i in range(col...  12.7 us
    ppermute x7, starting transfers between devices, to_row(): return lax.ppermute(array, 'row', [(i, i ^ k) for i in range(row_count)])  10.9 us
    ppermute x6, starting transfers between devices, to_x(): lax.ppermute(array, 'col', [(i, i ^ CORES * k + cross) for i in range(col...  8.45 us
    pallas_call x1, Pallas kernels, on_device(): pl.pallas_call(functools.partial(finish_kernel, root), out_shape=[jax.Sha...  5.72 us
    pallas_call x1, Pallas kernels, on_device(): pl.pallas_call(functools.partial(select_kernel, x_count), out_shape=[VMEM...  2.62 us
    ppermute x5, waiting for transfers between devices, to_core(): return lax.ppermute(array, 'col', [(i, i ^ 1) for i in range(col_count)])  2.39 us
    ppermute x5, starting transfers between devices, to_core(): return lax.ppermute(array, 'col', [(i, i ^ 1) for i in range(col_count)])  1.24 us
  transfers between devices with their start and end apart: 18, of which 13 were waited for; matrix products, arithmetic and copies ran while one was open for 0% of the time, Pallas kernels for 0%

profile of v5, /device:TPU:32, one launch (start us, length us, event | category | flops | bytes accessed | tf_op | source)
XLA Modules:
  0.0 61.1 jit_solution(16203341458890942524)
XLA Ops:
  0.7 2.6 %select.17 = (f32[32,1024]{1,0:T(8,128)S(1)}, f32[32,1024]{1,0:T(8,128)S(1)}, f32[32,1024]{1,0:T(8,128)S(1)}, f32[32,1024]{1,0:T(8,128)S(1)}) custom-call(s32[64]{0:T(128)} %pivots_ref.1, f32[128,4096]{1,0:T(8,128)} %cand_ref.1), custom_call_target="tpu_custom_call" | custom-call | tf_op jit(solution)/shard_map/select/pallas_call | solution.py:222
  3.3 1.5 %collective-permute-start = (f32[32,1024]{1,0:T(8,128)S(1)}, f32[32,1024]{1,0:T(8,128)S(1)}, u32[]{:S(2)}, u32[]{:S(2)}) collective-permute-start(f32[32,1024]{1,0:T(8,128)S(1)} %get-tuple-element.13), channel_id=1, source_target_pairs={{0,2},{1,3},{2,0},{3,1},{4,6},{5,7},{6,4},{7,5},{8,10},{9,11},{10,... | collective-permute-start | bytes 393224 | tf_op jit(solution)/shard_map/ppermute | solution.py:210
  4.8 2.7 %collective-permute-start.1 = (f32[32,1024]{1,0:T(8,128)S(1)}, f32[32,1024]{1,0:T(8,128)S(1)}, u32[]{:S(2)}, u32[]{:S(2)}) collective-permute-start(f32[32,1024]{1,0:T(8,128)S(1)} %get-tuple-element.14), channel_id=1, source_target_pairs={{0,4},{1,5},{2,6},{3,7},{4,0},{5,1},{6,2},{7,3},{8,12},{9,13},{10,... | collective-permute-start | bytes 393224 | tf_op jit(solution)/shard_map/ppermute | solution.py:210
  7.5 0.5 collective-permute-start.2
  8.1 0.2 convert_reduce_fusion
  8.4 0.8 %collective-permute-done.rest_1_ = f32[32,1024]{1,0:T(8,128)S(1)} collective-permute-done((f32[32,1024]{1,0:T(8,128)S(1)}, f32[32,1024]{1,0:T(8,128)S(1)}, u32[]{:S(2)}, u32[]{:S(2)}) %collective-permute-start) | collective-permute-done | bytes 131104 | tf_op jit(solution)/shard_map/ppermute | solution.py:210
  9.2 4.3 %collective-permute-done.1.rest_2_ = f32[32,1024]{1,0:T(8,128)S(1)} collective-permute-done((f32[32,1024]{1,0:T(8,128)S(1)}, f32[32,1024]{1,0:T(8,128)S(1)}, u32[]{:S(2)}, u32[]{:S(2)}) %collective-permute-start.1) | collective-permute-done | bytes 131104 | tf_op jit(solution)/shard_map/ppermute | solution.py:210
  13.5 2.0 %collective-permute-done.2.rest_3_ = f32[32,1024]{1,0:T(8,128)S(1)} collective-permute-done((f32[32,1024]{1,0:T(8,128)S(1)}, f32[32,1024]{1,0:T(8,128)S(1)}, u32[]{:S(2)}, u32[]{:S(2)}) %collective-permute-start.2) | collective-permute-done | bytes 131104 | tf_op jit(solution)/shard_map/ppermute | solution.py:210
  15.5 0.2 merge.1
  15.8 1.3 %collective-permute-done.3 = f32[64,512]{1,0:T(8,128)S(1)} collective-permute-done((f32[64,512]{1,0:T(8,128)S(1)}, f32[64,512]{1,0:T(8,128)S(1)}, u32[]{:S(2)}, u32[]{:S(2)}) %collective-permute-start.3) | collective-permute-done | bytes 131104 | tf_op jit(solution)/shard_map/ppermute | solution.py:213
  17.2 0.8 %collective-permute-start.6 = (f32[64,512]{1,0:T(8,128)S(1)}, f32[64,512]{1,0:T(8,128)S(1)}, u32[]{:S(2)}, u32[]{:S(2)}) collective-permute-start(f32[64,512]{1,0:T(8,128)S(1)} %add.40.rest_0_), channel_id=1, source_target_pairs={{0,7},{1,6},{2,5},{3,4},{4,3},{5,2},{6,1},{7,0},{8,15},{9,14},{10,... | collective-permute-start | bytes 393224 | tf_op jit(solution)/shard_map/ppermute | solution.py:210
  18.0 0.9 %collective-permute-start.5 = (f32[64,512]{1,0:T(8,128)S(1)}, f32[64,512]{1,0:T(8,128)S(1)}, u32[]{:S(2)}, u32[]{:S(2)}) collective-permute-start(f32[64,512]{1,0:T(8,128)S(1)} %add.40.rest_0_), channel_id=1, source_target_pairs={{0,5},{1,4},{2,7},{3,6},{4,1},{5,0},{6,3},{7,2},{8,13},{9,12},{10,... | collective-permute-start | bytes 393224 | tf_op jit(solution)/shard_map/ppermute | solution.py:210
  18.9 2.0 %collective-permute-start.4 = (f32[64,512]{1,0:T(8,128)S(1)}, f32[64,512]{1,0:T(8,128)S(1)}, u32[]{:S(2)}, u32[]{:S(2)}) collective-permute-start(f32[64,512]{1,0:T(8,128)S(1)} %add.40.rest_0_), channel_id=1, source_target_pairs={{0,3},{1,2},{2,1},{3,0},{4,7},{5,6},{6,5},{7,4},{8,11},{9,10},{10,... | collective-permute-start | bytes 393224 | tf_op jit(solution)/shard_map/ppermute | solution.py:210
  20.9 0.3 collective-permute-start.7
  21.2 5.6 %collective-permute-done.6.rest_3_ = f32[64,512]{1,0:T(8,128)S(1)} collective-permute-done((f32[64,512]{1,0:T(8,128)S(1)}, f32[64,512]{1,0:T(8,128)S(1)}, u32[]{:S(2)}, u32[]{:S(2)}) %collective-permute-start.6) | collective-permute-done | bytes 131104 | tf_op jit(solution)/shard_map/ppermute | solution.py:210
  26.9 0.4 collective-permute-start.9
  27.3 0.3 collective-permute-start.8
  27.6 0.5 collective-permute-done.10.rest_7_
  28.1 0.2 collective-permute-done.9.rest_6_
  28.3 0.3 collective-permute-done.8.rest_5_
  28.6 1.0 %gram.1 = (f32[64,128]{1,0:T(8,128)S(1)}, bf16[128,4096]{1,0:T(8,128)(2,1)S(1)}) custom-call(f32[64,512]{1,0:T(8,128)S(1)} %add.40.rest_0_, f32[64,512]{1,0:T(8,128)S(1)} %collective-permute-done.4.rest_1_, f32[64,512]{1,0:T(8,128)S(1)} %collective-permute-done.5.rest_2_, f32[64,512]{1,0:T(8,128)S(1)} %collective-permute-done.6.rest_3_, ...), custom_call_target="tpu_custom_call" | custom-call | tf_op jit(solution)/shard_map/gram/pallas_call | solution.py:241
  29.6 3.3 %collective-permute-start.13 = (f32[64,128]{1,0:T(8,128)S(1)}, f32[64,128]{1,0:T(8,128)S(1)}, u32[]{:S(2)}, u32[]{:S(2)}) collective-permute-start(f32[64,128]{1,0:T(8,128)S(1)} %get-tuple-element.18), channel_id=1, source_target_pairs={{0,16},{8,24},{16,0},{24,8},{32,48},{40,56},{48,32},{56,40},{64,80... | collective-permute-start | bytes 98312 | tf_op jit(solution)/shard_map/ppermute | solution.py:216
  32.9 1.1 %collective-permute-start.12 = (f32[64,128]{1,0:T(8,128)S(1)}, f32[64,128]{1,0:T(8,128)S(1)}, u32[]{:S(2)}, u32[]{:S(2)}) collective-permute-start(f32[64,128]{1,0:T(8,128)S(1)} %get-tuple-element.18), channel_id=1, source_target_pairs={{0,24},{8,16},{16,8},{24,0},{32,56},{40,48},{48,40},{56,32},{64,88... | collective-permute-start | bytes 98312 | tf_op jit(solution)/shard_map/ppermute | solution.py:216
  34.0 1.2 %collective-permute-done.13 = f32[64,128]{1,0:T(8,128)S(1)} collective-permute-done((f32[64,128]{1,0:T(8,128)S(1)}, f32[64,128]{1,0:T(8,128)S(1)}, u32[]{:S(2)}, u32[]{:S(2)}) %collective-permute-start.13) | collective-permute-done | bytes 32800 | tf_op jit(solution)/shard_map/ppermute | solution.py:216
  35.1 2.9 %collective-permute-done.12 = f32[64,128]{1,0:T(8,128)S(1)} collective-permute-done((f32[64,128]{1,0:T(8,128)S(1)}, f32[64,128]{1,0:T(8,128)S(1)}, u32[]{:S(2)}, u32[]{:S(2)}) %collective-permute-start.12) | collective-permute-done | bytes 32800 | tf_op jit(solution)/shard_map/ppermute | solution.py:216
  38.0 5.5 %collective-permute-start.16 = (f32[64,128]{1,0:T(8,128)S(1)}, f32[64,128]{1,0:T(8,128)S(1)}, u32[]{:S(2)}, u32[]{:S(2)}) collective-permute-start(f32[64,128]{1,0:T(8,128)S(1)} %add_add_fusion.1), channel_id=1, source_target_pairs={{0,192},{8,200},{16,208},{24,216},{32,224},{40,232},{48,240},{56,2... | collective-permute-start | bytes 98312 | tf_op jit(solution)/shard_map/ppermute | solution.py:216
  43.5 0.5 collective-permute-start.15
  44.1 0.5 collective-permute-start.14
  44.5 0.9 %collective-permute-done.16 = f32[64,128]{1,0:T(8,128)S(1)} collective-permute-done((f32[64,128]{1,0:T(8,128)S(1)}, f32[64,128]{1,0:T(8,128)S(1)}, u32[]{:S(2)}, u32[]{:S(2)}) %collective-permute-start.16) | collective-permute-done | bytes 32800 | tf_op jit(solution)/shard_map/ppermute | solution.py:216
  45.4 5.0 %collective-permute-done.15 = f32[64,128]{1,0:T(8,128)S(1)} collective-permute-done((f32[64,128]{1,0:T(8,128)S(1)}, f32[64,128]{1,0:T(8,128)S(1)}, u32[]{:S(2)}, u32[]{:S(2)}) %collective-permute-start.15) | collective-permute-done | bytes 32800 | tf_op jit(solution)/shard_map/ppermute | solution.py:216
  50.6 4.8 %collective-permute-done.17.two_ref = f32[64,128]{1,0:T(8,128)S(1)} collective-permute-done((f32[64,128]{1,0:T(8,128)S(1)}, f32[64,128]{1,0:T(8,128)S(1)}, u32[]{:S(2)}, u32[]{:S(2)}) %collective-permute-start.17) | collective-permute-done | bytes 32800 | tf_op jit(solution)/shard_map/ppermute | solution.py:216
  55.4 5.7 %finish.1 = (f32[64,64]{1,0:T(8,128)}, f32[64,64]{1,0:T(8,128)}, f32[64,4096]{1,0:T(8,128)}, f32[64,4096]{1,0:T(8,128)}) custom-call(f32[64,128]{1,0:T(8,128)S(1)} %add_add_fusion.one_ref, f32[64,128]{1,0:T(8,128)S(1)} %collective-permute-done.17.two_ref, bf16[128,4096]{1,0:T(8,128)(2,1)S(1)} %get-tuple-element.19.panel_ref, f32[64,4096]{1,0:T(8,128)} %trail_ref.1), custom_call_target="tpu_custom_call" | custom-call | tf_op jit(solution)/shard_map/finish/pallas_call | solution.py:253
  (19 shorter events, 0.5 us)
Async XLA Ops:
  0.6 7.4 %copy-start.1 = (s32[64]{0:T(128)S(1)}, s32[64]{0:T(128)}, u32[]{:S(2)}) copy-start(s32[64]{0:T(128)} %pivots_ref.1) | copy-start | bytes 772
  0.6 28.0 %copy-start = (f32[64,4096]{1,0:T(8,128)S(1)}, f32[64,4096]{1,0:T(8,128)}, u32[]{:S(2)}) copy-start(f32[64,4096]{1,0:T(8,128)} %trail_ref.1) | copy-start | bytes 3145732
  3.3 5.9 %collective-permute-start = (f32[32,1024]{1,0:T(8,128)S(1)}, f32[32,1024]{1,0:T(8,128)S(1)}, u32[]{:S(2)}, u32[]{:S(2)}) collective-permute-start(f32[32,1024]{1,0:T(8,128)S(1)} %get-tuple-element.13), channel_id=1, source_target_pairs={{0,2},{1,3},{2,0},{3,1},{4,6},{5,7},{6,4},{7,5},{8,10},{9,11},{10,... | collective-permute-start | bytes 393224 | tf_op jit(solution)/shard_map/ppermute | solution.py:210
  4.8 8.7 %collective-permute-start.1 = (f32[32,1024]{1,0:T(8,128)S(1)}, f32[32,1024]{1,0:T(8,128)S(1)}, u32[]{:S(2)}, u32[]{:S(2)}) collective-permute-start(f32[32,1024]{1,0:T(8,128)S(1)} %get-tuple-element.14), channel_id=1, source_target_pairs={{0,4},{1,5},{2,6},{3,7},{4,0},{5,1},{6,2},{7,3},{8,12},{9,13},{10,... | collective-permute-start | bytes 393224 | tf_op jit(solution)/shard_map/ppermute | solution.py:210
  7.5 8.0 %collective-permute-start.2 = (f32[32,1024]{1,0:T(8,128)S(1)}, f32[32,1024]{1,0:T(8,128)S(1)}, u32[]{:S(2)}, u32[]{:S(2)}) collective-permute-start(f32[32,1024]{1,0:T(8,128)S(1)} %get-tuple-element.15), channel_id=1, source_target_pairs={{0,6},{1,7},{2,4},{3,5},{4,2},{5,3},{6,0},{7,1},{8,14},{9,15},{10,... | collective-permute-start | bytes 393224 | tf_op jit(solution)/shard_map/ppermute | solution.py:210
  15.7 1.4 %collective-permute-start.3 = (f32[64,512]{1,0:T(8,128)S(1)}, f32[64,512]{1,0:T(8,128)S(1)}, u32[]{:S(2)}, u32[]{:S(2)}) collective-permute-start(f32[64,512]{1,0:T(8,128)S(1)} %get-tuple-element.17), channel_id=1, source_target_pairs={{0,1},{1,0},{2,3},{3,2},{4,5},{5,4},{6,7},{7,6},{8,9},{9,8},{10,11... | collective-permute-start | bytes 393224 | tf_op jit(solution)/shard_map/ppermute | solution.py:213
  17.2 9.6 %collective-permute-start.6 = (f32[64,512]{1,0:T(8,128)S(1)}, f32[64,512]{1,0:T(8,128)S(1)}, u32[]{:S(2)}, u32[]{:S(2)}) collective-permute-start(f32[64,512]{1,0:T(8,128)S(1)} %add.40.rest_0_), channel_id=1, source_target_pairs={{0,7},{1,6},{2,5},{3,4},{4,3},{5,2},{6,1},{7,0},{8,15},{9,14},{10,... | collective-permute-start | bytes 393224 | tf_op jit(solution)/shard_map/ppermute | solution.py:210
  18.0 8.9 %collective-permute-start.5 = (f32[64,512]{1,0:T(8,128)S(1)}, f32[64,512]{1,0:T(8,128)S(1)}, u32[]{:S(2)}, u32[]{:S(2)}) collective-permute-start(f32[64,512]{1,0:T(8,128)S(1)} %add.40.rest_0_), channel_id=1, source_target_pairs={{0,5},{1,4},{2,7},{3,6},{4,1},{5,0},{6,3},{7,2},{8,13},{9,12},{10,... | collective-permute-start | bytes 393224 | tf_op jit(solution)/shard_map/ppermute | solution.py:210
  18.9 8.4 %collective-permute-start.4 = (f32[64,512]{1,0:T(8,128)S(1)}, f32[64,512]{1,0:T(8,128)S(1)}, u32[]{:S(2)}, u32[]{:S(2)}) collective-permute-start(f32[64,512]{1,0:T(8,128)S(1)} %add.40.rest_0_), channel_id=1, source_target_pairs={{0,3},{1,2},{2,1},{3,0},{4,7},{5,6},{6,5},{7,4},{8,11},{9,10},{10,... | collective-permute-start | bytes 393224 | tf_op jit(solution)/shard_map/ppermute | solution.py:210
  20.9 6.7 %collective-permute-start.7 = (f32[64,512]{1,0:T(8,128)S(1)}, f32[64,512]{1,0:T(8,128)S(1)}, u32[]{:S(2)}, u32[]{:S(2)}) collective-permute-start(f32[64,512]{1,0:T(8,128)S(1)} %add.40.rest_0_), channel_id=1, source_target_pairs={{0,1},{1,0},{2,3},{3,2},{4,5},{5,4},{6,7},{7,6},{8,9},{9,8},{10,11... | collective-permute-start | bytes 393224 | tf_op jit(solution)/shard_map/ppermute | solution.py:213
  26.8 1.3 %collective-permute-start.10 = (f32[64,512]{1,0:T(8,128)S(1)}, f32[64,512]{1,0:T(8,128)S(1)}, u32[]{:S(2)}, u32[]{:S(2)}) collective-permute-start(f32[64,512]{1,0:T(8,128)S(1)} %collective-permute-done.6.rest_3_), channel_id=1, source_target_pairs={{0,1},{1,0},{2,3},{3,2},{4,5},{5,4},{6,7},{7,6},{8,9},{9,8},{10,11... | collective-permute-start | bytes 393224 | tf_op jit(solution)/shard_map/ppermute | solution.py:213
  26.9 1.4 %collective-permute-start.9 = (f32[64,512]{1,0:T(8,128)S(1)}, f32[64,512]{1,0:T(8,128)S(1)}, u32[]{:S(2)}, u32[]{:S(2)}) collective-permute-start(f32[64,512]{1,0:T(8,128)S(1)} %collective-permute-done.5.rest_2_), channel_id=1, source_target_pairs={{0,1},{1,0},{2,3},{3,2},{4,5},{5,4},{6,7},{7,6},{8,9},{9,8},{10,11... | collective-permute-start | bytes 393224 | tf_op jit(solution)/shard_map/ppermute | solution.py:213
  27.3 1.3 %collective-permute-start.8 = (f32[64,512]{1,0:T(8,128)S(1)}, f32[64,512]{1,0:T(8,128)S(1)}, u32[]{:S(2)}, u32[]{:S(2)}) collective-permute-start(f32[64,512]{1,0:T(8,128)S(1)} %collective-permute-done.4.rest_1_), channel_id=1, source_target_pairs={{0,1},{1,0},{2,3},{3,2},{4,5},{5,4},{6,7},{7,6},{8,9},{9,8},{10,11... | collective-permute-start | bytes 393224 | tf_op jit(solution)/shard_map/ppermute | solution.py:213
  29.6 5.5 %collective-permute-start.13 = (f32[64,128]{1,0:T(8,128)S(1)}, f32[64,128]{1,0:T(8,128)S(1)}, u32[]{:S(2)}, u32[]{:S(2)}) collective-permute-start(f32[64,128]{1,0:T(8,128)S(1)} %get-tuple-element.18), channel_id=1, source_target_pairs={{0,16},{8,24},{16,0},{24,8},{32,48},{40,56},{48,32},{56,40},{64,80... | collective-permute-start | bytes 98312 | tf_op jit(solution)/shard_map/ppermute | solution.py:216
  32.9 5.1 %collective-permute-start.12 = (f32[64,128]{1,0:T(8,128)S(1)}, f32[64,128]{1,0:T(8,128)S(1)}, u32[]{:S(2)}, u32[]{:S(2)}) collective-permute-start(f32[64,128]{1,0:T(8,128)S(1)} %get-tuple-element.18), channel_id=1, source_target_pairs={{0,24},{8,16},{16,8},{24,0},{32,56},{40,48},{48,40},{56,32},{64,88... | collective-permute-start | bytes 98312 | tf_op jit(solution)/shard_map/ppermute | solution.py:216
  34.0 4.1 %collective-permute-start.11 = (f32[64,128]{1,0:T(8,128)S(1)}, f32[64,128]{1,0:T(8,128)S(1)}, u32[]{:S(2)}, u32[]{:S(2)}) collective-permute-start(f32[64,128]{1,0:T(8,128)S(1)} %get-tuple-element.18), channel_id=1, source_target_pairs={{0,8},{8,0},{16,24},{24,16},{32,40},{40,32},{48,56},{56,48},{64,72... | collective-permute-start | bytes 98312 | tf_op jit(solution)/shard_map/ppermute | solution.py:216
  38.0 7.4 %collective-permute-start.16 = (f32[64,128]{1,0:T(8,128)S(1)}, f32[64,128]{1,0:T(8,128)S(1)}, u32[]{:S(2)}, u32[]{:S(2)}) collective-permute-start(f32[64,128]{1,0:T(8,128)S(1)} %add_add_fusion.1), channel_id=1, source_target_pairs={{0,192},{8,200},{16,208},{24,216},{32,224},{40,232},{48,240},{56,2... | collective-permute-start | bytes 98312 | tf_op jit(solution)/shard_map/ppermute | solution.py:216
  43.5 6.9 %collective-permute-start.15 = (f32[64,128]{1,0:T(8,128)S(1)}, f32[64,128]{1,0:T(8,128)S(1)}, u32[]{:S(2)}, u32[]{:S(2)}) collective-permute-start(f32[64,128]{1,0:T(8,128)S(1)} %add_add_fusion.1), channel_id=1, source_target_pairs={{0,224},{8,232},{16,240},{24,248},{32,192},{40,200},{48,208},{56,2... | collective-permute-start | bytes 98312 | tf_op jit(solution)/shard_map/ppermute | solution.py:216
  44.1 6.4 %collective-permute-start.14 = (f32[64,128]{1,0:T(8,128)S(1)}, f32[64,128]{1,0:T(8,128)S(1)}, u32[]{:S(2)}, u32[]{:S(2)}) collective-permute-start(f32[64,128]{1,0:T(8,128)S(1)} %add_add_fusion.1), channel_id=1, source_target_pairs={{0,32},{8,40},{16,48},{24,56},{32,0},{40,8},{48,16},{56,24},{64,96... | collective-permute-start | bytes 98312 | tf_op jit(solution)/shard_map/ppermute | solution.py:216
  50.5 4.9 %collective-permute-start.17 = (f32[64,128]{1,0:T(8,128)S(1)}, f32[64,128]{1,0:T(8,128)S(1)}, u32[]{:S(2)}, u32[]{:S(2)}) collective-permute-start(f32[64,128]{1,0:T(8,128)S(1)} %add_add_fusion.one_ref), channel_id=1, source_target_pairs={{0,64},{8,72},{16,80},{24,88},{32,96},{40,104},{48,112},{56,120},{... | collective-permute-start | bytes 98312 | tf_op jit(solution)/shard_map/ppermute | solution.py:216

commit v6 on v5

--- a/solution.py
+++ b/solution.py
@@ -24,16 +24,17 @@
     cand_count, width = cand_ref.shape
     count = pivots_ref.shape[0]
     me = lax.axis_index("col")
+    first = me * cand_count
     rows[...] = jnp.zeros_like(rows)
 
     def row_copy(pivot, slot):
         return pltpu.make_async_copy(
-            cand_ref.at[pl.ds(pivot - me * cand_count, 1), :], rows.at[pl.ds(slot, 1), :], sems.at[slot]
+            cand_ref.at[pl.ds(pivot - first, 1), :], rows.at[pl.ds(slot, 1), :], sems.at[slot]
         )
 
     def fetch(i, slot):
         pivot = pivots_ref[i]
-        mine = pivot // cand_count == me
+        mine = (pivot >= first) & (pivot < first + cand_count)
 
         @pl.when(mine)
         def _():
@@ -44,7 +45,7 @@
     total = lax.fori_loop(0, count, fetch, jnp.int32(0), unroll=8)
 
     def drain(slot, carry):
-        row_copy(me * cand_count, slot).wait()
+        row_copy(first, slot).wait()
         return carry
 
     lax.fori_loop(0, total, drain, 0)
@@ -77,7 +78,7 @@
     me = lax.axis_index("col")
     my_x, my_core = me // CORES, me % CORES
     for k in range(x_count):
-        near_core = my_core if k == 0 else 1 - my_core
+        near_core = my_core
         for core, ref in ((near_core, mine[k]), (1 - near_core, other[k])):
             begin = pl.multiple_of(((my_x ^ k) * CORES + core) * piece, piece)
             high, low = split_bf16(ref[...])
@@ -236,7 +237,7 @@
         name="merge",
     )(near(keys), *map(near, arrived))
     own_piece = keep + to_core(send)
-    mine = [own_piece] + [to_x(own_piece, k, 1) for k in range(1, x_count)]
+    mine = [own_piece] + [to_x(own_piece, k, 0) for k in range(1, x_count)]
     other = [to_core(array) for array in mine]
     sums, panel = pl.pallas_call(
         functools.partial(gram_kernel, x_count),
@@ -245,9 +246,12 @@
         out_specs=[in_vmem] * 2,
         name="gram",
     )(*map(near, mine), *map(near, other), near(trailing))
-    for one, two in ((1, 3), (4, 28)):
-        sums = (sums + to_row(sums, one)) + (to_row(sums, two) + to_row(sums, one ^ two))
-    far = to_row(sums, 8)
+    for partners in ((1, 2, 3), (4, 8, 12)):
+        terms = [sums] + [to_row(sums, k) for k in partners]
+        while len(terms) > 1:
+            terms = [one + two for one, two in zip(terms[::2], terms[1::2])]
+        sums = terms[0]
+    far = to_row(sums, 28)
     anywhere = pl.BlockSpec(memory_space=pl.ANY)
     large = (count, width)
     return pl.pallas_call(

time: 61.3 us -> 59.4 us (0.969)
  waiting for transfers between devices: 29.8 us -> 24.1 us
  starting transfers between devices: 20.6 us -> 24.5 us
    ppermute x7, waiting for transfers between devices: 14.8 us -> 8.82 us  [to_row(): return lax.ppermute(array, 'row', [(i, i ^ k) for i in range(row_count)])]
    ppermute x7, starting transfers between devices: 10.9 us -> 14.9 us  [to_row(): return lax.ppermute(array, 'row', [(i, i ^ k) for i in range(row_count)])]
    ppermute x5, starting transfers between devices: 1.24 us -> 0.61 us  [to_core(): return lax.ppermute(array, 'col', [(i, i ^ 1) for i in range(col_count)])]
  transfers between devices with their start and end apart: 18 -> 18, of which waited for: 13 -> 14; matrix products, arithmetic and copies ran while one was open for 0% -> 1% of each run, Pallas kernels for 0% -> 0%
where the time goes in v6:
time: 59.4 us; the launch traced here: 58.9 us
  starting transfers between devices  24.5 us (41%)
  waiting for transfers between devices  24.1 us (41%)
  Pallas kernels  9.23 us (16%)
  between operations  0.74 us (1%)
    ppermute x7, starting transfers between devices, to_row(): return lax.ppermute(array, 'row', [(i, i ^ k) for i in range(row_count)])  14.9 us
    ppermute x6, waiting for transfers between devices, to_x(): lax.ppermute(array, 'col', [(i, i ^ CORES * k + cross) for i in range(col...  12.6 us
    ppermute x6, starting transfers between devices, to_x(): lax.ppermute(array, 'col', [(i, i ^ CORES * k + cross) for i in range(col...  8.97 us
    ppermute x7, waiting for transfers between devices, to_row(): return lax.ppermute(array, 'row', [(i, i ^ k) for i in range(row_count)])  8.82 us
    pallas_call x1, Pallas kernels, on_device(): pl.pallas_call(functools.partial(finish_kernel, root), out_shape=[jax.Sha...  5.72 us
    ppermute x5, waiting for transfers between devices, to_core(): return lax.ppermute(array, 'col', [(i, i ^ 1) for i in range(col_count)])  2.68 us
    pallas_call x1, Pallas kernels, on_device(): pl.pallas_call(functools.partial(select_kernel, x_count), out_shape=[VMEM...  2.31 us
  transfers between devices with their start and end apart: 18, of which 14 were waited for; matrix products, arithmetic and copies ran while one was open for 1% of the time, Pallas kernels for 0%

profile of v6, /device:TPU:32, one launch (start us, length us, event | category | flops | bytes accessed | tf_op | source)
XLA Modules:
  0.0 58.9 jit_solution(4870722559834032521)
XLA Ops:
  0.7 2.3 %select.17 = (f32[32,1024]{1,0:T(8,128)S(1)}, f32[32,1024]{1,0:T(8,128)S(1)}, f32[32,1024]{1,0:T(8,128)S(1)}, f32[32,1024]{1,0:T(8,128)S(1)}) custom-call(s32[64]{0:T(128)} %pivots_ref.1, f32[128,4096]{1,0:T(8,128)} %cand_ref.1), custom_call_target="tpu_custom_call" | custom-call | tf_op jit(solution)/shard_map/select/pallas_call | solution.py:223
  3.0 1.7 %collective-permute-start = (f32[32,1024]{1,0:T(8,128)S(1)}, f32[32,1024]{1,0:T(8,128)S(1)}, u32[]{:S(2)}, u32[]{:S(2)}) collective-permute-start(f32[32,1024]{1,0:T(8,128)S(1)} %get-tuple-element.13), channel_id=1, source_target_pairs={{0,2},{1,3},{2,0},{3,1},{4,6},{5,7},{6,4},{7,5},{8,10},{9,11},{10,... | collective-permute-start | bytes 393224 | tf_op jit(solution)/shard_map/ppermute | solution.py:211
  4.7 2.7 %collective-permute-start.1 = (f32[32,1024]{1,0:T(8,128)S(1)}, f32[32,1024]{1,0:T(8,128)S(1)}, u32[]{:S(2)}, u32[]{:S(2)}) collective-permute-start(f32[32,1024]{1,0:T(8,128)S(1)} %get-tuple-element.14), channel_id=1, source_target_pairs={{0,4},{1,5},{2,6},{3,7},{4,0},{5,1},{6,2},{7,3},{8,12},{9,13},{10,... | collective-permute-start | bytes 393224 | tf_op jit(solution)/shard_map/ppermute | solution.py:211
  7.3 0.4 collective-permute-start.2
  7.8 0.2 convert_reduce_fusion
  8.1 1.0 %collective-permute-done.rest_1_ = f32[32,1024]{1,0:T(8,128)S(1)} collective-permute-done((f32[32,1024]{1,0:T(8,128)S(1)}, f32[32,1024]{1,0:T(8,128)S(1)}, u32[]{:S(2)}, u32[]{:S(2)}) %collective-permute-start) | collective-permute-done | bytes 131104 | tf_op jit(solution)/shard_map/ppermute | solution.py:211
  9.1 4.1 %collective-permute-done.1.rest_2_ = f32[32,1024]{1,0:T(8,128)S(1)} collective-permute-done((f32[32,1024]{1,0:T(8,128)S(1)}, f32[32,1024]{1,0:T(8,128)S(1)}, u32[]{:S(2)}, u32[]{:S(2)}) %collective-permute-start.1) | collective-permute-done | bytes 131104 | tf_op jit(solution)/shard_map/ppermute | solution.py:211
  13.2 1.9 %collective-permute-done.2.rest_3_ = f32[32,1024]{1,0:T(8,128)S(1)} collective-permute-done((f32[32,1024]{1,0:T(8,128)S(1)}, f32[32,1024]{1,0:T(8,128)S(1)}, u32[]{:S(2)}, u32[]{:S(2)}) %collective-permute-start.2) | collective-permute-done | bytes 131104 | tf_op jit(solution)/shard_map/ppermute | solution.py:211
  15.1 0.2 merge.1
  15.5 1.3 %collective-permute-done.3 = f32[64,512]{1,0:T(8,128)S(1)} collective-permute-done((f32[64,512]{1,0:T(8,128)S(1)}, f32[64,512]{1,0:T(8,128)S(1)}, u32[]{:S(2)}, u32[]{:S(2)}) %collective-permute-start.3) | collective-permute-done | bytes 131104 | tf_op jit(solution)/shard_map/ppermute | solution.py:214
  16.8 1.0 %collective-permute-start.6 = (f32[64,512]{1,0:T(8,128)S(1)}, f32[64,512]{1,0:T(8,128)S(1)}, u32[]{:S(2)}, u32[]{:S(2)}) collective-permute-start(f32[64,512]{1,0:T(8,128)S(1)} %add.40.rest_0_), channel_id=1, source_target_pairs={{0,6},{1,7},{2,4},{3,5},{4,2},{5,3},{6,0},{7,1},{8,14},{9,15},{10,... | collective-permute-start | bytes 393224 | tf_op jit(solution)/shard_map/ppermute | solution.py:211
  17.9 0.8 %collective-permute-start.5 = (f32[64,512]{1,0:T(8,128)S(1)}, f32[64,512]{1,0:T(8,128)S(1)}, u32[]{:S(2)}, u32[]{:S(2)}) collective-permute-start(f32[64,512]{1,0:T(8,128)S(1)} %add.40.rest_0_), channel_id=1, source_target_pairs={{0,4},{1,5},{2,6},{3,7},{4,0},{5,1},{6,2},{7,3},{8,12},{9,13},{10,... | collective-permute-start | bytes 393224 | tf_op jit(solution)/shard_map/ppermute | solution.py:211
  18.7 2.3 %collective-permute-start.4 = (f32[64,512]{1,0:T(8,128)S(1)}, f32[64,512]{1,0:T(8,128)S(1)}, u32[]{:S(2)}, u32[]{:S(2)}) collective-permute-start(f32[64,512]{1,0:T(8,128)S(1)} %add.40.rest_0_), channel_id=1, source_target_pairs={{0,2},{1,3},{2,0},{3,1},{4,6},{5,7},{6,4},{7,5},{8,10},{9,11},{10,... | collective-permute-start | bytes 393224 | tf_op jit(solution)/shard_map/ppermute | solution.py:211
  21.0 5.5 %collective-permute-done.6.rest_3_ = f32[64,512]{1,0:T(8,128)S(1)} collective-permute-done((f32[64,512]{1,0:T(8,128)S(1)}, f32[64,512]{1,0:T(8,128)S(1)}, u32[]{:S(2)}, u32[]{:S(2)}) %collective-permute-start.6) | collective-permute-done | bytes 131104 | tf_op jit(solution)/shard_map/ppermute | solution.py:211
  26.5 0.5 collective-permute-start.9
  27.1 0.7 %collective-permute-done.10.rest_7_ = f32[64,512]{1,0:T(8,128)S(1)} collective-permute-done((f32[64,512]{1,0:T(8,128)S(1)}, f32[64,512]{1,0:T(8,128)S(1)}, u32[]{:S(2)}, u32[]{:S(2)}) %collective-permute-start.10) | collective-permute-done | bytes 131104 | tf_op jit(solution)/shard_map/ppermute | solution.py:214
  27.8 0.2 collective-permute-done.9.rest_6_
  28.0 0.4 collective-permute-done.8.rest_5_
  28.5 1.0 %gram.1 = (f32[64,128]{1,0:T(8,128)S(1)}, bf16[128,4096]{1,0:T(8,128)(2,1)S(1)}) custom-call(f32[64,512]{1,0:T(8,128)S(1)} %add.40.rest_0_, f32[64,512]{1,0:T(8,128)S(1)} %collective-permute-done.4.rest_1_, f32[64,512]{1,0:T(8,128)S(1)} %collective-permute-done.5.rest_2_, f32[64,512]{1,0:T(8,128)S(1)} %collective-permute-done.6.rest_3_, ...), custom_call_target="tpu_custom_call" | custom-call | tf_op jit(solution)/shard_map/gram/pallas_call | solution.py:242
  29.4 3.1 %collective-permute-start.13 = (f32[64,128]{1,0:T(8,128)S(1)}, f32[64,128]{1,0:T(8,128)S(1)}, u32[]{:S(2)}, u32[]{:S(2)}) collective-permute-start(f32[64,128]{1,0:T(8,128)S(1)} %get-tuple-element.18), channel_id=1, source_target_pairs={{0,24},{8,16},{16,8},{24,0},{32,56},{40,48},{48,40},{56,32},{64,88... | collective-permute-start | bytes 98312 | tf_op jit(solution)/shard_map/ppermute | solution.py:217
  32.5 0.6 %collective-permute-start.12 = (f32[64,128]{1,0:T(8,128)S(1)}, f32[64,128]{1,0:T(8,128)S(1)}, u32[]{:S(2)}, u32[]{:S(2)}) collective-permute-start(f32[64,128]{1,0:T(8,128)S(1)} %get-tuple-element.18), channel_id=1, source_target_pairs={{0,16},{8,24},{16,0},{24,8},{32,48},{40,56},{48,32},{56,40},{64,80... | collective-permute-start | bytes 98312 | tf_op jit(solution)/shard_map/ppermute | solution.py:217
  33.2 0.4 collective-permute-start.11
  33.6 1.0 %collective-permute-done.13 = f32[64,128]{1,0:T(8,128)S(1)} collective-permute-done((f32[64,128]{1,0:T(8,128)S(1)}, f32[64,128]{1,0:T(8,128)S(1)}, u32[]{:S(2)}, u32[]{:S(2)}) %collective-permute-start.13) | collective-permute-done | bytes 32800 | tf_op jit(solution)/shard_map/ppermute | solution.py:217
  34.6 3.3 %collective-permute-done.12 = f32[64,128]{1,0:T(8,128)S(1)} collective-permute-done((f32[64,128]{1,0:T(8,128)S(1)}, f32[64,128]{1,0:T(8,128)S(1)}, u32[]{:S(2)}, u32[]{:S(2)}) %collective-permute-start.12) | collective-permute-done | bytes 32800 | tf_op jit(solution)/shard_map/ppermute | solution.py:217
  38.0 2.0 %collective-permute-start.16 = (f32[64,128]{1,0:T(8,128)S(1)}, f32[64,128]{1,0:T(8,128)S(1)}, u32[]{:S(2)}, u32[]{:S(2)}) collective-permute-start(f32[64,128]{1,0:T(8,128)S(1)} %add_add_fusion.1), channel_id=1, source_target_pairs={{0,96},{8,104},{16,112},{24,120},{32,64},{40,72},{48,80},{56,88},{... | collective-permute-start | bytes 98312 | tf_op jit(solution)/shard_map/ppermute | solution.py:217
  40.0 1.4 %collective-permute-start.15 = (f32[64,128]{1,0:T(8,128)S(1)}, f32[64,128]{1,0:T(8,128)S(1)}, u32[]{:S(2)}, u32[]{:S(2)}) collective-permute-start(f32[64,128]{1,0:T(8,128)S(1)} %add_add_fusion.1), channel_id=1, source_target_pairs={{0,64},{8,72},{16,80},{24,88},{32,96},{40,104},{48,112},{56,120},{... | collective-permute-start | bytes 98312 | tf_op jit(solution)/shard_map/ppermute | solution.py:217
  41.4 1.4 %collective-permute-start.14 = (f32[64,128]{1,0:T(8,128)S(1)}, f32[64,128]{1,0:T(8,128)S(1)}, u32[]{:S(2)}, u32[]{:S(2)}) collective-permute-start(f32[64,128]{1,0:T(8,128)S(1)} %add_add_fusion.1), channel_id=1, source_target_pairs={{0,32},{8,40},{16,48},{24,56},{32,0},{40,8},{48,16},{56,24},{64,96... | collective-permute-start | bytes 98312 | tf_op jit(solution)/shard_map/ppermute | solution.py:217
  42.8 2.3 %collective-permute-done.15 = f32[64,128]{1,0:T(8,128)S(1)} collective-permute-done((f32[64,128]{1,0:T(8,128)S(1)}, f32[64,128]{1,0:T(8,128)S(1)}, u32[]{:S(2)}, u32[]{:S(2)}) %collective-permute-start.15) | collective-permute-done | bytes 32800 | tf_op jit(solution)/shard_map/ppermute | solution.py:217
  45.1 0.2 collective-permute-done.14
  45.4 5.9 %collective-permute-start.17 = (f32[64,128]{1,0:T(8,128)S(1)}, f32[64,128]{1,0:T(8,128)S(1)}, u32[]{:S(2)}, u32[]{:S(2)}) collective-permute-start(f32[64,128]{1,0:T(8,128)S(1)} %add_add_fusion.one_ref), channel_id=1, source_target_pairs={{0,224},{8,232},{16,240},{24,248},{32,192},{40,200},{48,208},{56,2... | collective-permute-start | bytes 98312 | tf_op jit(solution)/shard_map/ppermute | solution.py:217
  51.3 1.9 %collective-permute-done.17.two_ref = f32[64,128]{1,0:T(8,128)S(1)} collective-permute-done((f32[64,128]{1,0:T(8,128)S(1)}, f32[64,128]{1,0:T(8,128)S(1)}, u32[]{:S(2)}, u32[]{:S(2)}) %collective-permute-start.17) | collective-permute-done | bytes 32800 | tf_op jit(solution)/shard_map/ppermute | solution.py:217
  53.2 5.7 %finish.1 = (f32[64,64]{1,0:T(8,128)}, f32[64,64]{1,0:T(8,128)}, f32[64,4096]{1,0:T(8,128)}, f32[64,4096]{1,0:T(8,128)}) custom-call(f32[64,128]{1,0:T(8,128)S(1)} %add_add_fusion.one_ref, f32[64,128]{1,0:T(8,128)S(1)} %collective-permute-done.17.two_ref, bf16[128,4096]{1,0:T(8,128)(2,1)S(1)} %get-tuple-element.19.panel_ref, f32[64,4096]{1,0:T(8,128)} %trail_ref.1), custom_call_target="tpu_custom_call" | custom-call | tf_op jit(solution)/shard_map/finish/pallas_call | solution.py:257
  (19 shorter events, 0.4 us)
Async XLA Ops:
  0.6 7.1 %copy-start.1 = (s32[64]{0:T(128)S(1)}, s32[64]{0:T(128)}, u32[]{:S(2)}) copy-start(s32[64]{0:T(128)} %pivots_ref.1) | copy-start | bytes 772
  0.6 27.8 %copy-start = (f32[64,4096]{1,0:T(8,128)S(1)}, f32[64,4096]{1,0:T(8,128)}, u32[]{:S(2)}) copy-start(f32[64,4096]{1,0:T(8,128)} %trail_ref.1) | copy-start | bytes 3145732
  3.0 6.1 %collective-permute-start = (f32[32,1024]{1,0:T(8,128)S(1)}, f32[32,1024]{1,0:T(8,128)S(1)}, u32[]{:S(2)}, u32[]{:S(2)}) collective-permute-start(f32[32,1024]{1,0:T(8,128)S(1)} %get-tuple-element.13), channel_id=1, source_target_pairs={{0,2},{1,3},{2,0},{3,1},{4,6},{5,7},{6,4},{7,5},{8,10},{9,11},{10,... | collective-permute-start | bytes 393224 | tf_op jit(solution)/shard_map/ppermute | solution.py:211
  4.7 8.5 %collective-permute-start.1 = (f32[32,1024]{1,0:T(8,128)S(1)}, f32[32,1024]{1,0:T(8,128)S(1)}, u32[]{:S(2)}, u32[]{:S(2)}) collective-permute-start(f32[32,1024]{1,0:T(8,128)S(1)} %get-tuple-element.14), channel_id=1, source_target_pairs={{0,4},{1,5},{2,6},{3,7},{4,0},{5,1},{6,2},{7,3},{8,12},{9,13},{10,... | collective-permute-start | bytes 393224 | tf_op jit(solution)/shard_map/ppermute | solution.py:211
  7.3 7.8 %collective-permute-start.2 = (f32[32,1024]{1,0:T(8,128)S(1)}, f32[32,1024]{1,0:T(8,128)S(1)}, u32[]{:S(2)}, u32[]{:S(2)}) collective-permute-start(f32[32,1024]{1,0:T(8,128)S(1)} %get-tuple-element.15), channel_id=1, source_target_pairs={{0,6},{1,7},{2,4},{3,5},{4,2},{5,3},{6,0},{7,1},{8,14},{9,15},{10,... | collective-permute-start | bytes 393224 | tf_op jit(solution)/shard_map/ppermute | solution.py:211
  15.4 1.4 %collective-permute-start.3 = (f32[64,512]{1,0:T(8,128)S(1)}, f32[64,512]{1,0:T(8,128)S(1)}, u32[]{:S(2)}, u32[]{:S(2)}) collective-permute-start(f32[64,512]{1,0:T(8,128)S(1)} %get-tuple-element.17), channel_id=1, source_target_pairs={{0,1},{1,0},{2,3},{3,2},{4,5},{5,4},{6,7},{7,6},{8,9},{9,8},{10,11... | collective-permute-start | bytes 393224 | tf_op jit(solution)/shard_map/ppermute | solution.py:214
  16.8 9.7 %collective-permute-start.6 = (f32[64,512]{1,0:T(8,128)S(1)}, f32[64,512]{1,0:T(8,128)S(1)}, u32[]{:S(2)}, u32[]{:S(2)}) collective-permute-start(f32[64,512]{1,0:T(8,128)S(1)} %add.40.rest_0_), channel_id=1, source_target_pairs={{0,6},{1,7},{2,4},{3,5},{4,2},{5,3},{6,0},{7,1},{8,14},{9,15},{10,... | collective-permute-start | bytes 393224 | tf_op jit(solution)/shard_map/ppermute | solution.py:211
  17.9 8.6 %collective-permute-start.5 = (f32[64,512]{1,0:T(8,128)S(1)}, f32[64,512]{1,0:T(8,128)S(1)}, u32[]{:S(2)}, u32[]{:S(2)}) collective-permute-start(f32[64,512]{1,0:T(8,128)S(1)} %add.40.rest_0_), channel_id=1, source_target_pairs={{0,4},{1,5},{2,6},{3,7},{4,0},{5,1},{6,2},{7,3},{8,12},{9,13},{10,... | collective-permute-start | bytes 393224 | tf_op jit(solution)/shard_map/ppermute | solution.py:211
  18.7 8.4 %collective-permute-start.4 = (f32[64,512]{1,0:T(8,128)S(1)}, f32[64,512]{1,0:T(8,128)S(1)}, u32[]{:S(2)}, u32[]{:S(2)}) collective-permute-start(f32[64,512]{1,0:T(8,128)S(1)} %add.40.rest_0_), channel_id=1, source_target_pairs={{0,2},{1,3},{2,0},{3,1},{4,6},{5,7},{6,4},{7,5},{8,10},{9,11},{10,... | collective-permute-start | bytes 393224 | tf_op jit(solution)/shard_map/ppermute | solution.py:211
  21.0 6.1 %collective-permute-start.7 = (f32[64,512]{1,0:T(8,128)S(1)}, f32[64,512]{1,0:T(8,128)S(1)}, u32[]{:S(2)}, u32[]{:S(2)}) collective-permute-start(f32[64,512]{1,0:T(8,128)S(1)} %add.40.rest_0_), channel_id=1, source_target_pairs={{0,1},{1,0},{2,3},{3,2},{4,5},{5,4},{6,7},{7,6},{8,9},{9,8},{10,11... | collective-permute-start | bytes 393224 | tf_op jit(solution)/shard_map/ppermute | solution.py:214
  26.5 1.3 %collective-permute-start.10 = (f32[64,512]{1,0:T(8,128)S(1)}, f32[64,512]{1,0:T(8,128)S(1)}, u32[]{:S(2)}, u32[]{:S(2)}) collective-permute-start(f32[64,512]{1,0:T(8,128)S(1)} %collective-permute-done.6.rest_3_), channel_id=1, source_target_pairs={{0,1},{1,0},{2,3},{3,2},{4,5},{5,4},{6,7},{7,6},{8,9},{9,8},{10,11... | collective-permute-start | bytes 393224 | tf_op jit(solution)/shard_map/ppermute | solution.py:214
  26.5 1.5 %collective-permute-start.9 = (f32[64,512]{1,0:T(8,128)S(1)}, f32[64,512]{1,0:T(8,128)S(1)}, u32[]{:S(2)}, u32[]{:S(2)}) collective-permute-start(f32[64,512]{1,0:T(8,128)S(1)} %collective-permute-done.5.rest_2_), channel_id=1, source_target_pairs={{0,1},{1,0},{2,3},{3,2},{4,5},{5,4},{6,7},{7,6},{8,9},{9,8},{10,11... | collective-permute-start | bytes 393224 | tf_op jit(solution)/shard_map/ppermute | solution.py:214
  27.1 1.3 %collective-permute-start.8 = (f32[64,512]{1,0:T(8,128)S(1)}, f32[64,512]{1,0:T(8,128)S(1)}, u32[]{:S(2)}, u32[]{:S(2)}) collective-permute-start(f32[64,512]{1,0:T(8,128)S(1)} %collective-permute-done.4.rest_1_), channel_id=1, source_target_pairs={{0,1},{1,0},{2,3},{3,2},{4,5},{5,4},{6,7},{7,6},{8,9},{9,8},{10,11... | collective-permute-start | bytes 393224 | tf_op jit(solution)/shard_map/ppermute | solution.py:214
  29.4 5.2 %collective-permute-start.13 = (f32[64,128]{1,0:T(8,128)S(1)}, f32[64,128]{1,0:T(8,128)S(1)}, u32[]{:S(2)}, u32[]{:S(2)}) collective-permute-start(f32[64,128]{1,0:T(8,128)S(1)} %get-tuple-element.18), channel_id=1, source_target_pairs={{0,24},{8,16},{16,8},{24,0},{32,56},{40,48},{48,40},{56,32},{64,88... | collective-permute-start | bytes 98312 | tf_op jit(solution)/shard_map/ppermute | solution.py:217
  32.5 5.4 %collective-permute-start.12 = (f32[64,128]{1,0:T(8,128)S(1)}, f32[64,128]{1,0:T(8,128)S(1)}, u32[]{:S(2)}, u32[]{:S(2)}) collective-permute-start(f32[64,128]{1,0:T(8,128)S(1)} %get-tuple-element.18), channel_id=1, source_target_pairs={{0,16},{8,24},{16,0},{24,8},{32,48},{40,56},{48,32},{56,40},{64,80... | collective-permute-start | bytes 98312 | tf_op jit(solution)/shard_map/ppermute | solution.py:217
  33.2 4.8 %collective-permute-start.11 = (f32[64,128]{1,0:T(8,128)S(1)}, f32[64,128]{1,0:T(8,128)S(1)}, u32[]{:S(2)}, u32[]{:S(2)}) collective-permute-start(f32[64,128]{1,0:T(8,128)S(1)} %get-tuple-element.18), channel_id=1, source_target_pairs={{0,8},{8,0},{16,24},{24,16},{32,40},{40,32},{48,56},{56,48},{64,72... | collective-permute-start | bytes 98312 | tf_op jit(solution)/shard_map/ppermute | solution.py:217
  38.0 4.8 %collective-permute-start.16 = (f32[64,128]{1,0:T(8,128)S(1)}, f32[64,128]{1,0:T(8,128)S(1)}, u32[]{:S(2)}, u32[]{:S(2)}) collective-permute-start(f32[64,128]{1,0:T(8,128)S(1)} %add_add_fusion.1), channel_id=1, source_target_pairs={{0,96},{8,104},{16,112},{24,120},{32,64},{40,72},{48,80},{56,88},{... | collective-permute-start | bytes 98312 | tf_op jit(solution)/shard_map/ppermute | solution.py:217
  40.0 5.2 %collective-permute-start.15 = (f32[64,128]{1,0:T(8,128)S(1)}, f32[64,128]{1,0:T(8,128)S(1)}, u32[]{:S(2)}, u32[]{:S(2)}) collective-permute-start(f32[64,128]{1,0:T(8,128)S(1)} %add_add_fusion.1), channel_id=1, source_target_pairs={{0,64},{8,72},{16,80},{24,88},{32,96},{40,104},{48,112},{56,120},{... | collective-permute-start | bytes 98312 | tf_op jit(solution)/shard_map/ppermute | solution.py:217
  41.4 4.0 %collective-permute-start.14 = (f32[64,128]{1,0:T(8,128)S(1)}, f32[64,128]{1,0:T(8,128)S(1)}, u32[]{:S(2)}, u32[]{:S(2)}) collective-permute-start(f32[64,128]{1,0:T(8,128)S(1)} %add_add_fusion.1), channel_id=1, source_target_pairs={{0,32},{8,40},{16,48},{24,56},{32,0},{40,8},{48,16},{56,24},{64,96... | collective-permute-start | bytes 98312 | tf_op jit(solution)/shard_map/ppermute | solution.py:217
  45.4 7.8 %collective-permute-start.17 = (f32[64,128]{1,0:T(8,128)S(1)}, f32[64,128]{1,0:T(8,128)S(1)}, u32[]{:S(2)}, u32[]{:S(2)}) collective-permute-start(f32[64,128]{1,0:T(8,128)S(1)} %add_add_fusion.one_ref), channel_id=1, source_target_pairs={{0,224},{8,232},{16,240},{24,248},{32,192},{40,200},{48,208},{56,2... | collective-permute-start | bytes 98312 | tf_op jit(solution)/shard_map/ppermute | solution.py:217

commit v7 on v6

--- a/solution.py
+++ b/solution.py
@@ -153,9 +153,9 @@
     return jnp.concatenate(blocks, axis=0), jnp.concatenate(scales, axis=0)
 
 
-def finish_kernel(
-    root, one_ref, two_ref, panel_ref, trail_ref, upper_ref, coef_ref, basis_ref, next_ref, trail, basis, left_over, in_sem, out_sems
-):
+def finish_kernel(root, one_ref, two_ref, panel_ref, trail_ref, *rest):
+    upper_ref, coef_ref, basis_ref, next_ref = rest[:4]
+    upper, coef_out, trail, basis, left_over, in_sem, small_sems, out_sems = rest[4:]
     count = one_ref.shape[0]
     fetch = pltpu.make_async_copy(trail_ref, trail, in_sem)
     fetch.start()
@@ -164,8 +164,13 @@
     rows = lax.broadcasted_iota(jnp.int32, square, 0)
     lanes = lax.broadcasted_iota(jnp.int32, square, 1)
     factor, coef = work[:, :count], work[:, count:]
-    upper_ref[...] = jnp.where(lanes >= rows, factor, 0.0) * jnp.float32(1.0 / root)
-    coef_ref[...] = coef * jnp.float32(1.0 / root)
+    upper[...] = jnp.where(lanes >= rows, factor, 0.0) * jnp.float32(1.0 / root)
+    coef_out[...] = coef * jnp.float32(1.0 / root)
+    copies = []
+    for i, (source, target) in enumerate(((upper, upper_ref), (coef_out, coef_ref))):
+        copy = pltpu.make_async_copy(source, target, small_sems.at[i])
+        copy.start()
+        copies.append(copy)
     inverse = jnp.where(lanes < rows, factor, jnp.where(lanes == rows, scale[:, :count], 0.0))
     weights = outer_sum(coef, inverse)
     high, low = split_bf16(jnp.concatenate([inverse * jnp.float32(root), weights], axis=0))
@@ -173,7 +178,6 @@
     fetch.wait()
     chunks = out_sems.shape[0]
     width = panel_ref.shape[1] // chunks
-    copies = []
     for c in range(chunks):
         here = slice(c * width, (c + 1) * width)
         block = panel_ref[:, here]
@@ -259,9 +263,10 @@
         out_shape=[jax.ShapeDtypeStruct((count, count), f32)] * 2
         + [jax.ShapeDtypeStruct(large, f32)] * 2,
         in_specs=[in_vmem] * 3 + [anywhere],
-        out_specs=[in_vmem] * 2 + [anywhere] * 2,
-        scratch_shapes=[VMEM(large, f32)] * 3
-        + [pltpu.SemaphoreType.DMA(()), pltpu.SemaphoreType.DMA((4, 2))],
+        out_specs=[anywhere] * 4,
+        scratch_shapes=[VMEM((count, count), f32)] * 2
+        + [VMEM(large, f32)] * 3
+        + [pltpu.SemaphoreType.DMA(shape) for shape in ((), (2,), (4, 2))],
         name="finish",
     )(near(sums), near(far), near(panel), trailing)
 

time: 59.4 us -> 59 us (level)
    pallas_call x1, Pallas kernels: 5.72 us -> 5.12 us  [on_device(): pl.pallas_call(functools.partial(finish_kernel, root), out_shape=[jax.Sha...]
where the time goes in v7:
time: 59 us; the launch traced here: 58.6 us
  starting transfers between devices  24.5 us (42%)
  waiting for transfers between devices  24.2 us (41%)
  Pallas kernels  8.75 us (15%)
  between operations  0.74 us (1%)
    ppermute x7, starting transfers between devices, to_row(): return lax.ppermute(array, 'row', [(i, i ^ k) for i in range(row_count)])  14.9 us
    ppermute x6, waiting for transfers between devices, to_x(): lax.ppermute(array, 'col', [(i, i ^ CORES * k + cross) for i in range(col...  12.7 us
    ppermute x6, starting transfers between devices, to_x(): lax.ppermute(array, 'col', [(i, i ^ CORES * k + cross) for i in range(col...  8.97 us
    ppermute x7, waiting for transfers between devices, to_row(): return lax.ppermute(array, 'row', [(i, i ^ k) for i in range(row_count)])  8.82 us
    pallas_call x1, Pallas kernels, on_device(): pl.pallas_call(functools.partial(finish_kernel, root), out_shape=[jax.Sha...  5.12 us
    ppermute x5, waiting for transfers between devices, to_core(): return lax.ppermute(array, 'col', [(i, i ^ 1) for i in range(col_count)])  2.68 us
    pallas_call x1, Pallas kernels, on_device(): pl.pallas_call(functools.partial(select_kernel, x_count), out_shape=[VMEM...  2.43 us
  transfers between devices with their start and end apart: 18, of which 14 were waited for; matrix products, arithmetic and copies ran while one was open for 1% of the time, Pallas kernels for 0%

profile of v7, /device:TPU:32, one launch (start us, length us, event | category | flops | bytes accessed | tf_op | source)
XLA Modules:
  0.0 58.6 jit_solution(6135648258982121656)
XLA Ops:
  0.7 2.4 %select.17 = (f32[32,1024]{1,0:T(8,128)S(1)}, f32[32,1024]{1,0:T(8,128)S(1)}, f32[32,1024]{1,0:T(8,128)S(1)}, f32[32,1024]{1,0:T(8,128)S(1)}) custom-call(s32[64]{0:T(128)} %pivots_ref.1, f32[128,4096]{1,0:T(8,128)} %cand_ref.1), custom_call_target="tpu_custom_call" | custom-call | tf_op jit(solution)/shard_map/select/pallas_call | solution.py:227
  3.1 1.4 %collective-permute-start = (f32[32,1024]{1,0:T(8,128)S(1)}, f32[32,1024]{1,0:T(8,128)S(1)}, u32[]{:S(2)}, u32[]{:S(2)}) collective-permute-start(f32[32,1024]{1,0:T(8,128)S(1)} %get-tuple-element.13), channel_id=1, source_target_pairs={{0,2},{1,3},{2,0},{3,1},{4,6},{5,7},{6,4},{7,5},{8,10},{9,11},{10,... | collective-permute-start | bytes 393224 | tf_op jit(solution)/shard_map/ppermute | solution.py:215
  4.5 2.8 %collective-permute-start.1 = (f32[32,1024]{1,0:T(8,128)S(1)}, f32[32,1024]{1,0:T(8,128)S(1)}, u32[]{:S(2)}, u32[]{:S(2)}) collective-permute-start(f32[32,1024]{1,0:T(8,128)S(1)} %get-tuple-element.14), channel_id=1, source_target_pairs={{0,4},{1,5},{2,6},{3,7},{4,0},{5,1},{6,2},{7,3},{8,12},{9,13},{10,... | collective-permute-start | bytes 393224 | tf_op jit(solution)/shard_map/ppermute | solution.py:215
  7.3 0.5 collective-permute-start.2
  7.9 0.2 convert_reduce_fusion
  8.2 0.6 %collective-permute-done.rest_1_ = f32[32,1024]{1,0:T(8,128)S(1)} collective-permute-done((f32[32,1024]{1,0:T(8,128)S(1)}, f32[32,1024]{1,0:T(8,128)S(1)}, u32[]{:S(2)}, u32[]{:S(2)}) %collective-permute-start) | collective-permute-done | bytes 131104 | tf_op jit(solution)/shard_map/ppermute | solution.py:215
  8.8 4.5 %collective-permute-done.1.rest_2_ = f32[32,1024]{1,0:T(8,128)S(1)} collective-permute-done((f32[32,1024]{1,0:T(8,128)S(1)}, f32[32,1024]{1,0:T(8,128)S(1)}, u32[]{:S(2)}, u32[]{:S(2)}) %collective-permute-start.1) | collective-permute-done | bytes 131104 | tf_op jit(solution)/shard_map/ppermute | solution.py:215
  13.4 2.0 %collective-permute-done.2.rest_3_ = f32[32,1024]{1,0:T(8,128)S(1)} collective-permute-done((f32[32,1024]{1,0:T(8,128)S(1)}, f32[32,1024]{1,0:T(8,128)S(1)}, u32[]{:S(2)}, u32[]{:S(2)}) %collective-permute-start.2) | collective-permute-done | bytes 131104 | tf_op jit(solution)/shard_map/ppermute | solution.py:215
  15.4 0.2 merge.1
  15.7 1.3 %collective-permute-done.3 = f32[64,512]{1,0:T(8,128)S(1)} collective-permute-done((f32[64,512]{1,0:T(8,128)S(1)}, f32[64,512]{1,0:T(8,128)S(1)}, u32[]{:S(2)}, u32[]{:S(2)}) %collective-permute-start.3) | collective-permute-done | bytes 131104 | tf_op jit(solution)/shard_map/ppermute | solution.py:218
  17.1 0.7 %collective-permute-start.6 = (f32[64,512]{1,0:T(8,128)S(1)}, f32[64,512]{1,0:T(8,128)S(1)}, u32[]{:S(2)}, u32[]{:S(2)}) collective-permute-start(f32[64,512]{1,0:T(8,128)S(1)} %add.40.rest_0_), channel_id=1, source_target_pairs={{0,6},{1,7},{2,4},{3,5},{4,2},{5,3},{6,0},{7,1},{8,14},{9,15},{10,... | collective-permute-start | bytes 393224 | tf_op jit(solution)/shard_map/ppermute | solution.py:215
  17.8 0.9 %collective-permute-start.5 = (f32[64,512]{1,0:T(8,128)S(1)}, f32[64,512]{1,0:T(8,128)S(1)}, u32[]{:S(2)}, u32[]{:S(2)}) collective-permute-start(f32[64,512]{1,0:T(8,128)S(1)} %add.40.rest_0_), channel_id=1, source_target_pairs={{0,4},{1,5},{2,6},{3,7},{4,0},{5,1},{6,2},{7,3},{8,12},{9,13},{10,... | collective-permute-start | bytes 393224 | tf_op jit(solution)/shard_map/ppermute | solution.py:215
  18.7 2.5 %collective-permute-start.4 = (f32[64,512]{1,0:T(8,128)S(1)}, f32[64,512]{1,0:T(8,128)S(1)}, u32[]{:S(2)}, u32[]{:S(2)}) collective-permute-start(f32[64,512]{1,0:T(8,128)S(1)} %add.40.rest_0_), channel_id=1, source_target_pairs={{0,2},{1,3},{2,0},{3,1},{4,6},{5,7},{6,4},{7,5},{8,10},{9,11},{10,... | collective-permute-start | bytes 393224 | tf_op jit(solution)/shard_map/ppermute | solution.py:215
  21.3 5.5 %collective-permute-done.6.rest_3_ = f32[64,512]{1,0:T(8,128)S(1)} collective-permute-done((f32[64,512]{1,0:T(8,128)S(1)}, f32[64,512]{1,0:T(8,128)S(1)}, u32[]{:S(2)}, u32[]{:S(2)}) %collective-permute-start.6) | collective-permute-done | bytes 131104 | tf_op jit(solution)/shard_map/ppermute | solution.py:215
  26.7 0.5 collective-permute-start.9
  27.4 0.7 %collective-permute-done.10.rest_7_ = f32[64,512]{1,0:T(8,128)S(1)} collective-permute-done((f32[64,512]{1,0:T(8,128)S(1)}, f32[64,512]{1,0:T(8,128)S(1)}, u32[]{:S(2)}, u32[]{:S(2)}) %collective-permute-start.10) | collective-permute-done | bytes 131104 | tf_op jit(solution)/shard_map/ppermute | solution.py:218
  28.1 0.2 collective-permute-done.9.rest_6_
  28.3 0.4 collective-permute-done.8.rest_5_
  28.7 1.0 %gram.1 = (f32[64,128]{1,0:T(8,128)S(1)}, bf16[128,4096]{1,0:T(8,128)(2,1)S(1)}) custom-call(f32[64,512]{1,0:T(8,128)S(1)} %add.40.rest_0_, f32[64,512]{1,0:T(8,128)S(1)} %collective-permute-done.4.rest_1_, f32[64,512]{1,0:T(8,128)S(1)} %collective-permute-done.5.rest_2_, f32[64,512]{1,0:T(8,128)S(1)} %collective-permute-done.6.rest_3_, ...), custom_call_target="tpu_custom_call" | custom-call | tf_op jit(solution)/shard_map/gram/pallas_call | solution.py:246
  29.7 3.1 %collective-permute-start.13 = (f32[64,128]{1,0:T(8,128)S(1)}, f32[64,128]{1,0:T(8,128)S(1)}, u32[]{:S(2)}, u32[]{:S(2)}) collective-permute-start(f32[64,128]{1,0:T(8,128)S(1)} %get-tuple-element.18), channel_id=1, source_target_pairs={{0,24},{8,16},{16,8},{24,0},{32,56},{40,48},{48,40},{56,32},{64,88... | collective-permute-start | bytes 98312 | tf_op jit(solution)/shard_map/ppermute | solution.py:221
  32.8 0.6 %collective-permute-start.12 = (f32[64,128]{1,0:T(8,128)S(1)}, f32[64,128]{1,0:T(8,128)S(1)}, u32[]{:S(2)}, u32[]{:S(2)}) collective-permute-start(f32[64,128]{1,0:T(8,128)S(1)} %get-tuple-element.18), channel_id=1, source_target_pairs={{0,16},{8,24},{16,0},{24,8},{32,48},{40,56},{48,32},{56,40},{64,80... | collective-permute-start | bytes 98312 | tf_op jit(solution)/shard_map/ppermute | solution.py:221
  33.4 0.5 collective-permute-start.11
  33.9 1.0 %collective-permute-done.13 = f32[64,128]{1,0:T(8,128)S(1)} collective-permute-done((f32[64,128]{1,0:T(8,128)S(1)}, f32[64,128]{1,0:T(8,128)S(1)}, u32[]{:S(2)}, u32[]{:S(2)}) %collective-permute-start.13) | collective-permute-done | bytes 32800 | tf_op jit(solution)/shard_map/ppermute | solution.py:221
  34.9 3.3 %collective-permute-done.12 = f32[64,128]{1,0:T(8,128)S(1)} collective-permute-done((f32[64,128]{1,0:T(8,128)S(1)}, f32[64,128]{1,0:T(8,128)S(1)}, u32[]{:S(2)}, u32[]{:S(2)}) %collective-permute-start.12) | collective-permute-done | bytes 32800 | tf_op jit(solution)/shard_map/ppermute | solution.py:221
  38.2 2.0 %collective-permute-start.16 = (f32[64,128]{1,0:T(8,128)S(1)}, f32[64,128]{1,0:T(8,128)S(1)}, u32[]{:S(2)}, u32[]{:S(2)}) collective-permute-start(f32[64,128]{1,0:T(8,128)S(1)} %add_add_fusion.1), channel_id=1, source_target_pairs={{0,96},{8,104},{16,112},{24,120},{32,64},{40,72},{48,80},{56,88},{... | collective-permute-start | bytes 98312 | tf_op jit(solution)/shard_map/ppermute | solution.py:221
  40.2 1.4 %collective-permute-start.15 = (f32[64,128]{1,0:T(8,128)S(1)}, f32[64,128]{1,0:T(8,128)S(1)}, u32[]{:S(2)}, u32[]{:S(2)}) collective-permute-start(f32[64,128]{1,0:T(8,128)S(1)} %add_add_fusion.1), channel_id=1, source_target_pairs={{0,64},{8,72},{16,80},{24,88},{32,96},{40,104},{48,112},{56,120},{... | collective-permute-start | bytes 98312 | tf_op jit(solution)/shard_map/ppermute | solution.py:221
  41.7 1.4 %collective-permute-start.14 = (f32[64,128]{1,0:T(8,128)S(1)}, f32[64,128]{1,0:T(8,128)S(1)}, u32[]{:S(2)}, u32[]{:S(2)}) collective-permute-start(f32[64,128]{1,0:T(8,128)S(1)} %add_add_fusion.1), channel_id=1, source_target_pairs={{0,32},{8,40},{16,48},{24,56},{32,0},{40,8},{48,16},{56,24},{64,96... | collective-permute-start | bytes 98312 | tf_op jit(solution)/shard_map/ppermute | solution.py:221
  43.1 2.3 %collective-permute-done.15 = f32[64,128]{1,0:T(8,128)S(1)} collective-permute-done((f32[64,128]{1,0:T(8,128)S(1)}, f32[64,128]{1,0:T(8,128)S(1)}, u32[]{:S(2)}, u32[]{:S(2)}) %collective-permute-start.15) | collective-permute-done | bytes 32800 | tf_op jit(solution)/shard_map/ppermute | solution.py:221
  45.4 0.2 collective-permute-done.14
  45.6 5.9 %collective-permute-start.17 = (f32[64,128]{1,0:T(8,128)S(1)}, f32[64,128]{1,0:T(8,128)S(1)}, u32[]{:S(2)}, u32[]{:S(2)}) collective-permute-start(f32[64,128]{1,0:T(8,128)S(1)} %add_add_fusion.one_ref), channel_id=1, source_target_pairs={{0,224},{8,232},{16,240},{24,248},{32,192},{40,200},{48,208},{56,2... | collective-permute-start | bytes 98312 | tf_op jit(solution)/shard_map/ppermute | solution.py:221
  51.6 1.9 %collective-permute-done.17.two_ref = f32[64,128]{1,0:T(8,128)S(1)} collective-permute-done((f32[64,128]{1,0:T(8,128)S(1)}, f32[64,128]{1,0:T(8,128)S(1)}, u32[]{:S(2)}, u32[]{:S(2)}) %collective-permute-start.17) | collective-permute-done | bytes 32800 | tf_op jit(solution)/shard_map/ppermute | solution.py:221
  53.5 5.1 %finish.1 = (f32[64,64]{1,0:T(8,128)}, f32[64,64]{1,0:T(8,128)}, f32[64,4096]{1,0:T(8,128)}, f32[64,4096]{1,0:T(8,128)}) custom-call(f32[64,128]{1,0:T(8,128)S(1)} %add_add_fusion.one_ref, f32[64,128]{1,0:T(8,128)S(1)} %collective-permute-done.17.two_ref, bf16[128,4096]{1,0:T(8,128)(2,1)S(1)} %get-tuple-element.19.panel_ref, f32[64,4096]{1,0:T(8,128)} %trail_ref.1), custom_call_target="tpu_custom_call" | custom-call | tf_op jit(solution)/shard_map/finish/pallas_call | solution.py:261
  (19 shorter events, 0.4 us)
Async XLA Ops:
  0.6 7.3 %copy-start.1 = (s32[64]{0:T(128)S(1)}, s32[64]{0:T(128)}, u32[]{:S(2)}) copy-start(s32[64]{0:T(128)} %pivots_ref.1) | copy-start | bytes 772
  0.6 28.1 %copy-start = (f32[64,4096]{1,0:T(8,128)S(1)}, f32[64,4096]{1,0:T(8,128)}, u32[]{:S(2)}) copy-start(f32[64,4096]{1,0:T(8,128)} %trail_ref.1) | copy-start | bytes 3145732
  3.1 5.7 %collective-permute-start = (f32[32,1024]{1,0:T(8,128)S(1)}, f32[32,1024]{1,0:T(8,128)S(1)}, u32[]{:S(2)}, u32[]{:S(2)}) collective-permute-start(f32[32,1024]{1,0:T(8,128)S(1)} %get-tuple-element.13), channel_id=1, source_target_pairs={{0,2},{1,3},{2,0},{3,1},{4,6},{5,7},{6,4},{7,5},{8,10},{9,11},{10,... | collective-permute-start | bytes 393224 | tf_op jit(solution)/shard_map/ppermute | solution.py:215
  4.5 8.9 %collective-permute-start.1 = (f32[32,1024]{1,0:T(8,128)S(1)}, f32[32,1024]{1,0:T(8,128)S(1)}, u32[]{:S(2)}, u32[]{:S(2)}) collective-permute-start(f32[32,1024]{1,0:T(8,128)S(1)} %get-tuple-element.14), channel_id=1, source_target_pairs={{0,4},{1,5},{2,6},{3,7},{4,0},{5,1},{6,2},{7,3},{8,12},{9,13},{10,... | collective-permute-start | bytes 393224 | tf_op jit(solution)/shard_map/ppermute | solution.py:215
  7.3 8.0 %collective-permute-start.2 = (f32[32,1024]{1,0:T(8,128)S(1)}, f32[32,1024]{1,0:T(8,128)S(1)}, u32[]{:S(2)}, u32[]{:S(2)}) collective-permute-start(f32[32,1024]{1,0:T(8,128)S(1)} %get-tuple-element.15), channel_id=1, source_target_pairs={{0,6},{1,7},{2,4},{3,5},{4,2},{5,3},{6,0},{7,1},{8,14},{9,15},{10,... | collective-permute-start | bytes 393224 | tf_op jit(solution)/shard_map/ppermute | solution.py:215
  15.6 1.4 %collective-permute-start.3 = (f32[64,512]{1,0:T(8,128)S(1)}, f32[64,512]{1,0:T(8,128)S(1)}, u32[]{:S(2)}, u32[]{:S(2)}) collective-permute-start(f32[64,512]{1,0:T(8,128)S(1)} %get-tuple-element.17), channel_id=1, source_target_pairs={{0,1},{1,0},{2,3},{3,2},{4,5},{5,4},{6,7},{7,6},{8,9},{9,8},{10,11... | collective-permute-start | bytes 393224 | tf_op jit(solution)/shard_map/ppermute | solution.py:218
  17.1 9.7 %collective-permute-start.6 = (f32[64,512]{1,0:T(8,128)S(1)}, f32[64,512]{1,0:T(8,128)S(1)}, u32[]{:S(2)}, u32[]{:S(2)}) collective-permute-start(f32[64,512]{1,0:T(8,128)S(1)} %add.40.rest_0_), channel_id=1, source_target_pairs={{0,6},{1,7},{2,4},{3,5},{4,2},{5,3},{6,0},{7,1},{8,14},{9,15},{10,... | collective-permute-start | bytes 393224 | tf_op jit(solution)/shard_map/ppermute | solution.py:215
  17.8 8.9 %collective-permute-start.5 = (f32[64,512]{1,0:T(8,128)S(1)}, f32[64,512]{1,0:T(8,128)S(1)}, u32[]{:S(2)}, u32[]{:S(2)}) collective-permute-start(f32[64,512]{1,0:T(8,128)S(1)} %add.40.rest_0_), channel_id=1, source_target_pairs={{0,4},{1,5},{2,6},{3,7},{4,0},{5,1},{6,2},{7,3},{8,12},{9,13},{10,... | collective-permute-start | bytes 393224 | tf_op jit(solution)/shard_map/ppermute | solution.py:215
  18.7 8.6 %collective-permute-start.4 = (f32[64,512]{1,0:T(8,128)S(1)}, f32[64,512]{1,0:T(8,128)S(1)}, u32[]{:S(2)}, u32[]{:S(2)}) collective-permute-start(f32[64,512]{1,0:T(8,128)S(1)} %add.40.rest_0_), channel_id=1, source_target_pairs={{0,2},{1,3},{2,0},{3,1},{4,6},{5,7},{6,4},{7,5},{8,10},{9,11},{10,... | collective-permute-start | bytes 393224 | tf_op jit(solution)/shard_map/ppermute | solution.py:215
  21.3 6.1 %collective-permute-start.7 = (f32[64,512]{1,0:T(8,128)S(1)}, f32[64,512]{1,0:T(8,128)S(1)}, u32[]{:S(2)}, u32[]{:S(2)}) collective-permute-start(f32[64,512]{1,0:T(8,128)S(1)} %add.40.rest_0_), channel_id=1, source_target_pairs={{0,1},{1,0},{2,3},{3,2},{4,5},{5,4},{6,7},{7,6},{8,9},{9,8},{10,11... | collective-permute-start | bytes 393224 | tf_op jit(solution)/shard_map/ppermute | solution.py:218
  26.7 1.3 %collective-permute-start.10 = (f32[64,512]{1,0:T(8,128)S(1)}, f32[64,512]{1,0:T(8,128)S(1)}, u32[]{:S(2)}, u32[]{:S(2)}) collective-permute-start(f32[64,512]{1,0:T(8,128)S(1)} %collective-permute-done.6.rest_3_), channel_id=1, source_target_pairs={{0,1},{1,0},{2,3},{3,2},{4,5},{5,4},{6,7},{7,6},{8,9},{9,8},{10,11... | collective-permute-start | bytes 393224 | tf_op jit(solution)/shard_map/ppermute | solution.py:218
  26.7 1.5 %collective-permute-start.9 = (f32[64,512]{1,0:T(8,128)S(1)}, f32[64,512]{1,0:T(8,128)S(1)}, u32[]{:S(2)}, u32[]{:S(2)}) collective-permute-start(f32[64,512]{1,0:T(8,128)S(1)} %collective-permute-done.5.rest_2_), channel_id=1, source_target_pairs={{0,1},{1,0},{2,3},{3,2},{4,5},{5,4},{6,7},{7,6},{8,9},{9,8},{10,11... | collective-permute-start | bytes 393224 | tf_op jit(solution)/shard_map/ppermute | solution.py:218
  27.4 1.3 %collective-permute-start.8 = (f32[64,512]{1,0:T(8,128)S(1)}, f32[64,512]{1,0:T(8,128)S(1)}, u32[]{:S(2)}, u32[]{:S(2)}) collective-permute-start(f32[64,512]{1,0:T(8,128)S(1)} %collective-permute-done.4.rest_1_), channel_id=1, source_target_pairs={{0,1},{1,0},{2,3},{3,2},{4,5},{5,4},{6,7},{7,6},{8,9},{9,8},{10,11... | collective-permute-start | bytes 393224 | tf_op jit(solution)/shard_map/ppermute | solution.py:218
  29.7 5.2 %collective-permute-start.13 = (f32[64,128]{1,0:T(8,128)S(1)}, f32[64,128]{1,0:T(8,128)S(1)}, u32[]{:S(2)}, u32[]{:S(2)}) collective-permute-start(f32[64,128]{1,0:T(8,128)S(1)} %get-tuple-element.18), channel_id=1, source_target_pairs={{0,24},{8,16},{16,8},{24,0},{32,56},{40,48},{48,40},{56,32},{64,88... | collective-permute-start | bytes 98312 | tf_op jit(solution)/shard_map/ppermute | solution.py:221
  32.8 5.4 %collective-permute-start.12 = (f32[64,128]{1,0:T(8,128)S(1)}, f32[64,128]{1,0:T(8,128)S(1)}, u32[]{:S(2)}, u32[]{:S(2)}) collective-permute-start(f32[64,128]{1,0:T(8,128)S(1)} %get-tuple-element.18), channel_id=1, source_target_pairs={{0,16},{8,24},{16,0},{24,8},{32,48},{40,56},{48,32},{56,40},{64,80... | collective-permute-start | bytes 98312 | tf_op jit(solution)/shard_map/ppermute | solution.py:221
  33.4 4.8 %collective-permute-start.11 = (f32[64,128]{1,0:T(8,128)S(1)}, f32[64,128]{1,0:T(8,128)S(1)}, u32[]{:S(2)}, u32[]{:S(2)}) collective-permute-start(f32[64,128]{1,0:T(8,128)S(1)} %get-tuple-element.18), channel_id=1, source_target_pairs={{0,8},{8,0},{16,24},{24,16},{32,40},{40,32},{48,56},{56,48},{64,72... | collective-permute-start | bytes 98312 | tf_op jit(solution)/shard_map/ppermute | solution.py:221
  38.2 4.8 %collective-permute-start.16 = (f32[64,128]{1,0:T(8,128)S(1)}, f32[64,128]{1,0:T(8,128)S(1)}, u32[]{:S(2)}, u32[]{:S(2)}) collective-permute-start(f32[64,128]{1,0:T(8,128)S(1)} %add_add_fusion.1), channel_id=1, source_target_pairs={{0,96},{8,104},{16,112},{24,120},{32,64},{40,72},{48,80},{56,88},{... | collective-permute-start | bytes 98312 | tf_op jit(solution)/shard_map/ppermute | solution.py:221
  40.2 5.2 %collective-permute-start.15 = (f32[64,128]{1,0:T(8,128)S(1)}, f32[64,128]{1,0:T(8,128)S(1)}, u32[]{:S(2)}, u32[]{:S(2)}) collective-permute-start(f32[64,128]{1,0:T(8,128)S(1)} %add_add_fusion.1), channel_id=1, source_target_pairs={{0,64},{8,72},{16,80},{24,88},{32,96},{40,104},{48,112},{56,120},{... | collective-permute-start | bytes 98312 | tf_op jit(solution)/shard_map/ppermute | solution.py:221
  41.7 4.0 %collective-permute-start.14 = (f32[64,128]{1,0:T(8,128)S(1)}, f32[64,128]{1,0:T(8,128)S(1)}, u32[]{:S(2)}, u32[]{:S(2)}) collective-permute-start(f32[64,128]{1,0:T(8,128)S(1)} %add_add_fusion.1), channel_id=1, source_target_pairs={{0,32},{8,40},{16,48},{24,56},{32,0},{40,8},{48,16},{56,24},{64,96... | collective-permute-start | bytes 98312 | tf_op jit(solution)/shard_map/ppermute | solution.py:221
  45.6 7.8 %collective-permute-start.17 = (f32[64,128]{1,0:T(8,128)S(1)}, f32[64,128]{1,0:T(8,128)S(1)}, u32[]{:S(2)}, u32[]{:S(2)}) collective-permute-start(f32[64,128]{1,0:T(8,128)S(1)} %add_add_fusion.one_ref), channel_id=1, source_target_pairs={{0,224},{8,232},{16,240},{24,248},{32,192},{40,200},{48,208},{56,2... | collective-permute-start | bytes 98312 | tf_op jit(solution)/shard_map/ppermute | solution.py:221

commit v8 on v7

--- a/solution.py
+++ b/solution.py
@@ -117,7 +117,7 @@
 
 
 def eliminate(work):
-    size = 8
+    size = 32
     count, width = work.shape
     shape = (size, width)
     blocks = [work[begin : begin + size] for begin in range(0, count, size)]

time: 59 us -> 58 us (0.983)
  Pallas kernels: 8.75 us -> 7.65 us
    pallas_call x1, Pallas kernels: 5.12 us -> 4.03 us  [on_device(): pl.pallas_call(functools.partial(finish_kernel, root), out_shape=[jax.Sha...]
where the time goes in v8:
time: 58 us; the launch traced here: 57.6 us
  starting transfers between devices  24.5 us (42%)
  waiting for transfers between devices  24.4 us (42%)
  Pallas kernels  7.65 us (13%)
  between operations  0.74 us (1%)
    ppermute x7, starting transfers between devices, to_row(): return lax.ppermute(array, 'row', [(i, i ^ k) for i in range(row_count)])  14.9 us
    ppermute x6, waiting for transfers between devices, to_x(): lax.ppermute(array, 'col', [(i, i ^ CORES * k + cross) for i in range(col...  12.9 us
    ppermute x6, starting transfers between devices, to_x(): lax.ppermute(array, 'col', [(i, i ^ CORES * k + cross) for i in range(col...  8.97 us
    ppermute x7, waiting for transfers between devices, to_row(): return lax.ppermute(array, 'row', [(i, i ^ k) for i in range(row_count)])  8.82 us
    pallas_call x1, Pallas kernels, on_device(): pl.pallas_call(functools.partial(finish_kernel, root), out_shape=[jax.Sha...  4.03 us
    ppermute x5, waiting for transfers between devices, to_core(): return lax.ppermute(array, 'col', [(i, i ^ 1) for i in range(col_count)])  2.68 us
    pallas_call x1, Pallas kernels, on_device(): pl.pallas_call(functools.partial(select_kernel, x_count), out_shape=[VMEM...  2.42 us
  transfers between devices with their start and end apart: 18, of which 14 were waited for; matrix products, arithmetic and copies ran while one was open for 1% of the time, Pallas kernels for 0%

profile of v8, /device:TPU:32, one launch (start us, length us, event | category | flops | bytes accessed | tf_op | source)
XLA Modules:
  0.0 57.6 jit_solution(4291199630103834218)
XLA Ops:
  0.7 2.4 %select.17 = (f32[32,1024]{1,0:T(8,128)S(1)}, f32[32,1024]{1,0:T(8,128)S(1)}, f32[32,1024]{1,0:T(8,128)S(1)}, f32[32,1024]{1,0:T(8,128)S(1)}) custom-call(s32[64]{0:T(128)} %pivots_ref.1, f32[128,4096]{1,0:T(8,128)} %cand_ref.1), custom_call_target="tpu_custom_call" | custom-call | tf_op jit(solution)/shard_map/select/pallas_call | solution.py:227
  3.1 1.4 %collective-permute-start = (f32[32,1024]{1,0:T(8,128)S(1)}, f32[32,1024]{1,0:T(8,128)S(1)}, u32[]{:S(2)}, u32[]{:S(2)}) collective-permute-start(f32[32,1024]{1,0:T(8,128)S(1)} %get-tuple-element.13), channel_id=1, source_target_pairs={{0,2},{1,3},{2,0},{3,1},{4,6},{5,7},{6,4},{7,5},{8,10},{9,11},{10,... | collective-permute-start | bytes 393224 | tf_op jit(solution)/shard_map/ppermute | solution.py:215
  4.5 2.8 %collective-permute-start.1 = (f32[32,1024]{1,0:T(8,128)S(1)}, f32[32,1024]{1,0:T(8,128)S(1)}, u32[]{:S(2)}, u32[]{:S(2)}) collective-permute-start(f32[32,1024]{1,0:T(8,128)S(1)} %get-tuple-element.14), channel_id=1, source_target_pairs={{0,4},{1,5},{2,6},{3,7},{4,0},{5,1},{6,2},{7,3},{8,12},{9,13},{10,... | collective-permute-start | bytes 393224 | tf_op jit(solution)/shard_map/ppermute | solution.py:215
  7.3 0.6 collective-permute-start.2
  7.9 0.2 convert_reduce_fusion
  8.2 0.4 collective-permute-done.rest_1_
  8.6 4.8 %collective-permute-done.1.rest_2_ = f32[32,1024]{1,0:T(8,128)S(1)} collective-permute-done((f32[32,1024]{1,0:T(8,128)S(1)}, f32[32,1024]{1,0:T(8,128)S(1)}, u32[]{:S(2)}, u32[]{:S(2)}) %collective-permute-start.1) | collective-permute-done | bytes 131104 | tf_op jit(solution)/shard_map/ppermute | solution.py:215
  13.4 2.1 %collective-permute-done.2.rest_3_ = f32[32,1024]{1,0:T(8,128)S(1)} collective-permute-done((f32[32,1024]{1,0:T(8,128)S(1)}, f32[32,1024]{1,0:T(8,128)S(1)}, u32[]{:S(2)}, u32[]{:S(2)}) %collective-permute-start.2) | collective-permute-done | bytes 131104 | tf_op jit(solution)/shard_map/ppermute | solution.py:215
  15.5 0.2 merge.1
  15.8 1.3 %collective-permute-done.3 = f32[64,512]{1,0:T(8,128)S(1)} collective-permute-done((f32[64,512]{1,0:T(8,128)S(1)}, f32[64,512]{1,0:T(8,128)S(1)}, u32[]{:S(2)}, u32[]{:S(2)}) %collective-permute-start.3) | collective-permute-done | bytes 131104 | tf_op jit(solution)/shard_map/ppermute | solution.py:218
  17.2 0.8 %collective-permute-start.6 = (f32[64,512]{1,0:T(8,128)S(1)}, f32[64,512]{1,0:T(8,128)S(1)}, u32[]{:S(2)}, u32[]{:S(2)}) collective-permute-start(f32[64,512]{1,0:T(8,128)S(1)} %add.40.rest_0_), channel_id=1, source_target_pairs={{0,6},{1,7},{2,4},{3,5},{4,2},{5,3},{6,0},{7,1},{8,14},{9,15},{10,... | collective-permute-start | bytes 393224 | tf_op jit(solution)/shard_map/ppermute | solution.py:215
  17.9 1.0 %collective-permute-start.5 = (f32[64,512]{1,0:T(8,128)S(1)}, f32[64,512]{1,0:T(8,128)S(1)}, u32[]{:S(2)}, u32[]{:S(2)}) collective-permute-start(f32[64,512]{1,0:T(8,128)S(1)} %add.40.rest_0_), channel_id=1, source_target_pairs={{0,4},{1,5},{2,6},{3,7},{4,0},{5,1},{6,2},{7,3},{8,12},{9,13},{10,... | collective-permute-start | bytes 393224 | tf_op jit(solution)/shard_map/ppermute | solution.py:215
  18.9 2.5 %collective-permute-start.4 = (f32[64,512]{1,0:T(8,128)S(1)}, f32[64,512]{1,0:T(8,128)S(1)}, u32[]{:S(2)}, u32[]{:S(2)}) collective-permute-start(f32[64,512]{1,0:T(8,128)S(1)} %add.40.rest_0_), channel_id=1, source_target_pairs={{0,2},{1,3},{2,0},{3,1},{4,6},{5,7},{6,4},{7,5},{8,10},{9,11},{10,... | collective-permute-start | bytes 393224 | tf_op jit(solution)/shard_map/ppermute | solution.py:215
  21.4 5.5 %collective-permute-done.6.rest_3_ = f32[64,512]{1,0:T(8,128)S(1)} collective-permute-done((f32[64,512]{1,0:T(8,128)S(1)}, f32[64,512]{1,0:T(8,128)S(1)}, u32[]{:S(2)}, u32[]{:S(2)}) %collective-permute-start.6) | collective-permute-done | bytes 131104 | tf_op jit(solution)/shard_map/ppermute | solution.py:215
  26.8 0.5 collective-permute-start.9
  27.5 0.7 %collective-permute-done.10.rest_7_ = f32[64,512]{1,0:T(8,128)S(1)} collective-permute-done((f32[64,512]{1,0:T(8,128)S(1)}, f32[64,512]{1,0:T(8,128)S(1)}, u32[]{:S(2)}, u32[]{:S(2)}) %collective-permute-start.10) | collective-permute-done | bytes 131104 | tf_op jit(solution)/shard_map/ppermute | solution.py:218
  28.2 0.2 collective-permute-done.9.rest_6_
  28.4 0.4 collective-permute-done.8.rest_5_
  28.8 1.0 %gram.1 = (f32[64,128]{1,0:T(8,128)S(1)}, bf16[128,4096]{1,0:T(8,128)(2,1)S(1)}) custom-call(f32[64,512]{1,0:T(8,128)S(1)} %add.40.rest_0_, f32[64,512]{1,0:T(8,128)S(1)} %collective-permute-done.4.rest_1_, f32[64,512]{1,0:T(8,128)S(1)} %collective-permute-done.5.rest_2_, f32[64,512]{1,0:T(8,128)S(1)} %collective-permute-done.6.rest_3_, ...), custom_call_target="tpu_custom_call" | custom-call | tf_op jit(solution)/shard_map/gram/pallas_call | solution.py:246
  29.8 3.1 %collective-permute-start.13 = (f32[64,128]{1,0:T(8,128)S(1)}, f32[64,128]{1,0:T(8,128)S(1)}, u32[]{:S(2)}, u32[]{:S(2)}) collective-permute-start(f32[64,128]{1,0:T(8,128)S(1)} %get-tuple-element.18), channel_id=1, source_target_pairs={{0,24},{8,16},{16,8},{24,0},{32,56},{40,48},{48,40},{56,32},{64,88... | collective-permute-start | bytes 98312 | tf_op jit(solution)/shard_map/ppermute | solution.py:221
  32.9 0.6 %collective-permute-start.12 = (f32[64,128]{1,0:T(8,128)S(1)}, f32[64,128]{1,0:T(8,128)S(1)}, u32[]{:S(2)}, u32[]{:S(2)}) collective-permute-start(f32[64,128]{1,0:T(8,128)S(1)} %get-tuple-element.18), channel_id=1, source_target_pairs={{0,16},{8,24},{16,0},{24,8},{32,48},{40,56},{48,32},{56,40},{64,80... | collective-permute-start | bytes 98312 | tf_op jit(solution)/shard_map/ppermute | solution.py:221
  33.5 0.4 collective-permute-start.11
  34.0 1.0 %collective-permute-done.13 = f32[64,128]{1,0:T(8,128)S(1)} collective-permute-done((f32[64,128]{1,0:T(8,128)S(1)}, f32[64,128]{1,0:T(8,128)S(1)}, u32[]{:S(2)}, u32[]{:S(2)}) %collective-permute-start.13) | collective-permute-done | bytes 32800 | tf_op jit(solution)/shard_map/ppermute | solution.py:221
  35.0 3.3 %collective-permute-done.12 = f32[64,128]{1,0:T(8,128)S(1)} collective-permute-done((f32[64,128]{1,0:T(8,128)S(1)}, f32[64,128]{1,0:T(8,128)S(1)}, u32[]{:S(2)}, u32[]{:S(2)}) %collective-permute-start.12) | collective-permute-done | bytes 32800 | tf_op jit(solution)/shard_map/ppermute | solution.py:221
  38.3 2.0 %collective-permute-start.16 = (f32[64,128]{1,0:T(8,128)S(1)}, f32[64,128]{1,0:T(8,128)S(1)}, u32[]{:S(2)}, u32[]{:S(2)}) collective-permute-start(f32[64,128]{1,0:T(8,128)S(1)} %add_add_fusion.1), channel_id=1, source_target_pairs={{0,96},{8,104},{16,112},{24,120},{32,64},{40,72},{48,80},{56,88},{... | collective-permute-start | bytes 98312 | tf_op jit(solution)/shard_map/ppermute | solution.py:221
  40.3 1.4 %collective-permute-start.15 = (f32[64,128]{1,0:T(8,128)S(1)}, f32[64,128]{1,0:T(8,128)S(1)}, u32[]{:S(2)}, u32[]{:S(2)}) collective-permute-start(f32[64,128]{1,0:T(8,128)S(1)} %add_add_fusion.1), channel_id=1, source_target_pairs={{0,64},{8,72},{16,80},{24,88},{32,96},{40,104},{48,112},{56,120},{... | collective-permute-start | bytes 98312 | tf_op jit(solution)/shard_map/ppermute | solution.py:221
  41.8 1.4 %collective-permute-start.14 = (f32[64,128]{1,0:T(8,128)S(1)}, f32[64,128]{1,0:T(8,128)S(1)}, u32[]{:S(2)}, u32[]{:S(2)}) collective-permute-start(f32[64,128]{1,0:T(8,128)S(1)} %add_add_fusion.1), channel_id=1, source_target_pairs={{0,32},{8,40},{16,48},{24,56},{32,0},{40,8},{48,16},{56,24},{64,96... | collective-permute-start | bytes 98312 | tf_op jit(solution)/shard_map/ppermute | solution.py:221
  43.1 2.3 %collective-permute-done.15 = f32[64,128]{1,0:T(8,128)S(1)} collective-permute-done((f32[64,128]{1,0:T(8,128)S(1)}, f32[64,128]{1,0:T(8,128)S(1)}, u32[]{:S(2)}, u32[]{:S(2)}) %collective-permute-start.15) | collective-permute-done | bytes 32800 | tf_op jit(solution)/shard_map/ppermute | solution.py:221
  45.5 0.2 collective-permute-done.14
  45.7 5.9 %collective-permute-start.17 = (f32[64,128]{1,0:T(8,128)S(1)}, f32[64,128]{1,0:T(8,128)S(1)}, u32[]{:S(2)}, u32[]{:S(2)}) collective-permute-start(f32[64,128]{1,0:T(8,128)S(1)} %add_add_fusion.one_ref), channel_id=1, source_target_pairs={{0,224},{8,232},{16,240},{24,248},{32,192},{40,200},{48,208},{56,2... | collective-permute-start | bytes 98312 | tf_op jit(solution)/shard_map/ppermute | solution.py:221
  51.6 1.9 %collective-permute-done.17.two_ref = f32[64,128]{1,0:T(8,128)S(1)} collective-permute-done((f32[64,128]{1,0:T(8,128)S(1)}, f32[64,128]{1,0:T(8,128)S(1)}, u32[]{:S(2)}, u32[]{:S(2)}) %collective-permute-start.17) | collective-permute-done | bytes 32800 | tf_op jit(solution)/shard_map/ppermute | solution.py:221
  53.5 4.0 %finish.1 = (f32[64,64]{1,0:T(8,128)}, f32[64,64]{1,0:T(8,128)}, f32[64,4096]{1,0:T(8,128)}, f32[64,4096]{1,0:T(8,128)}) custom-call(f32[64,128]{1,0:T(8,128)S(1)} %add_add_fusion.one_ref, f32[64,128]{1,0:T(8,128)S(1)} %collective-permute-done.17.two_ref, bf16[128,4096]{1,0:T(8,128)(2,1)S(1)} %get-tuple-element.19.panel_ref, f32[64,4096]{1,0:T(8,128)} %trail_ref.1), custom_call_target="tpu_custom_call" | custom-call | tf_op jit(solution)/shard_map/finish/pallas_call | solution.py:261
  (19 shorter events, 0.4 us)
Async XLA Ops:
  0.6 7.2 %copy-start.1 = (s32[64]{0:T(128)S(1)}, s32[64]{0:T(128)}, u32[]{:S(2)}) copy-start(s32[64]{0:T(128)} %pivots_ref.1) | copy-start | bytes 772
  0.6 28.2 %copy-start = (f32[64,4096]{1,0:T(8,128)S(1)}, f32[64,4096]{1,0:T(8,128)}, u32[]{:S(2)}) copy-start(f32[64,4096]{1,0:T(8,128)} %trail_ref.1) | copy-start | bytes 3145732
  3.1 5.5 %collective-permute-start = (f32[32,1024]{1,0:T(8,128)S(1)}, f32[32,1024]{1,0:T(8,128)S(1)}, u32[]{:S(2)}, u32[]{:S(2)}) collective-permute-start(f32[32,1024]{1,0:T(8,128)S(1)} %get-tuple-element.13), channel_id=1, source_target_pairs={{0,2},{1,3},{2,0},{3,1},{4,6},{5,7},{6,4},{7,5},{8,10},{9,11},{10,... | collective-permute-start | bytes 393224 | tf_op jit(solution)/shard_map/ppermute | solution.py:215
  4.5 8.9 %collective-permute-start.1 = (f32[32,1024]{1,0:T(8,128)S(1)}, f32[32,1024]{1,0:T(8,128)S(1)}, u32[]{:S(2)}, u32[]{:S(2)}) collective-permute-start(f32[32,1024]{1,0:T(8,128)S(1)} %get-tuple-element.14), channel_id=1, source_target_pairs={{0,4},{1,5},{2,6},{3,7},{4,0},{5,1},{6,2},{7,3},{8,12},{9,13},{10,... | collective-permute-start | bytes 393224 | tf_op jit(solution)/shard_map/ppermute | solution.py:215
  7.3 8.2 %collective-permute-start.2 = (f32[32,1024]{1,0:T(8,128)S(1)}, f32[32,1024]{1,0:T(8,128)S(1)}, u32[]{:S(2)}, u32[]{:S(2)}) collective-permute-start(f32[32,1024]{1,0:T(8,128)S(1)} %get-tuple-element.15), channel_id=1, source_target_pairs={{0,6},{1,7},{2,4},{3,5},{4,2},{5,3},{6,0},{7,1},{8,14},{9,15},{10,... | collective-permute-start | bytes 393224 | tf_op jit(solution)/shard_map/ppermute | solution.py:215
  15.7 1.4 %collective-permute-start.3 = (f32[64,512]{1,0:T(8,128)S(1)}, f32[64,512]{1,0:T(8,128)S(1)}, u32[]{:S(2)}, u32[]{:S(2)}) collective-permute-start(f32[64,512]{1,0:T(8,128)S(1)} %get-tuple-element.17), channel_id=1, source_target_pairs={{0,1},{1,0},{2,3},{3,2},{4,5},{5,4},{6,7},{7,6},{8,9},{9,8},{10,11... | collective-permute-start | bytes 393224 | tf_op jit(solution)/shard_map/ppermute | solution.py:218
  17.2 9.7 %collective-permute-start.6 = (f32[64,512]{1,0:T(8,128)S(1)}, f32[64,512]{1,0:T(8,128)S(1)}, u32[]{:S(2)}, u32[]{:S(2)}) collective-permute-start(f32[64,512]{1,0:T(8,128)S(1)} %add.40.rest_0_), channel_id=1, source_target_pairs={{0,6},{1,7},{2,4},{3,5},{4,2},{5,3},{6,0},{7,1},{8,14},{9,15},{10,... | collective-permute-start | bytes 393224 | tf_op jit(solution)/shard_map/ppermute | solution.py:215
  17.9 8.9 %collective-permute-start.5 = (f32[64,512]{1,0:T(8,128)S(1)}, f32[64,512]{1,0:T(8,128)S(1)}, u32[]{:S(2)}, u32[]{:S(2)}) collective-permute-start(f32[64,512]{1,0:T(8,128)S(1)} %add.40.rest_0_), channel_id=1, source_target_pairs={{0,4},{1,5},{2,6},{3,7},{4,0},{5,1},{6,2},{7,3},{8,12},{9,13},{10,... | collective-permute-start | bytes 393224 | tf_op jit(solution)/shard_map/ppermute | solution.py:215
  18.9 8.6 %collective-permute-start.4 = (f32[64,512]{1,0:T(8,128)S(1)}, f32[64,512]{1,0:T(8,128)S(1)}, u32[]{:S(2)}, u32[]{:S(2)}) collective-permute-start(f32[64,512]{1,0:T(8,128)S(1)} %add.40.rest_0_), channel_id=1, source_target_pairs={{0,2},{1,3},{2,0},{3,1},{4,6},{5,7},{6,4},{7,5},{8,10},{9,11},{10,... | collective-permute-start | bytes 393224 | tf_op jit(solution)/shard_map/ppermute | solution.py:215
  21.4 6.1 %collective-permute-start.7 = (f32[64,512]{1,0:T(8,128)S(1)}, f32[64,512]{1,0:T(8,128)S(1)}, u32[]{:S(2)}, u32[]{:S(2)}) collective-permute-start(f32[64,512]{1,0:T(8,128)S(1)} %add.40.rest_0_), channel_id=1, source_target_pairs={{0,1},{1,0},{2,3},{3,2},{4,5},{5,4},{6,7},{7,6},{8,9},{9,8},{10,11... | collective-permute-start | bytes 393224 | tf_op jit(solution)/shard_map/ppermute | solution.py:218
  26.8 1.3 %collective-permute-start.10 = (f32[64,512]{1,0:T(8,128)S(1)}, f32[64,512]{1,0:T(8,128)S(1)}, u32[]{:S(2)}, u32[]{:S(2)}) collective-permute-start(f32[64,512]{1,0:T(8,128)S(1)} %collective-permute-done.6.rest_3_), channel_id=1, source_target_pairs={{0,1},{1,0},{2,3},{3,2},{4,5},{5,4},{6,7},{7,6},{8,9},{9,8},{10,11... | collective-permute-start | bytes 393224 | tf_op jit(solution)/shard_map/ppermute | solution.py:218
  26.8 1.5 %collective-permute-start.9 = (f32[64,512]{1,0:T(8,128)S(1)}, f32[64,512]{1,0:T(8,128)S(1)}, u32[]{:S(2)}, u32[]{:S(2)}) collective-permute-start(f32[64,512]{1,0:T(8,128)S(1)} %collective-permute-done.5.rest_2_), channel_id=1, source_target_pairs={{0,1},{1,0},{2,3},{3,2},{4,5},{5,4},{6,7},{7,6},{8,9},{9,8},{10,11... | collective-permute-start | bytes 393224 | tf_op jit(solution)/shard_map/ppermute | solution.py:218
  27.5 1.3 %collective-permute-start.8 = (f32[64,512]{1,0:T(8,128)S(1)}, f32[64,512]{1,0:T(8,128)S(1)}, u32[]{:S(2)}, u32[]{:S(2)}) collective-permute-start(f32[64,512]{1,0:T(8,128)S(1)} %collective-permute-done.4.rest_1_), channel_id=1, source_target_pairs={{0,1},{1,0},{2,3},{3,2},{4,5},{5,4},{6,7},{7,6},{8,9},{9,8},{10,11... | collective-permute-start | bytes 393224 | tf_op jit(solution)/shard_map/ppermute | solution.py:218
  29.8 5.2 %collective-permute-start.13 = (f32[64,128]{1,0:T(8,128)S(1)}, f32[64,128]{1,0:T(8,128)S(1)}, u32[]{:S(2)}, u32[]{:S(2)}) collective-permute-start(f32[64,128]{1,0:T(8,128)S(1)} %get-tuple-element.18), channel_id=1, source_target_pairs={{0,24},{8,16},{16,8},{24,0},{32,56},{40,48},{48,40},{56,32},{64,88... | collective-permute-start | bytes 98312 | tf_op jit(solution)/shard_map/ppermute | solution.py:221
  32.9 5.4 %collective-permute-start.12 = (f32[64,128]{1,0:T(8,128)S(1)}, f32[64,128]{1,0:T(8,128)S(1)}, u32[]{:S(2)}, u32[]{:S(2)}) collective-permute-start(f32[64,128]{1,0:T(8,128)S(1)} %get-tuple-element.18), channel_id=1, source_target_pairs={{0,16},{8,24},{16,0},{24,8},{32,48},{40,56},{48,32},{56,40},{64,80... | collective-permute-start | bytes 98312 | tf_op jit(solution)/shard_map/ppermute | solution.py:221
  33.5 4.8 %collective-permute-start.11 = (f32[64,128]{1,0:T(8,128)S(1)}, f32[64,128]{1,0:T(8,128)S(1)}, u32[]{:S(2)}, u32[]{:S(2)}) collective-permute-start(f32[64,128]{1,0:T(8,128)S(1)} %get-tuple-element.18), channel_id=1, source_target_pairs={{0,8},{8,0},{16,24},{24,16},{32,40},{40,32},{48,56},{56,48},{64,72... | collective-permute-start | bytes 98312 | tf_op jit(solution)/shard_map/ppermute | solution.py:221
  38.3 4.8 %collective-permute-start.16 = (f32[64,128]{1,0:T(8,128)S(1)}, f32[64,128]{1,0:T(8,128)S(1)}, u32[]{:S(2)}, u32[]{:S(2)}) collective-permute-start(f32[64,128]{1,0:T(8,128)S(1)} %add_add_fusion.1), channel_id=1, source_target_pairs={{0,96},{8,104},{16,112},{24,120},{32,64},{40,72},{48,80},{56,88},{... | collective-permute-start | bytes 98312 | tf_op jit(solution)/shard_map/ppermute | solution.py:221
  40.3 5.2 %collective-permute-start.15 = (f32[64,128]{1,0:T(8,128)S(1)}, f32[64,128]{1,0:T(8,128)S(1)}, u32[]{:S(2)}, u32[]{:S(2)}) collective-permute-start(f32[64,128]{1,0:T(8,128)S(1)} %add_add_fusion.1), channel_id=1, source_target_pairs={{0,64},{8,72},{16,80},{24,88},{32,96},{40,104},{48,112},{56,120},{... | collective-permute-start | bytes 98312 | tf_op jit(solution)/shard_map/ppermute | solution.py:221
  41.8 4.0 %collective-permute-start.14 = (f32[64,128]{1,0:T(8,128)S(1)}, f32[64,128]{1,0:T(8,128)S(1)}, u32[]{:S(2)}, u32[]{:S(2)}) collective-permute-start(f32[64,128]{1,0:T(8,128)S(1)} %add_add_fusion.1), channel_id=1, source_target_pairs={{0,32},{8,40},{16,48},{24,56},{32,0},{40,8},{48,16},{56,24},{64,96... | collective-permute-start | bytes 98312 | tf_op jit(solution)/shard_map/ppermute | solution.py:221
  45.7 7.8 %collective-permute-start.17 = (f32[64,128]{1,0:T(8,128)S(1)}, f32[64,128]{1,0:T(8,128)S(1)}, u32[]{:S(2)}, u32[]{:S(2)}) collective-permute-start(f32[64,128]{1,0:T(8,128)S(1)} %add_add_fusion.one_ref), channel_id=1, source_target_pairs={{0,224},{8,232},{16,240},{24,248},{32,192},{40,200},{48,208},{56,2... | collective-permute-start | bytes 98312 | tf_op jit(solution)/shard_map/ppermute | solution.py:221

commit v9 on v8

--- a/solution.py
+++ b/solution.py
@@ -117,39 +117,53 @@
 
 
 def eliminate(work):
-    size = 32
+    size, group = 32, 8
     count, width = work.shape
-    shape = (size, width)
-    blocks = [work[begin : begin + size] for begin in range(0, count, size)]
+    shape = (group, width)
+    blocks = [work[begin : begin + group] for begin in range(0, count, group)]
+    scales = [jnp.zeros(shape, jnp.float32)] * len(blocks)
     rows = lax.broadcasted_iota(jnp.int32, shape, 0)
     lanes = lax.broadcasted_iota(jnp.int32, shape, 1)
-    scales = []
-    for b in range(len(blocks)):
-        block = blocks[b]
+    for begin in range(0, count, size):
+        first, last = begin // group, (begin + size) // group
         columns = [
-            jnp.broadcast_to(block[:, size * b + k : size * b + k + 1], shape) for k in range(size)
+            {
+                h: jnp.broadcast_to(blocks[h][:, begin + k : begin + k + 1], shape)
+                for h in range(first + k // group, last)
+            }
+            for k in range(size)
         ]
-        scale = jnp.zeros(shape, jnp.float32)
         for j in range(size):
-            pivot = jnp.broadcast_to(columns[j][j : j + 1], shape)
-            scale = jnp.where(rows == j, lax.rsqrt(pivot), scale)
-            below = rows > j
-            factor = jnp.where(below, columns[j] * (1.0 / pivot), 0.0)
+            g, r = first + j // group, j % group
+            pivot = jnp.broadcast_to(columns[j][g][r : r + 1], shape)
+            inverse = lax.rsqrt(pivot)
+            scales[g] = jnp.where(rows == r, inverse, scales[g])
+            below = rows > r
+            factors = {h: column * inverse for h, column in columns[j].items()}
+            factors[g] = jnp.where(below, factors[g], 0.0)
             for k in range(j + 1, size):
-                columns[k] -= factor * jnp.broadcast_to(columns[k][j : j + 1], shape)
-            here = lanes == size * b + j
-            row = jnp.where(here, 1.0, jnp.broadcast_to(block[j : j + 1], shape))
-            block = jnp.where(here & below, 0.0, block) - factor * row
-        block *= scale
-        blocks[b] = block
-        scales.append(scale)
-        if b + 1 < len(blocks):
-            place = lanes - size * b
+                h, s = first + k // group, k % group
+                across = jnp.broadcast_to(columns[j][h][s : s + 1], shape) * inverse
+                for h in columns[k]:
+                    columns[k][h] -= factors[h] * across
+            here = lanes == begin + j
+            row = jnp.where(here, 1.0, jnp.broadcast_to(blocks[g][r : r + 1], shape)) * inverse
+            for h in range(g, last):
+                cleared = jnp.where(here & below if h == g else here, 0.0, blocks[h])
+                blocks[h] = cleared - factors[h] * row
+        for h in range(first, last):
+            blocks[h] *= scales[h]
+        if last < len(blocks):
+            block = jnp.concatenate(blocks[first:last], axis=0)
+            scale = jnp.concatenate(scales[first:last], axis=0)
+            place = lax.broadcasted_iota(jnp.int32, block.shape, 1) - begin
+            order = lax.broadcasted_iota(jnp.int32, block.shape, 0)
+            lower = jnp.where(place < order, block, jnp.where(place == order, scale, 0.0))
             inside = (place >= 0) & (place < size)
-            inverse = jnp.where(place < rows, block, jnp.where(place == rows, scale, 0.0))
-            update = outer_sum(block[:, :count], jnp.where(inside, inverse, block))
-            for c in range(b + 1, len(blocks)):
-                blocks[c] = jnp.where(inside, 0.0, blocks[c]) - update[size * c : size * (c + 1)]
+            update = outer_sum(block[:, :count], jnp.where(inside, lower, block))
+            inside = (lanes >= begin) & (lanes < begin + size)
+            for h in range(last, len(blocks)):
+                blocks[h] = jnp.where(inside, 0.0, blocks[h]) - update[group * h : group * (h + 1)]
     return jnp.concatenate(blocks, axis=0), jnp.concatenate(scales, axis=0)
 
 

time: 58 us -> 57.5 us (level)
  no operation moved by 1% of the time
where the time goes in v9:
time: 57.5 us; the launch traced here: 57.2 us
  starting transfers between devices  24.5 us (43%)
  waiting for transfers between devices  24.4 us (42%)
  Pallas kernels  7.31 us (13%)
  between operations  0.74 us (1%)
    ppermute x7, starting transfers between devices, to_row(): return lax.ppermute(array, 'row', [(i, i ^ k) for i in range(row_count)])  14.9 us
    ppermute x6, waiting for transfers between devices, to_x(): lax.ppermute(array, 'col', [(i, i ^ CORES * k + cross) for i in range(col...  12.9 us
    ppermute x6, starting transfers between devices, to_x(): lax.ppermute(array, 'col', [(i, i ^ CORES * k + cross) for i in range(col...  8.97 us
    ppermute x7, waiting for transfers between devices, to_row(): return lax.ppermute(array, 'row', [(i, i ^ k) for i in range(row_count)])  8.82 us
    pallas_call x1, Pallas kernels, on_device(): pl.pallas_call(functools.partial(finish_kernel, root), out_shape=[jax.Sha...  3.82 us
    ppermute x5, waiting for transfers between devices, to_core(): return lax.ppermute(array, 'col', [(i, i ^ 1) for i in range(col_count)])  2.68 us
    pallas_call x1, Pallas kernels, on_device(): pl.pallas_call(functools.partial(select_kernel, x_count), out_shape=[VMEM...  2.29 us
  transfers between devices with their start and end apart: 18, of which 14 were waited for; matrix products, arithmetic and copies ran while one was open for 1% of the time, Pallas kernels for 0%

profile of v9, /device:TPU:32, one launch (start us, length us, event | category | flops | bytes accessed | tf_op | source)
XLA Modules:
  0.0 57.2 jit_solution(14729453979071888942)
XLA Ops:
  0.7 2.3 %select.17 = (f32[32,1024]{1,0:T(8,128)S(1)}, f32[32,1024]{1,0:T(8,128)S(1)}, f32[32,1024]{1,0:T(8,128)S(1)}, f32[32,1024]{1,0:T(8,128)S(1)}) custom-call(s32[64]{0:T(128)} %pivots_ref.1, f32[128,4096]{1,0:T(8,128)} %cand_ref.1), custom_call_target="tpu_custom_call" | custom-call | tf_op jit(solution)/shard_map/select/pallas_call | solution.py:241
  2.9 1.6 %collective-permute-start = (f32[32,1024]{1,0:T(8,128)S(1)}, f32[32,1024]{1,0:T(8,128)S(1)}, u32[]{:S(2)}, u32[]{:S(2)}) collective-permute-start(f32[32,1024]{1,0:T(8,128)S(1)} %get-tuple-element.13), channel_id=1, source_target_pairs={{0,2},{1,3},{2,0},{3,1},{4,6},{5,7},{6,4},{7,5},{8,10},{9,11},{10,... | collective-permute-start | bytes 393224 | tf_op jit(solution)/shard_map/ppermute | solution.py:229
  4.6 2.7 %collective-permute-start.1 = (f32[32,1024]{1,0:T(8,128)S(1)}, f32[32,1024]{1,0:T(8,128)S(1)}, u32[]{:S(2)}, u32[]{:S(2)}) collective-permute-start(f32[32,1024]{1,0:T(8,128)S(1)} %get-tuple-element.14), channel_id=1, source_target_pairs={{0,4},{1,5},{2,6},{3,7},{4,0},{5,1},{6,2},{7,3},{8,12},{9,13},{10,... | collective-permute-start | bytes 393224 | tf_op jit(solution)/shard_map/ppermute | solution.py:229
  7.2 0.5 collective-permute-start.2
  7.8 0.2 convert_reduce_fusion
  8.1 0.9 %collective-permute-done.rest_1_ = f32[32,1024]{1,0:T(8,128)S(1)} collective-permute-done((f32[32,1024]{1,0:T(8,128)S(1)}, f32[32,1024]{1,0:T(8,128)S(1)}, u32[]{:S(2)}, u32[]{:S(2)}) %collective-permute-start) | collective-permute-done | bytes 131104 | tf_op jit(solution)/shard_map/ppermute | solution.py:229
  9.0 4.4 %collective-permute-done.1.rest_2_ = f32[32,1024]{1,0:T(8,128)S(1)} collective-permute-done((f32[32,1024]{1,0:T(8,128)S(1)}, f32[32,1024]{1,0:T(8,128)S(1)}, u32[]{:S(2)}, u32[]{:S(2)}) %collective-permute-start.1) | collective-permute-done | bytes 131104 | tf_op jit(solution)/shard_map/ppermute | solution.py:229
  13.3 2.0 %collective-permute-done.2.rest_3_ = f32[32,1024]{1,0:T(8,128)S(1)} collective-permute-done((f32[32,1024]{1,0:T(8,128)S(1)}, f32[32,1024]{1,0:T(8,128)S(1)}, u32[]{:S(2)}, u32[]{:S(2)}) %collective-permute-start.2) | collective-permute-done | bytes 131104 | tf_op jit(solution)/shard_map/ppermute | solution.py:229
  15.4 0.2 merge.1
  15.7 1.3 %collective-permute-done.3 = f32[64,512]{1,0:T(8,128)S(1)} collective-permute-done((f32[64,512]{1,0:T(8,128)S(1)}, f32[64,512]{1,0:T(8,128)S(1)}, u32[]{:S(2)}, u32[]{:S(2)}) %collective-permute-start.3) | collective-permute-done | bytes 131104 | tf_op jit(solution)/shard_map/ppermute | solution.py:232
  17.1 0.9 %collective-permute-start.6 = (f32[64,512]{1,0:T(8,128)S(1)}, f32[64,512]{1,0:T(8,128)S(1)}, u32[]{:S(2)}, u32[]{:S(2)}) collective-permute-start(f32[64,512]{1,0:T(8,128)S(1)} %add.40.rest_0_), channel_id=1, source_target_pairs={{0,6},{1,7},{2,4},{3,5},{4,2},{5,3},{6,0},{7,1},{8,14},{9,15},{10,... | collective-permute-start | bytes 393224 | tf_op jit(solution)/shard_map/ppermute | solution.py:229
  18.0 0.9 %collective-permute-start.5 = (f32[64,512]{1,0:T(8,128)S(1)}, f32[64,512]{1,0:T(8,128)S(1)}, u32[]{:S(2)}, u32[]{:S(2)}) collective-permute-start(f32[64,512]{1,0:T(8,128)S(1)} %add.40.rest_0_), channel_id=1, source_target_pairs={{0,4},{1,5},{2,6},{3,7},{4,0},{5,1},{6,2},{7,3},{8,12},{9,13},{10,... | collective-permute-start | bytes 393224 | tf_op jit(solution)/shard_map/ppermute | solution.py:229
  18.8 2.4 %collective-permute-start.4 = (f32[64,512]{1,0:T(8,128)S(1)}, f32[64,512]{1,0:T(8,128)S(1)}, u32[]{:S(2)}, u32[]{:S(2)}) collective-permute-start(f32[64,512]{1,0:T(8,128)S(1)} %add.40.rest_0_), channel_id=1, source_target_pairs={{0,2},{1,3},{2,0},{3,1},{4,6},{5,7},{6,4},{7,5},{8,10},{9,11},{10,... | collective-permute-start | bytes 393224 | tf_op jit(solution)/shard_map/ppermute | solution.py:229
  21.2 5.5 %collective-permute-done.6.rest_3_ = f32[64,512]{1,0:T(8,128)S(1)} collective-permute-done((f32[64,512]{1,0:T(8,128)S(1)}, f32[64,512]{1,0:T(8,128)S(1)}, u32[]{:S(2)}, u32[]{:S(2)}) %collective-permute-start.6) | collective-permute-done | bytes 131104 | tf_op jit(solution)/shard_map/ppermute | solution.py:229
  26.7 0.5 collective-permute-start.9
  27.3 0.7 %collective-permute-done.10.rest_7_ = f32[64,512]{1,0:T(8,128)S(1)} collective-permute-done((f32[64,512]{1,0:T(8,128)S(1)}, f32[64,512]{1,0:T(8,128)S(1)}, u32[]{:S(2)}, u32[]{:S(2)}) %collective-permute-start.10) | collective-permute-done | bytes 131104 | tf_op jit(solution)/shard_map/ppermute | solution.py:232
  28.1 0.2 collective-permute-done.9.rest_6_
  28.2 0.4 collective-permute-done.8.rest_5_
  28.7 1.0 %gram.1 = (f32[64,128]{1,0:T(8,128)S(1)}, bf16[128,4096]{1,0:T(8,128)(2,1)S(1)}) custom-call(f32[64,512]{1,0:T(8,128)S(1)} %add.40.rest_0_, f32[64,512]{1,0:T(8,128)S(1)} %collective-permute-done.4.rest_1_, f32[64,512]{1,0:T(8,128)S(1)} %collective-permute-done.5.rest_2_, f32[64,512]{1,0:T(8,128)S(1)} %collective-permute-done.6.rest_3_, ...), custom_call_target="tpu_custom_call" | custom-call | tf_op jit(solution)/shard_map/gram/pallas_call | solution.py:260
  29.7 3.1 %collective-permute-start.13 = (f32[64,128]{1,0:T(8,128)S(1)}, f32[64,128]{1,0:T(8,128)S(1)}, u32[]{:S(2)}, u32[]{:S(2)}) collective-permute-start(f32[64,128]{1,0:T(8,128)S(1)} %get-tuple-element.18), channel_id=1, source_target_pairs={{0,24},{8,16},{16,8},{24,0},{32,56},{40,48},{48,40},{56,32},{64,88... | collective-permute-start | bytes 98312 | tf_op jit(solution)/shard_map/ppermute | solution.py:235
  32.8 0.6 %collective-permute-start.12 = (f32[64,128]{1,0:T(8,128)S(1)}, f32[64,128]{1,0:T(8,128)S(1)}, u32[]{:S(2)}, u32[]{:S(2)}) collective-permute-start(f32[64,128]{1,0:T(8,128)S(1)} %get-tuple-element.18), channel_id=1, source_target_pairs={{0,16},{8,24},{16,0},{24,8},{32,48},{40,56},{48,32},{56,40},{64,80... | collective-permute-start | bytes 98312 | tf_op jit(solution)/shard_map/ppermute | solution.py:235
  33.4 0.5 collective-permute-start.11
  33.8 1.0 %collective-permute-done.13 = f32[64,128]{1,0:T(8,128)S(1)} collective-permute-done((f32[64,128]{1,0:T(8,128)S(1)}, f32[64,128]{1,0:T(8,128)S(1)}, u32[]{:S(2)}, u32[]{:S(2)}) %collective-permute-start.13) | collective-permute-done | bytes 32800 | tf_op jit(solution)/shard_map/ppermute | solution.py:235
  34.9 3.3 %collective-permute-done.12 = f32[64,128]{1,0:T(8,128)S(1)} collective-permute-done((f32[64,128]{1,0:T(8,128)S(1)}, f32[64,128]{1,0:T(8,128)S(1)}, u32[]{:S(2)}, u32[]{:S(2)}) %collective-permute-start.12) | collective-permute-done | bytes 32800 | tf_op jit(solution)/shard_map/ppermute | solution.py:235
  38.2 2.0 %collective-permute-start.16 = (f32[64,128]{1,0:T(8,128)S(1)}, f32[64,128]{1,0:T(8,128)S(1)}, u32[]{:S(2)}, u32[]{:S(2)}) collective-permute-start(f32[64,128]{1,0:T(8,128)S(1)} %add_add_fusion.1), channel_id=1, source_target_pairs={{0,96},{8,104},{16,112},{24,120},{32,64},{40,72},{48,80},{56,88},{... | collective-permute-start | bytes 98312 | tf_op jit(solution)/shard_map/ppermute | solution.py:235
  40.2 1.4 %collective-permute-start.15 = (f32[64,128]{1,0:T(8,128)S(1)}, f32[64,128]{1,0:T(8,128)S(1)}, u32[]{:S(2)}, u32[]{:S(2)}) collective-permute-start(f32[64,128]{1,0:T(8,128)S(1)} %add_add_fusion.1), channel_id=1, source_target_pairs={{0,64},{8,72},{16,80},{24,88},{32,96},{40,104},{48,112},{56,120},{... | collective-permute-start | bytes 98312 | tf_op jit(solution)/shard_map/ppermute | solution.py:235
  41.6 1.4 %collective-permute-start.14 = (f32[64,128]{1,0:T(8,128)S(1)}, f32[64,128]{1,0:T(8,128)S(1)}, u32[]{:S(2)}, u32[]{:S(2)}) collective-permute-start(f32[64,128]{1,0:T(8,128)S(1)} %add_add_fusion.1), channel_id=1, source_target_pairs={{0,32},{8,40},{16,48},{24,56},{32,0},{40,8},{48,16},{56,24},{64,96... | collective-permute-start | bytes 98312 | tf_op jit(solution)/shard_map/ppermute | solution.py:235
  43.0 2.3 %collective-permute-done.15 = f32[64,128]{1,0:T(8,128)S(1)} collective-permute-done((f32[64,128]{1,0:T(8,128)S(1)}, f32[64,128]{1,0:T(8,128)S(1)}, u32[]{:S(2)}, u32[]{:S(2)}) %collective-permute-start.15) | collective-permute-done | bytes 32800 | tf_op jit(solution)/shard_map/ppermute | solution.py:235
  45.4 0.2 collective-permute-done.14
  45.6 5.9 %collective-permute-start.17 = (f32[64,128]{1,0:T(8,128)S(1)}, f32[64,128]{1,0:T(8,128)S(1)}, u32[]{:S(2)}, u32[]{:S(2)}) collective-permute-start(f32[64,128]{1,0:T(8,128)S(1)} %add_add_fusion.one_ref), channel_id=1, source_target_pairs={{0,224},{8,232},{16,240},{24,248},{32,192},{40,200},{48,208},{56,2... | collective-permute-start | bytes 98312 | tf_op jit(solution)/shard_map/ppermute | solution.py:235
  51.5 1.9 %collective-permute-done.17.two_ref = f32[64,128]{1,0:T(8,128)S(1)} collective-permute-done((f32[64,128]{1,0:T(8,128)S(1)}, f32[64,128]{1,0:T(8,128)S(1)}, u32[]{:S(2)}, u32[]{:S(2)}) %collective-permute-start.17) | collective-permute-done | bytes 32800 | tf_op jit(solution)/shard_map/ppermute | solution.py:235
  53.4 3.8 %finish.1 = (f32[64,64]{1,0:T(8,128)}, f32[64,64]{1,0:T(8,128)}, f32[64,4096]{1,0:T(8,128)}, f32[64,4096]{1,0:T(8,128)}) custom-call(f32[64,128]{1,0:T(8,128)S(1)} %add_add_fusion.one_ref, f32[64,128]{1,0:T(8,128)S(1)} %collective-permute-done.17.two_ref, bf16[128,4096]{1,0:T(8,128)(2,1)S(1)} %get-tuple-element.19.panel_ref, f32[64,4096]{1,0:T(8,128)} %trail_ref.1), custom_call_target="tpu_custom_call" | custom-call | tf_op jit(solution)/shard_map/finish/pallas_call | solution.py:275
  (19 shorter events, 0.4 us)
Async XLA Ops:
  0.6 7.1 %copy-start.1 = (s32[64]{0:T(128)S(1)}, s32[64]{0:T(128)}, u32[]{:S(2)}) copy-start(s32[64]{0:T(128)} %pivots_ref.1) | copy-start | bytes 772
  0.6 28.0 %copy-start = (f32[64,4096]{1,0:T(8,128)S(1)}, f32[64,4096]{1,0:T(8,128)}, u32[]{:S(2)}) copy-start(f32[64,4096]{1,0:T(8,128)} %trail_ref.1) | copy-start | bytes 3145732
  2.9 6.0 %collective-permute-start = (f32[32,1024]{1,0:T(8,128)S(1)}, f32[32,1024]{1,0:T(8,128)S(1)}, u32[]{:S(2)}, u32[]{:S(2)}) collective-permute-start(f32[32,1024]{1,0:T(8,128)S(1)} %get-tuple-element.13), channel_id=1, source_target_pairs={{0,2},{1,3},{2,0},{3,1},{4,6},{5,7},{6,4},{7,5},{8,10},{9,11},{10,... | collective-permute-start | bytes 393224 | tf_op jit(solution)/shard_map/ppermute | solution.py:229
  4.6 8.7 %collective-permute-start.1 = (f32[32,1024]{1,0:T(8,128)S(1)}, f32[32,1024]{1,0:T(8,128)S(1)}, u32[]{:S(2)}, u32[]{:S(2)}) collective-permute-start(f32[32,1024]{1,0:T(8,128)S(1)} %get-tuple-element.14), channel_id=1, source_target_pairs={{0,4},{1,5},{2,6},{3,7},{4,0},{5,1},{6,2},{7,3},{8,12},{9,13},{10,... | collective-permute-start | bytes 393224 | tf_op jit(solution)/shard_map/ppermute | solution.py:229
  7.2 8.1 %collective-permute-start.2 = (f32[32,1024]{1,0:T(8,128)S(1)}, f32[32,1024]{1,0:T(8,128)S(1)}, u32[]{:S(2)}, u32[]{:S(2)}) collective-permute-start(f32[32,1024]{1,0:T(8,128)S(1)} %get-tuple-element.15), channel_id=1, source_target_pairs={{0,6},{1,7},{2,4},{3,5},{4,2},{5,3},{6,0},{7,1},{8,14},{9,15},{10,... | collective-permute-start | bytes 393224 | tf_op jit(solution)/shard_map/ppermute | solution.py:229
  15.6 1.4 %collective-permute-start.3 = (f32[64,512]{1,0:T(8,128)S(1)}, f32[64,512]{1,0:T(8,128)S(1)}, u32[]{:S(2)}, u32[]{:S(2)}) collective-permute-start(f32[64,512]{1,0:T(8,128)S(1)} %get-tuple-element.17), channel_id=1, source_target_pairs={{0,1},{1,0},{2,3},{3,2},{4,5},{5,4},{6,7},{7,6},{8,9},{9,8},{10,11... | collective-permute-start | bytes 393224 | tf_op jit(solution)/shard_map/ppermute | solution.py:232
  17.1 9.7 %collective-permute-start.6 = (f32[64,512]{1,0:T(8,128)S(1)}, f32[64,512]{1,0:T(8,128)S(1)}, u32[]{:S(2)}, u32[]{:S(2)}) collective-permute-start(f32[64,512]{1,0:T(8,128)S(1)} %add.40.rest_0_), channel_id=1, source_target_pairs={{0,6},{1,7},{2,4},{3,5},{4,2},{5,3},{6,0},{7,1},{8,14},{9,15},{10,... | collective-permute-start | bytes 393224 | tf_op jit(solution)/shard_map/ppermute | solution.py:229
  18.0 8.8 %collective-permute-start.5 = (f32[64,512]{1,0:T(8,128)S(1)}, f32[64,512]{1,0:T(8,128)S(1)}, u32[]{:S(2)}, u32[]{:S(2)}) collective-permute-start(f32[64,512]{1,0:T(8,128)S(1)} %add.40.rest_0_), channel_id=1, source_target_pairs={{0,4},{1,5},{2,6},{3,7},{4,0},{5,1},{6,2},{7,3},{8,12},{9,13},{10,... | collective-permute-start | bytes 393224 | tf_op jit(solution)/shard_map/ppermute | solution.py:229
  18.8 8.5 %collective-permute-start.4 = (f32[64,512]{1,0:T(8,128)S(1)}, f32[64,512]{1,0:T(8,128)S(1)}, u32[]{:S(2)}, u32[]{:S(2)}) collective-permute-start(f32[64,512]{1,0:T(8,128)S(1)} %add.40.rest_0_), channel_id=1, source_target_pairs={{0,2},{1,3},{2,0},{3,1},{4,6},{5,7},{6,4},{7,5},{8,10},{9,11},{10,... | collective-permute-start | bytes 393224 | tf_op jit(solution)/shard_map/ppermute | solution.py:229
  21.2 6.1 %collective-permute-start.7 = (f32[64,512]{1,0:T(8,128)S(1)}, f32[64,512]{1,0:T(8,128)S(1)}, u32[]{:S(2)}, u32[]{:S(2)}) collective-permute-start(f32[64,512]{1,0:T(8,128)S(1)} %add.40.rest_0_), channel_id=1, source_target_pairs={{0,1},{1,0},{2,3},{3,2},{4,5},{5,4},{6,7},{7,6},{8,9},{9,8},{10,11... | collective-permute-start | bytes 393224 | tf_op jit(solution)/shard_map/ppermute | solution.py:232
  26.7 1.3 %collective-permute-start.10 = (f32[64,512]{1,0:T(8,128)S(1)}, f32[64,512]{1,0:T(8,128)S(1)}, u32[]{:S(2)}, u32[]{:S(2)}) collective-permute-start(f32[64,512]{1,0:T(8,128)S(1)} %collective-permute-done.6.rest_3_), channel_id=1, source_target_pairs={{0,1},{1,0},{2,3},{3,2},{4,5},{5,4},{6,7},{7,6},{8,9},{9,8},{10,11... | collective-permute-start | bytes 393224 | tf_op jit(solution)/shard_map/ppermute | solution.py:232
  26.7 1.5 %collective-permute-start.9 = (f32[64,512]{1,0:T(8,128)S(1)}, f32[64,512]{1,0:T(8,128)S(1)}, u32[]{:S(2)}, u32[]{:S(2)}) collective-permute-start(f32[64,512]{1,0:T(8,128)S(1)} %collective-permute-done.5.rest_2_), channel_id=1, source_target_pairs={{0,1},{1,0},{2,3},{3,2},{4,5},{5,4},{6,7},{7,6},{8,9},{9,8},{10,11... | collective-permute-start | bytes 393224 | tf_op jit(solution)/shard_map/ppermute | solution.py:232
  27.3 1.3 %collective-permute-start.8 = (f32[64,512]{1,0:T(8,128)S(1)}, f32[64,512]{1,0:T(8,128)S(1)}, u32[]{:S(2)}, u32[]{:S(2)}) collective-permute-start(f32[64,512]{1,0:T(8,128)S(1)} %collective-permute-done.4.rest_1_), channel_id=1, source_target_pairs={{0,1},{1,0},{2,3},{3,2},{4,5},{5,4},{6,7},{7,6},{8,9},{9,8},{10,11... | collective-permute-start | bytes 393224 | tf_op jit(solution)/shard_map/ppermute | solution.py:232
  29.7 5.2 %collective-permute-start.13 = (f32[64,128]{1,0:T(8,128)S(1)}, f32[64,128]{1,0:T(8,128)S(1)}, u32[]{:S(2)}, u32[]{:S(2)}) collective-permute-start(f32[64,128]{1,0:T(8,128)S(1)} %get-tuple-element.18), channel_id=1, source_target_pairs={{0,24},{8,16},{16,8},{24,0},{32,56},{40,48},{48,40},{56,32},{64,88... | collective-permute-start | bytes 98312 | tf_op jit(solution)/shard_map/ppermute | solution.py:235
  32.8 5.4 %collective-permute-start.12 = (f32[64,128]{1,0:T(8,128)S(1)}, f32[64,128]{1,0:T(8,128)S(1)}, u32[]{:S(2)}, u32[]{:S(2)}) collective-permute-start(f32[64,128]{1,0:T(8,128)S(1)} %get-tuple-element.18), channel_id=1, source_target_pairs={{0,16},{8,24},{16,0},{24,8},{32,48},{40,56},{48,32},{56,40},{64,80... | collective-permute-start | bytes 98312 | tf_op jit(solution)/shard_map/ppermute | solution.py:235
  33.4 4.8 %collective-permute-start.11 = (f32[64,128]{1,0:T(8,128)S(1)}, f32[64,128]{1,0:T(8,128)S(1)}, u32[]{:S(2)}, u32[]{:S(2)}) collective-permute-start(f32[64,128]{1,0:T(8,128)S(1)} %get-tuple-element.18), channel_id=1, source_target_pairs={{0,8},{8,0},{16,24},{24,16},{32,40},{40,32},{48,56},{56,48},{64,72... | collective-permute-start | bytes 98312 | tf_op jit(solution)/shard_map/ppermute | solution.py:235
  38.2 4.8 %collective-permute-start.16 = (f32[64,128]{1,0:T(8,128)S(1)}, f32[64,128]{1,0:T(8,128)S(1)}, u32[]{:S(2)}, u32[]{:S(2)}) collective-permute-start(f32[64,128]{1,0:T(8,128)S(1)} %add_add_fusion.1), channel_id=1, source_target_pairs={{0,96},{8,104},{16,112},{24,120},{32,64},{40,72},{48,80},{56,88},{... | collective-permute-start | bytes 98312 | tf_op jit(solution)/shard_map/ppermute | solution.py:235
  40.2 5.2 %collective-permute-start.15 = (f32[64,128]{1,0:T(8,128)S(1)}, f32[64,128]{1,0:T(8,128)S(1)}, u32[]{:S(2)}, u32[]{:S(2)}) collective-permute-start(f32[64,128]{1,0:T(8,128)S(1)} %add_add_fusion.1), channel_id=1, source_target_pairs={{0,64},{8,72},{16,80},{24,88},{32,96},{40,104},{48,112},{56,120},{... | collective-permute-start | bytes 98312 | tf_op jit(solution)/shard_map/ppermute | solution.py:235
  41.6 4.0 %collective-permute-start.14 = (f32[64,128]{1,0:T(8,128)S(1)}, f32[64,128]{1,0:T(8,128)S(1)}, u32[]{:S(2)}, u32[]{:S(2)}) collective-permute-start(f32[64,128]{1,0:T(8,128)S(1)} %add_add_fusion.1), channel_id=1, source_target_pairs={{0,32},{8,40},{16,48},{24,56},{32,0},{40,8},{48,16},{56,24},{64,96... | collective-permute-start | bytes 98312 | tf_op jit(solution)/shard_map/ppermute | solution.py:235
  45.6 7.8 %collective-permute-start.17 = (f32[64,128]{1,0:T(8,128)S(1)}, f32[64,128]{1,0:T(8,128)S(1)}, u32[]{:S(2)}, u32[]{:S(2)}) collective-permute-start(f32[64,128]{1,0:T(8,128)S(1)} %add_add_fusion.one_ref), channel_id=1, source_target_pairs={{0,224},{8,232},{16,240},{24,248},{32,192},{40,200},{48,208},{56,2... | collective-permute-start | bytes 98312 | tf_op jit(solution)/shard_map/ppermute | solution.py:235
